TPU v7x, 32 devices: a whole 2x2x4 slice. The times are simulated.
32 devices in a mesh: seq: 8 (over z, y), ch: 4 (over x, core).
Axes of the slice: x: 2, y: 2, z: 4, core: 2. Of those that a mesh axis runs over, the one named last changes fastest.
Arguments:
- value_in: bfloat16 [4096, 1024], P('ch', 'seq'), may hold values from -6 to 6
- gate_inner: bfloat16 [4096, 1024], P('ch', 'seq'), may hold values from -6 to 6
- gate_outer: bfloat16 [4096, 1024], P('ch', 'seq'), may hold values from -6 to 6
- out_grad: bfloat16 [4096, 1024], P('ch', 'seq'), may hold values from -6 to 6
- filter_proj: bfloat16 [2, 4096, 64], P(None, 'ch'), may hold values from -0.75 to 0.75
- decay: float32 [2, 4096], P(None, 'ch'), may hold values from 0.00048828125 to 0.05
- frequency: float32 [64], replicated, may hold values from 0.001 to 3
Outputs:
- grad_value: bfloat16 [4096, 1024], P('ch', 'seq')
- grad_gate_inner: bfloat16 [4096, 1024], P('ch', 'seq')
- grad_gate_outer: bfloat16 [4096, 1024], P('ch', 'seq')
- filter_grad: float32 [2, 4096, 64], P(None, 'ch')
All inputs are finite; a program needn't handle non-finite values.
Results may differ from a plain program's by a relative error of at most 0.0025.
Values may be sent and summed in bfloat16 or wider, within the bound.
No kernel may reach another device: no remote copies, remote signals or barrier semaphores. Data moves between devices by JAX's collectives and lax.ppermute only.
A program may use at most 64 MiB of HBM per device.

v0:
```python
import math
import functools
import numpy as np
import ml_dtypes
import jax
import jax.numpy as jnp
from jax import lax
from jax.experimental import pallas as pl
from jax.experimental.pallas import tpu as pltpu
from jax.sharding import PartitionSpec as P

BLOCKS = 8
LANES = 128
COS1, COS2, COS3 = (math.cos(math.pi / 8), math.cos(math.pi / 4), math.cos(3 * math.pi / 8))
STEP = 16


def class_tables():
    points = BLOCKS * LANES * 2
    lane = np.arange(LANES)
    forward = np.zeros((BLOCKS, 2 * LANES, 2 * LANES))
    inverse = np.zeros((BLOCKS, 2 * LANES, 2 * LANES))
    for residue in range(1, BLOCKS):
        angle = 2 * np.pi * np.outer(lane, 16 * lane + residue) / points
        cos, sin = np.cos(angle), np.sin(angle)
        forward[residue] = np.block([[cos, -sin], [-sin, -cos]])
        inverse[residue] = np.block([[cos.T, sin.T], [-sin.T, cos.T]]) * (2.0 / points)
    half = LANES // 2
    for offset, first in ((0, 0), (8, half)):
        angle = 2 * np.pi * np.outer(lane, 16 * lane[:half] + offset) / points
        cos, sin = np.cos(angle), np.sin(angle)
        rows = slice(0, LANES) if offset == 0 else slice(LANES, 2 * LANES)
        re_cols, im_cols = slice(first, first + half), slice(LANES + first, LANES + first + half)
        forward[0, rows, re_cols] = cos
        forward[0, rows, im_cols] = -sin
        inverse[0, re_cols, rows] = cos.T * (2.0 / points)
        inverse[0, im_cols, rows] = -sin.T * (2.0 / points)
    forward[0, :LANES, LANES] = (-1.0) ** lane
    inverse[0, 0, :LANES] = 1.0 / points
    inverse[0, LANES, :LANES] = (-1.0) ** lane / points
    return forward, inverse


def split_table(table):
    high = table.astype(ml_dtypes.bfloat16)
    low = (table - high.astype(np.float64)).astype(ml_dtypes.bfloat16)
    return high, low


def fold(x):
    s = [x[a] + x[a + 4] for a in range(4)]
    d = [x[a] - x[a + 4] for a in range(4)]
    t0, t1 = s[0] + s[2], s[1] + s[3]
    u0, u1 = s[0] - s[2], s[1] - s[3]
    p, w = (d[1] - d[3]) * COS2, (d[1] + d[3]) * COS2
    p1, p2, p3 = x[1] - x[7], (x[2] - x[6]) * COS2, x[3] - x[5]
    n1, n2, n3 = x[1] + x[7], (x[2] + x[6]) * COS2, x[3] + x[5]
    a0, b0 = x[0] + p2, x[0] - p2
    c0, d0 = p1 * COS1 + p3 * COS3, p1 * COS3 - p3 * COS1
    a1, b1 = n2 + x[4], n2 - x[4]
    c1, d1 = n1 * COS3 + n3 * COS1, n1 * COS1 - n3 * COS3
    return (
        (t0 + t1, t0 - t1),
        (a0 + c0, c1 + a1),
        (d[0] + p, d[2] + w),
        (b0 + d0, d1 + b1),
        (u0, u1),
        (b0 - d0, d1 - b1),
        (d[0] - p, w - d[2]),
        (a0 - c0, c1 - a1),
    )


def unfold(z):
    (z0, z8), (r1, i1), (r2, i2), (r3, i3), (r4, i4), (r5, i5), (r6, i6), (r7, i7) = z
    even, odd = z0 + z8, z0 - z8
    g = [even + r4, odd - i4, even - r4, odd + i4]
    dr, di = r2 - r6, i2 + i6
    h = [r2 + r6, (dr - di) * COS2, i6 - i2, (dr + di) * -COS2]
    rs, rd, ts, td = r1 + r7, r1 - r7, r3 + r5, r3 - r5
    js, jd, ks, kd = i1 + i7, i1 - i7, i3 + i5, i3 - i5
    k = [None, rd * COS1 + td * COS3, (rs - ts) * COS2, rd * COS3 - td * COS1]
    m = [None, js * COS3 + ks * COS1, (jd + kd) * COS2, js * COS1 - ks * COS3]
    o = [rs + ts, k[1] - m[1], k[2] - m[2], k[3] - m[3], kd - jd, -(k[3] + m[3]), -(k[2] + m[2]), -(k[1] + m[1])]
    return [g[a] + h[a] + o[a] for a in range(4)] + [g[a] - h[a] + o[a + 4] for a in range(4)]


def halves(x):
    high = x.astype(jnp.bfloat16)
    return high, (x - high.astype(jnp.float32)).astype(jnp.bfloat16)


def split_features(features):
    high = lax.reduce_precision(features, 8, 7)
    return high.astype(jnp.bfloat16), (features - high).astype(jnp.bfloat16)


def put(hi_ref, lo_ref, index, parts):
    for part, x in enumerate(parts):
        high, low = halves(x)
        lanes = slice(part * LANES, (part + 1) * LANES)
        hi_ref[index + (lanes,)] = high
        lo_ref[index + (lanes,)] = low


def store_folded(hi_ref, lo_ref, rows, blocks):
    for residue, parts in enumerate(fold(blocks)):
        put(hi_ref, lo_ref, (residue, rows), parts)


def times(high, low, table_hi, table_lo):
    dot = functools.partial(jnp.dot, preferred_element_type=jnp.float32)
    return dot(high, table_hi) + (dot(low, table_hi) + dot(high, table_lo))


def multiplied(left, right, conj, residue):
    a_re, a_im = left
    b_re, b_im = right
    rr, ii, ri, ir = a_re * b_re, a_im * b_im, a_re * b_im, a_im * b_re
    if conj:
        re, im = rr + ii, ri - ir
    else:
        re, im = rr - ii, ri + ir
    if residue == 0:
        shared = lax.broadcasted_iota(jnp.int32, re.shape, 1) == 0
        re, im = jnp.where(shared, rr, re), jnp.where(shared, ii, im)
    return re, im


def window_blocks(rate):
    rate = jnp.broadcast_to(rate, (rate.shape[0], LANES))
    place = lax.broadcasted_iota(jnp.int32, rate.shape, 1).astype(jnp.float32)
    first = jnp.sqrt(2.0 * rate) * jnp.exp(-rate * place)
    return [first * jnp.exp(rate * (-float(LANES) * a)) if a else first for a in range(BLOCKS)]


def filter_kernel(proj, rate, features, table_hi, table_lo, spectra, filters, fold_hi, fold_lo):
    rows = proj.shape[0]
    for a in range(BLOCKS):
        filters[a] = jnp.dot(proj[...], features[a], preferred_element_type=jnp.float32)

    @pl.loop(0, rows // STEP)
    def _(step):
        at = pl.ds(pl.multiple_of(step * STEP, STEP), STEP)
        window = window_blocks(rate[at, :])
        store_folded(fold_hi, fold_lo, at, [filters[a, at, :] * window[a] for a in range(BLOCKS)])

    for residue in range(BLOCKS):
        spectra[residue] = times(fold_hi[residue], fold_lo[residue], table_hi[residue], table_lo[residue])


def main_kernel(
    moved, rate, filt, feat_hi, feat_lo, fwd_hi, fwd_lo, inv_hi, inv_lo,
    grads, proj_grad,
    one_hi, one_lo, two_hi, two_lo, spec, spec2, back, weighted_hi, weighted_lo,
):
    count = moved.shape[1] // 4
    value, inner, outer, grad = (moved.at[:, i * count : (i + 1) * count] for i in range(4))
    grad_value, grad_inner, grad_outer = (grads.at[:, i * count : (i + 1) * count] for i in range(3))

    def chunk(step):
        return pl.ds(pl.multiple_of(step * STEP, STEP), STEP), pl.ds(pl.multiple_of(count + step * STEP, STEP), STEP)

    def pair(ref, residue, rows):
        return ref[residue, rows, :LANES], ref[residue, rows, LANES:]

    upper, lower = slice(0, count), slice(count, 2 * count)

    @pl.loop(0, count // STEP)
    def _(step):
        at, below = chunk(step)
        store_folded(one_hi, one_lo, at, [value[a, at, :].astype(jnp.float32) for a in range(BLOCKS)])
        store_folded(one_hi, one_lo, below, [
            grad[a, at, :].astype(jnp.float32) * outer[a, at, :].astype(jnp.float32) for a in range(BLOCKS)])

    for residue in range(BLOCKS):
        spec[residue] = times(one_hi[residue], one_lo[residue], fwd_hi[residue], fwd_lo[residue])
        put(two_hi, two_lo, (residue, upper), multiplied(
            pair(filt, residue, upper), pair(spec, residue, upper), False, residue))
        put(two_hi, two_lo, (residue, lower), multiplied(
            pair(filt, residue, lower), pair(spec, residue, lower), True, residue))
        rows = slice(0, 2 * count)
        back[residue, rows, :] = times(
            two_hi[residue, rows, :], two_lo[residue, rows, :], inv_hi[residue], inv_lo[residue])

    @pl.loop(0, count // STEP)
    def _(step):
        at, below = chunk(step)
        gate = [inner[a, at, :].astype(jnp.float32) for a in range(BLOCKS)]
        inner_act = unfold([pair(back, residue, at) for residue in range(BLOCKS)])
        store_folded(one_hi, one_lo, at, [gate[a] * inner_act[a] for a in range(BLOCKS)])
        grad_mixed = unfold([pair(back, residue, below) for residue in range(BLOCKS)])
        for a in range(BLOCKS):
            grad_inner[a, at, :] = (grad_mixed[a] * inner_act[a]).astype(jnp.bfloat16)
        store_folded(one_hi, one_lo, below, [gate[a] * grad_mixed[a] for a in range(BLOCKS)])

    for residue in range(BLOCKS):
        spec2[...] = times(one_hi[residue], one_lo[residue], fwd_hi[residue], fwd_lo[residue])
        mixed = spec2[upper, :LANES], spec2[upper, LANES:]
        inner_grad = spec2[lower, :LANES], spec2[lower, LANES:]
        products = (
            multiplied(pair(filt, residue, lower), mixed, False, residue),
            multiplied(pair(filt, residue, upper), inner_grad, True, residue),
            multiplied(pair(spec, residue, upper), inner_grad, True, residue),
            multiplied(mixed, pair(spec, residue, lower), True, residue),
        )
        for place, product in enumerate(products):
            put(two_hi, two_lo, (residue, slice(place * count, (place + 1) * count)), product)
        back[residue] = times(two_hi[residue], two_lo[residue], inv_hi[residue], inv_lo[residue])

    @pl.loop(0, count // STEP)
    def _(step):
        def signal(place):
            at = pl.ds(pl.multiple_of(place * count + step * STEP, STEP), STEP)
            return unfold([pair(back, residue, at) for residue in range(BLOCKS)])

        at, below = chunk(step)
        outer_act = signal(0)
        for a in range(BLOCKS):
            grad_outer[a, at, :] = (grad[a, at, :].astype(jnp.float32) * outer_act[a]).astype(jnp.bfloat16)
        value_grad = signal(1)
        for a in range(BLOCKS):
            grad_value[a, at, :] = value_grad[a].astype(jnp.bfloat16)
        for place, rows in ((2, at), (3, below)):
            filter_grad = signal(place)
            window = window_blocks(rate[rows, :])
            for a in range(BLOCKS):
                high, low = halves(filter_grad[a] * window[a])
                lanes = slice(a * LANES, (a + 1) * LANES)
                weighted_hi[rows, lanes] = high
                weighted_lo[rows, lanes] = low

    total = None
    for place, rows in ((0, upper), (1, lower)):
        part = times(weighted_hi[rows, :], weighted_lo[rows, :], feat_hi[place], feat_lo[place])
        total = part if total is None else total + part
    proj_grad[...] = total


def vmem_call(kernel, out_shape, scratch, **extra):
    return pl.pallas_call(
        kernel,
        out_shape=out_shape,
        scratch_shapes=scratch,
        compiler_params=pltpu.CompilerParams(vmem_limit_bytes=56 * 2**20),
        **extra,
    )


def filter_spectra(proj_rows, rates, features, tables):
    count = proj_rows.shape[1]
    twice = proj_rows.reshape(2 * count, -1)
    twice = jnp.concatenate([twice, twice], 1)
    high, low = split_features(features)
    rows = jnp.concatenate([high, low], 1).reshape(BLOCKS, LANES, -1).transpose(0, 2, 1)
    bf, f32 = jnp.bfloat16, jnp.float32
    width = 2 * LANES
    return vmem_call(
        filter_kernel,
        jax.ShapeDtypeStruct((BLOCKS, 2 * count, width), f32),
        [pltpu.VMEM((BLOCKS, 2 * count, LANES), f32)] + [pltpu.VMEM((BLOCKS, 2 * count, width), bf)] * 2,
        name="filter_spectra",
    )(twice, rates.reshape(2 * count, 1), rows, *tables)


def operator_grads(moved, rates, spectra, features, forward, inverse):
    count = moved.shape[1] // 4
    high, low = split_features(features)
    zero = jnp.zeros_like(high)
    placed = [jnp.stack([jnp.concatenate([x, zero], 1), jnp.concatenate([zero, x], 1)]) for x in (high, low)]
    bf, f32 = jnp.bfloat16, jnp.float32
    width = 2 * LANES
    gradients = jax.ShapeDtypeStruct((BLOCKS, 3 * count, LANES), bf)
    return vmem_call(
        main_kernel,
        (gradients, jax.ShapeDtypeStruct((count, 2 * features.shape[1]), f32)),
        [pltpu.VMEM((BLOCKS, 2 * count, width), bf)] * 2
        + [pltpu.VMEM((BLOCKS, 4 * count, width), bf)] * 2
        + [pltpu.VMEM((BLOCKS, 2 * count, width), f32), pltpu.VMEM((2 * count, width), f32),
           pltpu.VMEM((BLOCKS, 4 * count, width), f32)]
        + [pltpu.VMEM((2 * count, BLOCKS * LANES), bf)] * 2,
        name="operator_grads",
    )(moved, rates.reshape(2 * count, 1), spectra, *placed, *forward, *inverse)


highest = lax.Precision.HIGHEST


def angle_table(rows, cols, period):
    row_idx = lax.broadcasted_iota(jnp.int32, (rows, cols), 0)
    col_idx = lax.broadcasted_iota(jnp.int32, (rows, cols), 1)
    angle = (row_idx * col_idx % period).astype(jnp.float32) * (2.0 * math.pi / period)
    return (jnp.cos(angle), jnp.sin(angle))


def split_length(total):
    return max((factor for factor in range(2, math.isqrt(total) + 1, 2) if total % factor == 0))


def forward_dft(signal):
    rows, length = signal.shape
    total = 2 * length
    first = split_length(total)
    second = total // first
    half = first // 2
    shaped = signal.reshape(rows, half, second)
    cos_one, sin_one = angle_table(half, first, first)
    part_re = jnp.einsum("mab,ak->mkb", shaped, cos_one, precision=highest)
    part_im = -jnp.einsum("mab,ak->mkb", shaped, sin_one, precision=highest)
    twist_cos, twist_sin = angle_table(first, second, total)
    turned_re = part_re * twist_cos + part_im * twist_sin
    turned_im = part_im * twist_cos - part_re * twist_sin
    cos_two, sin_two = angle_table(second, second, second)
    out_re = jnp.einsum("mkb,bl->mkl", turned_re, cos_two, precision=highest) + jnp.einsum(
        "mkb,bl->mkl", turned_im, sin_two, precision=highest
    )
    out_im = jnp.einsum("mkb,bl->mkl", turned_im, cos_two, precision=highest) - jnp.einsum(
        "mkb,bl->mkl", turned_re, sin_two, precision=highest
    )
    return (out_re, out_im)


def inverse_dft(spectrum):
    spec_re, spec_im = spectrum
    rows, first, second = spec_re.shape
    total = first * second
    half = first // 2
    cos_two, sin_two = angle_table(second, second, second)
    part_re = jnp.einsum("mkl,lb->mkb", spec_re, cos_two, precision=highest) - jnp.einsum(
        "mkl,lb->mkb", spec_im, sin_two, precision=highest
    )
    part_im = jnp.einsum("mkl,lb->mkb", spec_re, sin_two, precision=highest) + jnp.einsum(
        "mkl,lb->mkb", spec_im, cos_two, precision=highest
    )
    twist_cos, twist_sin = angle_table(first, second, total)
    turned_re = part_re * twist_cos - part_im * twist_sin
    turned_im = part_re * twist_sin + part_im * twist_cos
    cos_one, sin_one = angle_table(half, first, first)
    result = jnp.einsum("mkb,ak->mab", turned_re, cos_one, precision=highest) - jnp.einsum(
        "mkb,ak->mab", turned_im, sin_one, precision=highest
    )
    return result.reshape(rows, half * second) / total


def product_of(left, right, conj_left):
    left_re, left_im = left
    right_re, right_im = right
    if conj_left:
        left_im = -left_im
    return (left_re * right_re - left_im * right_im, left_re * right_im + left_im * right_re)


def rows_of(spectrum, start, count):
    return (spectrum[0][start : start + count], spectrum[1][start : start + count])


def joined(upper, lower):
    return (jnp.concatenate([upper[0], lower[0]], 0), jnp.concatenate([upper[1], lower[1]], 0))


def general_body(value_in, gate_inner, gate_outer, out_grad, filter_proj, decay, frequency):
    seq_pos = lax.axis_index("seq")
    value_cols, inner_cols, outer_cols, grad_cols = (
        lax.all_to_all(value_in, "seq", split_axis=0, concat_axis=1, tiled=True),
        lax.all_to_all(gate_inner, "seq", split_axis=0, concat_axis=1, tiled=True),
        lax.all_to_all(gate_outer, "seq", split_axis=0, concat_axis=1, tiled=True),
        lax.all_to_all(out_grad, "seq", split_axis=0, concat_axis=1, tiled=True),
    )
    count = value_cols.shape[0]
    length = value_cols.shape[1]
    first_row = seq_pos * count
    proj_rows = lax.dynamic_slice_in_dim(filter_proj, first_row, count, 1).astype(jnp.float32)
    rates = lax.dynamic_slice_in_dim(decay, first_row, count, 1)
    positions = lax.iota(jnp.float32, length)
    features = jnp.sin(frequency[None, :] * (positions[:, None] + 1.0))
    window = jnp.sqrt(2.0 * rates)[:, :, None] * jnp.exp(-rates[:, :, None] * positions)
    filters = jnp.einsum("kcf,tf->kct", proj_rows, features, precision=highest) * window
    value_f = value_cols.astype(jnp.float32)
    inner_f = inner_cols.astype(jnp.float32)
    spectra = forward_dft(jnp.concatenate([filters[0], filters[1], value_f], 0))
    inner_spec = rows_of(spectra, 0, count)
    outer_spec = rows_of(spectra, count, count)
    value_spec = rows_of(spectra, 2 * count, count)
    inner_act = inverse_dft(product_of(inner_spec, value_spec, False))
    mixed = inner_f * inner_act
    mixed_spec = forward_dft(mixed)
    outer_act = inverse_dft(product_of(outer_spec, mixed_spec, False))
    outer_f = outer_cols.astype(jnp.float32)
    grad_f = grad_cols.astype(jnp.float32)
    grad_outer = grad_f * outer_act
    grad_spec = forward_dft(grad_f * outer_f)
    outer_back = inverse_dft(
        joined(product_of(outer_spec, grad_spec, True), product_of(mixed_spec, grad_spec, True))
    )
    grad_mixed = outer_back[:count]
    grad_outer_filter = outer_back[count:]
    grad_inner = grad_mixed * inner_act
    inner_grad_spec = forward_dft(grad_mixed * inner_f)
    inner_back = inverse_dft(
        joined(
            product_of(inner_spec, inner_grad_spec, True),
            product_of(value_spec, inner_grad_spec, True),
        )
    )
    grad_value = inner_back[:count]
    grad_inner_filter = inner_back[count:]
    value_out, inner_out, outer_out = (
        lax.all_to_all(
            grad_value.astype(jnp.bfloat16), "seq", split_axis=1, concat_axis=0, tiled=True
        ),
        lax.all_to_all(
            grad_inner.astype(jnp.bfloat16), "seq", split_axis=1, concat_axis=0, tiled=True
        ),
        lax.all_to_all(
            grad_outer.astype(jnp.bfloat16), "seq", split_axis=1, concat_axis=0, tiled=True
        ),
    )
    weighted = jnp.stack([grad_inner_filter, grad_outer_filter]) * window
    own_grad = jnp.einsum("kct,tf->kcf", weighted, features, precision=highest)
    proj_grad = lax.all_gather(own_grad, "seq", axis=1, tiled=True)
    square_sum = lax.psum(jnp.sum(proj_grad * proj_grad), "ch")
    entries = proj_grad.size * lax.axis_size("ch")
    scale = lax.rsqrt(square_sum / entries + 1e-06)
    return (value_out, inner_out, outer_out, proj_grad * scale)


def swapped(x, hop):
    size = lax.axis_size("seq")
    return lax.ppermute(x, "seq", [(i, i ^ hop) for i in range(size)])


def gathered(x):
    place = lax.axis_index("seq")
    hop = BLOCKS // 2
    held = x[None]
    while hop:
        other = swapped(held, hop)
        mine_first = (place & hop) == 0
        held = jnp.where(mine_first, jnp.stack([held, other], 1), jnp.stack([other, held], 1))
        held = held.reshape((-1,) + x.shape)
        hop //= 2
    return held


def body(value_in, gate_inner, gate_outer, out_grad, filter_proj, decay, frequency):
    seq_pos = lax.axis_index("seq")
    channels, lanes = value_in.shape
    count = channels // BLOCKS
    length = BLOCKS * lanes
    forward, inverse = ([jnp.asarray(part) for part in split_table(table)] for table in class_tables())
    proj_rows = lax.dynamic_slice_in_dim(filter_proj, seq_pos * count, count, 1)
    rates = lax.dynamic_slice_in_dim(decay, seq_pos * count, count, 1)
    features = jnp.sin(frequency[None, :] * (lax.iota(jnp.float32, length)[:, None] + 1.0))
    spectra = filter_spectra(proj_rows, rates, features, forward)
    stacked = jnp.concatenate(
        [x.reshape(BLOCKS, count, lanes) for x in (value_in, gate_inner, gate_outer, out_grad)], 1
    )
    moved = lax.all_to_all(stacked, "seq", split_axis=0, concat_axis=0, tiled=True)
    grads, own_grad = operator_grads(moved, rates, spectra, features, forward, inverse)
    back = lax.all_to_all(grads, "seq", split_axis=0, concat_axis=0, tiled=True)
    outs = [back[:, i * count : (i + 1) * count].reshape(channels, lanes) for i in range(3)]
    proj_grad = gathered(own_grad)
    square_sum = jnp.sum(proj_grad * proj_grad)
    for hop in (1, 2):
        square_sum = square_sum + lax.ppermute(square_sum, "ch", [(i, i ^ hop) for i in range(4)])
    scale = lax.rsqrt(square_sum / (proj_grad.size * 4) + 1e-06)
    both = proj_grad.reshape(channels, 2, -1).transpose(1, 0, 2)
    return (*outs, both * scale)


def solution(mesh):
    def chosen(*arrays):
        whole = arrays[0].shape[1] == LANES and arrays[0].shape[0] % (BLOCKS * STEP) == 0
        fits = lax.axis_size("seq") == BLOCKS and lax.axis_size("ch") == 4
        return body(*arrays) if whole and fits else general_body(*arrays)

    split = P("ch", "seq")
    rows = P(None, "ch", None)
    return jax.shard_map(
        chosen,
        mesh=mesh,
        in_specs=(split, split, split, split, rows, P(None, "ch"), P()),
        out_specs=(split, split, split, rows),
        check_vma=False,
    )
```

profile of v0, /device:TPU:0, one launch (start us, length us, event | category | flops | bytes accessed | tf_op | source)
XLA Modules:
  0.0 99.7 jit_solution(2150229754996880181)
XLA Ops:
  0.7 2.3 %pad_maximum_fusion = bf16[8,512,128]{2,1,0:T(8,128)(2,1)} fusion(bf16[8,128,128]{2,1,0:T(8,128)(2,1)} %bitcast.43, bf16[8,128,128]{2,1,0:T(8,128)(2,1)} %bitcast.44, bf16[8,128,128]{2,1,0:T(8,128)(2,1)} %bitcast.45, bf16[8,128,128]{2,1,0:T(8,128)(2,1)} %bitcast.46), kind=kLoop, calls=%fused_computation | loop fusion | flops 4194304 | bytes 2097152 | tf_op jit(solution)/shard_map/concatenate | solution.py:455
  2.9 7.3 %all-to-all-start = ((bf16[8,512,128]{2,1,0:T(8,128)(2,1)}), bf16[8,512,128]{2,1,0:T(8,128)(2,1)S(1)}, u32[]{:S(2)}, u32[]{:S(2)}) async-start(bf16[8,512,128]{2,1,0:T(8,128)(2,1)} %pad_maximum_fusion), calls=%async_computation | async-start | bytes 2097152 | tf_op jit(solution)/shard_map/all_to_all | solution.py:458
  10.9 0.8 copy.23.rate
  12.6 0.9 reduce-precision_convert_fusion.1
  14.3 6.3 %filter_spectra.1.filt = f32[8,256,256]{2,1,0:T(8,128)} custom-call(bf16[256,128]{1,0:T(8,128)(2,1)} %pad_maximum_fusion.3.proj, f32[256,1]{1,0:T(8,128)} %copy.23.rate, bf16[8,128,128]{2,1,0:T(8,128)(2,1)} %maximum_bitcast_fusion.features, bf16[8,256,256]{2,1,0:T(8,128)(2,1)} %constant.39.clone.table_hi.fwd_hi, ...), custom_call_target="tpu_custom_call" | custom-call | tf_op jit(solution)/shard_map/filter_spectra/pallas_call | solution.py:258
  20.5 2.1 %fusion = (bf16[1024,64]{1,0:T(8,128)(2,1)S(1)}, bf16[1024,64]{1,0:T(8,128)(2,1)S(1)}) fusion(f32[1024]{0:T(1024)S(1)} %iota_add_fusion, f32[64]{0:T(128)S(1)} %copy-done.2), kind=kLoop, calls=%fused_computation.3 | loop fusion | flops 327680 | bytes 266496 | tf_op jit(solution)/shard_map/convert_element_type | solution.py:95
  22.9 0.8 pad_maximum_fusion.1.feat_hi
  23.7 0.8 pad_maximum_fusion.2.feat_lo
  24.6 11.4 %all-to-all-done.moved = bf16[8,512,128]{2,1,0:T(8,128)(2,1)S(1)} async-done(((bf16[8,512,128]{2,1,0:T(8,128)(2,1)}), bf16[8,512,128]{2,1,0:T(8,128)(2,1)S(1)}, u32[]{:S(2)}, u32[]{:S(2)}) %all-to-all-start) | async-done | bytes 1048608 | tf_op jit(solution)/shard_map/all_to_all | solution.py:458
  36.0 1.0 copy-done.1
  36.9 13.5 %operator_grads.1 = (bf16[8,384,128]{2,1,0:T(8,128)(2,1)}, f32[128,128]{1,0:T(8,128)}) custom-call(bf16[8,512,128]{2,1,0:T(8,128)(2,1)} %copy-done.1, f32[256,1]{1,0:T(8,128)} %copy.23.rate, f32[8,256,256]{2,1,0:T(8,128)} %filter_spectra.1.filt, bf16[2,1024,128]{2,1,0:T(8,128)(2,1)} %pad_maximum_fusion.1.feat_hi, ...), custom_call_target="tpu_custom_call" | custom-call | tf_op jit(solution)/shard_map/operator_grads/pallas_call | solution.py:274
  50.4 3.6 %all-to-all-start.1 = ((bf16[8,384,128]{2,1,0:T(8,128)(2,1)}), bf16[8,384,128]{2,1,0:T(8,128)(2,1)S(1)}, u32[]{:S(2)}, u32[]{:S(2)}) async-start(bf16[8,384,128]{2,1,0:T(8,128)(2,1)} %get-tuple-element.6), calls=%async_computation.1 | async-start | bytes 1572864 | tf_op jit(solution)/shard_map/all_to_all | solution.py:460
  54.0 2.9 %collective-permute-start = (f32[1,128,128]{2,1,0:T(8,128)}, f32[1,128,128]{2,1,0:T(8,128)S(1)}, u32[]{:S(2)}, u32[]{:S(2)}) collective-permute-start(f32[1,128,128]{2,1,0:T(8,128)} %bitcast.39), channel_id=1, source_target_pairs={{0,16},{4,20},{8,24},{12,28},{16,0},{20,4},{24,8},{28,12},{1,17},{... | collective-permute-start | bytes 196616 | tf_op jit(solution)/shard_map/ppermute | solution.py:429
  57.0 20.3 %collective-permute-done = f32[1,128,128]{2,1,0:T(8,128)S(1)} collective-permute-done((f32[1,128,128]{2,1,0:T(8,128)}, f32[1,128,128]{2,1,0:T(8,128)S(1)}, u32[]{:S(2)}, u32[]{:S(2)}) %collective-permute-start) | collective-permute-done | bytes 65568 | tf_op jit(solution)/shard_map/ppermute | solution.py:429
  77.2 0.9 maximum_select_fusion.3
  78.2 0.9 maximum_select_fusion.2
  79.2 4.0 %collective-permute-done.1 = f32[2,128,128]{2,1,0:T(8,128)S(1)} collective-permute-done((f32[2,128,128]{2,1,0:T(8,128)S(1)}, f32[2,128,128]{2,1,0:T(8,128)S(1)}, u32[]{:S(2)}, u32[]{:S(2)}) %collective-permute-start.1) | collective-permute-done | bytes 131104 | tf_op jit(solution)/shard_map/ppermute | solution.py:429
  83.2 1.4 %collective-permute-start.2 = (f32[4,128,128]{2,1,0:T(8,128)S(1)}, f32[4,128,128]{2,1,0:T(8,128)S(1)}, u32[]{:S(2)}, u32[]{:S(2)}) collective-permute-start(f32[4,128,128]{2,1,0:T(8,128)S(1)} %bitcast.29), channel_id=1, source_target_pairs={{0,4},{4,0},{8,12},{12,8},{16,20},{20,16},{24,28},{28,24},{1,5},{5... | collective-permute-start | bytes 786440 | tf_op jit(solution)/shard_map/ppermute | solution.py:429
  84.7 5.0 %collective-permute-done.2 = f32[4,128,128]{2,1,0:T(8,128)S(1)} collective-permute-done((f32[4,128,128]{2,1,0:T(8,128)S(1)}, f32[4,128,128]{2,1,0:T(8,128)S(1)}, u32[]{:S(2)}, u32[]{:S(2)}) %collective-permute-start.2) | collective-permute-done | bytes 262176 | tf_op jit(solution)/shard_map/ppermute | solution.py:429
  89.7 0.7 multiply_reduce_fusion
  90.4 1.2 %collective-permute-done.3 = f32[]{:T(128)} collective-permute-done((f32[]{:T(128)}, f32[]{:T(128)}, u32[]{:S(2)}, u32[]{:S(2)}) %collective-permute-start.3) | collective-permute-done | bytes 36 | tf_op jit(solution)/shard_map/ppermute | solution.py:465
  92.9 2.9 %collective-permute-start.4 = (f32[]{:T(128)}, f32[]{:T(128)}, u32[]{:S(2)}, u32[]{:S(2)}) collective-permute-start(f32[]{:T(128)} %add.43), channel_id=1, source_target_pairs={{0,2},{1,3},{2,0},{3,1},{4,6},{5,7},{6,4},{7,5},{8,10},{9,11},{10,... | collective-permute-start | bytes 20 | tf_op jit(solution)/shard_map/ppermute | solution.py:465
  97.6 1.2 %mul.51 = f32[1024,2,64]{0,2,1:T(8,128)} reshape(f32[4,2,128,128]{2,1,0,3:T(2,128)S(1)} %copy.26) | data formatting | bytes 1048576 | tf_op jit(solution)/shard_map/mul | solution.py:468
  98.8 0.9 fusion.3
  (21 shorter events, 3.8 us)
Async XLA Ops:
  0.6 11.1 %copy-start = (bf16[2,1024,64]{1,2,0:T(8,128)(2,1)S(1)}, bf16[2,1024,64]{1,2,0:T(8,128)(2,1)}, u32[]{:S(2)}) copy-start(bf16[2,1024,64]{1,2,0:T(8,128)(2,1)} %param.15) | copy-start | bytes 786436
  0.6 11.9 %copy-start.2 = (f32[64]{0:T(128)S(1)}, f32[64]{0:T(128)}, u32[]{:S(2)}) copy-start(f32[64]{0:T(128)} %param.17) | copy-start | bytes 772
  2.9 33.0 %all-to-all-start = ((bf16[8,512,128]{2,1,0:T(8,128)(2,1)}), bf16[8,512,128]{2,1,0:T(8,128)(2,1)S(1)}, u32[]{:S(2)}, u32[]{:S(2)}) async-start(bf16[8,512,128]{2,1,0:T(8,128)(2,1)} %pad_maximum_fusion), calls=%async_computation | async-start | bytes 2097152 | tf_op jit(solution)/shard_map/all_to_all | solution.py:458
  36.0 1.0 copy-start.1
  50.4 48.3 %all-to-all-start.1 = ((bf16[8,384,128]{2,1,0:T(8,128)(2,1)}), bf16[8,384,128]{2,1,0:T(8,128)(2,1)S(1)}, u32[]{:S(2)}, u32[]{:S(2)}) async-start(bf16[8,384,128]{2,1,0:T(8,128)(2,1)} %get-tuple-element.6), calls=%async_computation.1 | async-start | bytes 1572864 | tf_op jit(solution)/shard_map/all_to_all | solution.py:460
  54.0 23.2 %collective-permute-start = (f32[1,128,128]{2,1,0:T(8,128)}, f32[1,128,128]{2,1,0:T(8,128)S(1)}, u32[]{:S(2)}, u32[]{:S(2)}) collective-permute-start(f32[1,128,128]{2,1,0:T(8,128)} %bitcast.39), channel_id=1, source_target_pairs={{0,16},{4,20},{8,24},{12,28},{16,0},{20,4},{24,8},{28,12},{1,17},{... | collective-permute-start | bytes 196616 | tf_op jit(solution)/shard_map/ppermute | solution.py:429
  78.2 5.0 %collective-permute-start.1 = (f32[2,128,128]{2,1,0:T(8,128)S(1)}, f32[2,128,128]{2,1,0:T(8,128)S(1)}, u32[]{:S(2)}, u32[]{:S(2)}) collective-permute-start(f32[2,128,128]{2,1,0:T(8,128)S(1)} %maximum_select_fusion.3), channel_id=1, source_target_pairs={{0,8},{4,12},{8,0},{12,4},{16,24},{20,28},{24,16},{28,20},{1,9},{5... | collective-permute-start | bytes 393224 | tf_op jit(solution)/shard_map/ppermute | solution.py:429
  83.2 6.4 %collective-permute-start.2 = (f32[4,128,128]{2,1,0:T(8,128)S(1)}, f32[4,128,128]{2,1,0:T(8,128)S(1)}, u32[]{:S(2)}, u32[]{:S(2)}) collective-permute-start(f32[4,128,128]{2,1,0:T(8,128)S(1)} %bitcast.29), channel_id=1, source_target_pairs={{0,4},{4,0},{8,12},{12,8},{16,20},{20,16},{24,28},{28,24},{1,5},{5... | collective-permute-start | bytes 786440 | tf_op jit(solution)/shard_map/ppermute | solution.py:429
  90.4 1.2 %collective-permute-start.3 = (f32[]{:T(128)}, f32[]{:T(128)}, u32[]{:S(2)}, u32[]{:S(2)}) collective-permute-start(f32[]{:T(128)} %multiply_reduce_fusion), channel_id=1, source_target_pairs={{0,1},{1,0},{2,3},{3,2},{4,5},{5,4},{6,7},{7,6},{8,9},{9,8},{10,11... | collective-permute-start | bytes 20 | tf_op jit(solution)/shard_map/ppermute | solution.py:465
  92.9 3.6 %collective-permute-start.4 = (f32[]{:T(128)}, f32[]{:T(128)}, u32[]{:S(2)}, u32[]{:S(2)}) collective-permute-start(f32[]{:T(128)} %add.43), channel_id=1, source_target_pairs={{0,2},{1,3},{2,0},{3,1},{4,6},{5,7},{6,4},{7,5},{8,10},{9,11},{10,... | collective-permute-start | bytes 20 | tf_op jit(solution)/shard_map/ppermute | solution.py:465
where the time goes:
time: 100 us; the launch traced here: 99.7 us
  waiting for transfers between devices  42.6 us (43%)
  Pallas kernels  19.8 us (20%)
  starting transfers between devices  18.2 us (18%)
  other arithmetic  11.1 us (11%)
  local copies, waits for them, and re-layouts  5.34 us (5%)
  between operations  2.7 us (3%)
    ppermute x3, waiting for transfers between devices, swapped(): return lax.ppermute(x, 'seq', [(i, i ^ hop) for i in range(size)])  29.3 us
    pallas_call x1, Pallas kernels, operator_grads(): vmem_call(main_kernel, (gradients, jax.ShapeDtypeStruct((count, 2 * featu...  13.5 us
    all_to_all x1, waiting for transfers between devices, body(): lax.all_to_all(stacked, 'seq', split_axis=0, concat_axis=0, tiled=True)  11.4 us
    all_to_all x1, starting transfers between devices, body(): lax.all_to_all(stacked, 'seq', split_axis=0, concat_axis=0, tiled=True)  7.28 us
    pallas_call x1, Pallas kernels, filter_spectra(): vmem_call(filter_kernel, jax.ShapeDtypeStruct((BLOCKS, 2 * count, width),...  6.27 us
    ppermute x3, starting transfers between devices, swapped(): return lax.ppermute(x, 'seq', [(i, i ^ hop) for i in range(size)])  4.43 us
    all_to_all x1, starting transfers between devices, body(): back = lax.all_to_all(grads, 'seq', split_axis=0, concat_axis=0, tiled=True)  3.59 us
    convert_element_type x2, other arithmetic, split_features(): return (high.astype(jnp.bfloat16), (features - high).astype(jnp.bfloat16))  3 us
  transfers between devices with their start and end apart: 7, of which 6 were waited for; matrix products, arithmetic and copies ran while one was open for 12% of the time, Pallas kernels for 6%

commit v1 on v0

--- a/solution.py
+++ b/solution.py
@@ -13,38 +13,35 @@
 LANES = 128
 COS1, COS2, COS3 = (math.cos(math.pi / 8), math.cos(math.pi / 4), math.cos(3 * math.pi / 8))
 STEP = 16
-
-
-def class_tables():
+SENT, RETURNED = 3, 4
+LIMIT = 60
+PRODUCT_SCALE, OUTER_SCALE = 2.0**24, 2.0**-3
+
+
+def class_zero():
     points = BLOCKS * LANES * 2
     lane = np.arange(LANES)
-    forward = np.zeros((BLOCKS, 2 * LANES, 2 * LANES))
-    inverse = np.zeros((BLOCKS, 2 * LANES, 2 * LANES))
-    for residue in range(1, BLOCKS):
-        angle = 2 * np.pi * np.outer(lane, 16 * lane + residue) / points
-        cos, sin = np.cos(angle), np.sin(angle)
-        forward[residue] = np.block([[cos, -sin], [-sin, -cos]])
-        inverse[residue] = np.block([[cos.T, sin.T], [-sin.T, cos.T]]) * (2.0 / points)
     half = LANES // 2
-    for offset, first in ((0, 0), (8, half)):
+    forward = np.zeros((2 * LANES, 2 * LANES))
+    for offset, first, rows in ((0, 0, slice(0, LANES)), (8, half, slice(LANES, 2 * LANES))):
         angle = 2 * np.pi * np.outer(lane, 16 * lane[:half] + offset) / points
-        cos, sin = np.cos(angle), np.sin(angle)
-        rows = slice(0, LANES) if offset == 0 else slice(LANES, 2 * LANES)
-        re_cols, im_cols = slice(first, first + half), slice(LANES + first, LANES + first + half)
-        forward[0, rows, re_cols] = cos
-        forward[0, rows, im_cols] = -sin
-        inverse[0, re_cols, rows] = cos.T * (2.0 / points)
-        inverse[0, im_cols, rows] = -sin.T * (2.0 / points)
-    forward[0, :LANES, LANES] = (-1.0) ** lane
-    inverse[0, 0, :LANES] = 1.0 / points
-    inverse[0, LANES, :LANES] = (-1.0) ** lane / points
-    return forward, inverse
-
-
-def split_table(table):
-    high = table.astype(ml_dtypes.bfloat16)
-    low = (table - high.astype(np.float64)).astype(ml_dtypes.bfloat16)
-    return high, low
+        forward[rows, first : first + half] = np.cos(angle)
+        forward[rows, LANES + first : LANES + first + half] = -np.sin(angle)
+    forward[:LANES, LANES] = (-1.0) ** lane
+    inverse = forward.T.copy()
+    inverse[[0, LANES]] *= 0.5
+    parts = []
+    for table in (forward, inverse):
+        high = table.astype(ml_dtypes.bfloat16)
+        parts += [high, (table - high.astype(np.float64)).astype(ml_dtypes.bfloat16)]
+    return np.stack(parts)
+
+
+def angles():
+    lane = np.arange(LANES)
+    whole = 2 * np.pi * np.outer(lane, lane) / LANES
+    turn = 2 * np.pi * np.outer(lane, lane) / (2 * BLOCKS * LANES)
+    return np.stack([np.cos(whole), np.sin(whole), np.cos(turn), np.sin(turn)]).astype(np.float32)
 
 
 def fold(x):
@@ -74,15 +71,26 @@
 def unfold(z):
     (z0, z8), (r1, i1), (r2, i2), (r3, i3), (r4, i4), (r5, i5), (r6, i6), (r7, i7) = z
     even, odd = z0 + z8, z0 - z8
-    g = [even + r4, odd - i4, even - r4, odd + i4]
+    g = [even + r4, odd + i4, even - r4, odd - i4]
     dr, di = r2 - r6, i2 + i6
-    h = [r2 + r6, (dr - di) * COS2, i6 - i2, (dr + di) * -COS2]
+    h = [r2 + r6, (dr + di) * COS2, i2 - i6, (di - dr) * COS2]
     rs, rd, ts, td = r1 + r7, r1 - r7, r3 + r5, r3 - r5
     js, jd, ks, kd = i1 + i7, i1 - i7, i3 + i5, i3 - i5
     k = [None, rd * COS1 + td * COS3, (rs - ts) * COS2, rd * COS3 - td * COS1]
     m = [None, js * COS3 + ks * COS1, (jd + kd) * COS2, js * COS1 - ks * COS3]
-    o = [rs + ts, k[1] - m[1], k[2] - m[2], k[3] - m[3], kd - jd, -(k[3] + m[3]), -(k[2] + m[2]), -(k[1] + m[1])]
+    o = [rs + ts, k[1] + m[1], k[2] + m[2], k[3] + m[3], jd - kd, m[3] - k[3], m[2] - k[2], m[1] - k[1]]
     return [g[a] + h[a] + o[a] for a in range(4)] + [g[a] - h[a] + o[a + 4] for a in range(4)]
+
+
+def fourth_power(x, scale):
+    x = x * scale
+    return (x * x * (x * jnp.abs(x))).astype(jnp.bfloat16)
+
+
+def fourth_root(code, scale):
+    code = code.astype(jnp.float32)
+    size = jnp.sqrt(jnp.sqrt(jnp.abs(code))) * (1.0 / scale)
+    return jnp.where(code < 0, -size, size)
 
 
 def halves(x):
@@ -106,6 +114,25 @@
 def store_folded(hi_ref, lo_ref, rows, blocks):
     for residue, parts in enumerate(fold(blocks)):
         put(hi_ref, lo_ref, (residue, rows), parts)
+
+
+def make_table(angle, residue, table_hi, table_lo):
+    cos, sin = angle[0], angle[1]
+    turn_cos, turn_sin = angle[2, :, residue : residue + 1], angle[3, :, residue : residue + 1]
+    real = cos * turn_cos - sin * turn_sin
+    imag = -(sin * turn_cos + cos * turn_sin)
+    left, right = slice(0, LANES), slice(LANES, 2 * LANES)
+    for (rows, lanes), x in (((left, left), real), ((left, right), imag), ((right, left), imag), ((right, right), -real)):
+        high, low = halves(x)
+        table_hi[residue, rows, lanes] = high
+        table_lo[residue, rows, lanes] = low
+
+
+def times_transposed(high, low, table_hi, table_lo):
+    def dot(x, table):
+        return lax.dot_general(x, table, (((1,), (1,)), ((), ())), preferred_element_type=jnp.float32)
+
+    return dot(high, table_hi) + (dot(low, table_hi) + dot(high, table_lo))
 
 
 def times(high, low, table_hi, table_lo):
@@ -130,11 +157,18 @@
 def window_blocks(rate):
     rate = jnp.broadcast_to(rate, (rate.shape[0], LANES))
     place = lax.broadcasted_iota(jnp.int32, rate.shape, 1).astype(jnp.float32)
-    first = jnp.sqrt(2.0 * rate) * jnp.exp(-rate * place)
+    first = jnp.sqrt(2.0 * rate) * jnp.exp(-rate * place) * (1.0 / (BLOCKS * LANES))
     return [first * jnp.exp(rate * (-float(LANES) * a)) if a else first for a in range(BLOCKS)]
 
 
-def filter_kernel(proj, rate, features, table_hi, table_lo, spectra, filters, fold_hi, fold_lo):
+def fetched(sources, places, sems):
+    copies = [pltpu.make_async_copy(src, dst, sems.at[i]) for i, (src, dst) in enumerate(zip(sources, places))]
+    for copy in copies:
+        copy.start()
+    return copies
+
+
+def filter_kernel(proj, rate, features, angle, zero, spectra, filters, fold_hi, fold_lo, table_hi, table_lo):
     rows = proj.shape[0]
     for a in range(BLOCKS):
         filters[a] = jnp.dot(proj[...], features[a], preferred_element_type=jnp.float32)
@@ -145,18 +179,29 @@
         window = window_blocks(rate[at, :])
         store_folded(fold_hi, fold_lo, at, [filters[a, at, :] * window[a] for a in range(BLOCKS)])
 
-    for residue in range(BLOCKS):
+    spectra[0] = times(fold_hi[0], fold_lo[0], zero[0], zero[1])
+    for residue in range(1, BLOCKS):
+        make_table(angle, residue, table_hi, table_lo)
         spectra[residue] = times(fold_hi[residue], fold_lo[residue], table_hi[residue], table_lo[residue])
 
 
 def main_kernel(
-    moved, rate, filt, feat_hi, feat_lo, fwd_hi, fwd_lo, inv_hi, inv_lo,
-    grads, proj_grad,
-    one_hi, one_lo, two_hi, two_lo, spec, spec2, back, weighted_hi, weighted_lo,
+    moved, rate, filt, angle, zero, features,
+    results,
+    one_hi, one_lo, two_hi, two_lo, spec, spec2, back, weighted_hi, weighted_lo, table_hi, table_lo,
 ):
-    count = moved.shape[1] // 4
-    value, inner, outer, grad = (moved.at[:, i * count : (i + 1) * count] for i in range(4))
-    grad_value, grad_inner, grad_outer = (grads.at[:, i * count : (i + 1) * count] for i in range(3))
+    count = moved.shape[1] // SENT
+    value, inner, product = (moved.at[:, i * count : (i + 1) * count] for i in range(SENT))
+    grad_value, grad_inner, outer_coded = (results.at[:, i * count : (i + 1) * count] for i in range(3))
+    def forward(residue):
+        tables = (table_hi[residue], table_lo[residue]) if residue else (zero[0], zero[1])
+        return times(one_hi[residue], one_lo[residue], *tables)
+
+    def inverse(residue, rows):
+        high, low = two_hi[residue, rows, :], two_lo[residue, rows, :]
+        if residue:
+            return times_transposed(high, low, table_hi[residue], table_lo[residue])
+        return times(high, low, zero[2], zero[3])
 
     def chunk(step):
         return pl.ds(pl.multiple_of(step * STEP, STEP), STEP), pl.ds(pl.multiple_of(count + step * STEP, STEP), STEP)
@@ -170,18 +215,18 @@
     def _(step):
         at, below = chunk(step)
         store_folded(one_hi, one_lo, at, [value[a, at, :].astype(jnp.float32) for a in range(BLOCKS)])
-        store_folded(one_hi, one_lo, below, [
-            grad[a, at, :].astype(jnp.float32) * outer[a, at, :].astype(jnp.float32) for a in range(BLOCKS)])
+        store_folded(one_hi, one_lo, below, [fourth_root(product[a, at, :], PRODUCT_SCALE) for a in range(BLOCKS)])
 
     for residue in range(BLOCKS):
-        spec[residue] = times(one_hi[residue], one_lo[residue], fwd_hi[residue], fwd_lo[residue])
+        if residue:
+            make_table(angle, residue, table_hi, table_lo)
+        spec[residue] = forward(residue)
         put(two_hi, two_lo, (residue, upper), multiplied(
             pair(filt, residue, upper), pair(spec, residue, upper), False, residue))
         put(two_hi, two_lo, (residue, lower), multiplied(
             pair(filt, residue, lower), pair(spec, residue, lower), True, residue))
         rows = slice(0, 2 * count)
-        back[residue, rows, :] = times(
-            two_hi[residue, rows, :], two_lo[residue, rows, :], inv_hi[residue], inv_lo[residue])
+        back[residue, rows, :] = inverse(residue, rows)
 
     @pl.loop(0, count // STEP)
     def _(step):
@@ -195,7 +240,7 @@
         store_folded(one_hi, one_lo, below, [gate[a] * grad_mixed[a] for a in range(BLOCKS)])
 
     for residue in range(BLOCKS):
-        spec2[...] = times(one_hi[residue], one_lo[residue], fwd_hi[residue], fwd_lo[residue])
+        spec2[...] = forward(residue)
         mixed = spec2[upper, :LANES], spec2[upper, LANES:]
         inner_grad = spec2[lower, :LANES], spec2[lower, LANES:]
         products = (
@@ -206,7 +251,7 @@
         )
         for place, product in enumerate(products):
             put(two_hi, two_lo, (residue, slice(place * count, (place + 1) * count)), product)
-        back[residue] = times(two_hi[residue], two_lo[residue], inv_hi[residue], inv_lo[residue])
+        back[residue] = inverse(residue, slice(0, 4 * count))
 
     @pl.loop(0, count // STEP)
     def _(step):
@@ -217,7 +262,7 @@
         at, below = chunk(step)
         outer_act = signal(0)
         for a in range(BLOCKS):
-            grad_outer[a, at, :] = (grad[a, at, :].astype(jnp.float32) * outer_act[a]).astype(jnp.bfloat16)
+            outer_coded[a, at, :] = fourth_power(outer_act[a], OUTER_SCALE)
         value_grad = signal(1)
         for a in range(BLOCKS):
             grad_value[a, at, :] = value_grad[a].astype(jnp.bfloat16)
@@ -230,57 +275,176 @@
                 weighted_hi[rows, lanes] = high
                 weighted_lo[rows, lanes] = low
 
-    total = None
-    for place, rows in ((0, upper), (1, lower)):
-        part = times(weighted_hi[rows, :], weighted_lo[rows, :], feat_hi[place], feat_lo[place])
-        total = part if total is None else total + part
-    proj_grad[...] = total
-
-
-def vmem_call(kernel, out_shape, scratch, **extra):
+    dot = functools.partial(jnp.dot, preferred_element_type=jnp.float32)
+    total = (dot(weighted_hi[...], features[...]) + dot(weighted_lo[...], features[...])).T
+    half = total.shape[0] // 2
+    total = total[:half] + total[half:]
+    for place in range(2):
+        part = total[:, place * count : (place + 1) * count]
+        coded = (part * jnp.abs(part)).astype(jnp.bfloat16)
+        for a in range(BLOCKS):
+            results[a, 3 * count + place * half : 3 * count + (place + 1) * half] = coded
+
+
+def device_call(kernel, out_shape, scratch, in_vmem, out_vmem, name, limit):
+    def spec(inside):
+        return pl.BlockSpec(memory_space=pltpu.VMEM if inside else pl.ANY)
+
     return pl.pallas_call(
         kernel,
         out_shape=out_shape,
+        in_specs=[spec(inside) for inside in in_vmem],
+        out_specs=[spec(inside) for inside in out_vmem],
         scratch_shapes=scratch,
-        compiler_params=pltpu.CompilerParams(vmem_limit_bytes=56 * 2**20),
-        **extra,
-    )
-
-
-def filter_spectra(proj_rows, rates, features, tables):
-    count = proj_rows.shape[1]
-    twice = proj_rows.reshape(2 * count, -1)
-    twice = jnp.concatenate([twice, twice], 1)
-    high, low = split_features(features)
-    rows = jnp.concatenate([high, low], 1).reshape(BLOCKS, LANES, -1).transpose(0, 2, 1)
+        compiler_params=pltpu.CompilerParams(vmem_limit_bytes=limit * 2**20),
+        name=name,
+    )
+
+
+def filter_spectra(proj_rows, rates, terms, angle, zero):
+    rows = proj_rows.shape[0]
+    twice = jnp.concatenate([proj_rows, proj_rows], 1)
+    terms = terms.reshape(BLOCKS, LANES, -1).transpose(0, 2, 1)
     bf, f32 = jnp.bfloat16, jnp.float32
     width = 2 * LANES
-    return vmem_call(
+    return device_call(
         filter_kernel,
-        jax.ShapeDtypeStruct((BLOCKS, 2 * count, width), f32),
-        [pltpu.VMEM((BLOCKS, 2 * count, LANES), f32)] + [pltpu.VMEM((BLOCKS, 2 * count, width), bf)] * 2,
-        name="filter_spectra",
-    )(twice, rates.reshape(2 * count, 1), rows, *tables)
-
-
-def operator_grads(moved, rates, spectra, features, forward, inverse):
-    count = moved.shape[1] // 4
-    high, low = split_features(features)
-    zero = jnp.zeros_like(high)
-    placed = [jnp.stack([jnp.concatenate([x, zero], 1), jnp.concatenate([zero, x], 1)]) for x in (high, low)]
+        [jax.ShapeDtypeStruct((BLOCKS, rows, width), f32)],
+        [pltpu.VMEM((BLOCKS, rows, LANES), f32)]
+        + [pltpu.VMEM((BLOCKS, rows, width), bf)] * 2
+        + [pltpu.VMEM((BLOCKS, width, width), bf)] * 2,
+        (True,) * 5,
+        (True,),
+        "filter_spectra",
+        16,
+    )(twice, rates.reshape(rows, 1), terms, angle, zero)[0]
+
+
+def operator_grads(moved, rates, spectra, angle, zero, terms):
+    count = moved.shape[1] // SENT
     bf, f32 = jnp.bfloat16, jnp.float32
     width = 2 * LANES
-    gradients = jax.ShapeDtypeStruct((BLOCKS, 3 * count, LANES), bf)
-    return vmem_call(
+    return device_call(
         main_kernel,
-        (gradients, jax.ShapeDtypeStruct((count, 2 * features.shape[1]), f32)),
+        [jax.ShapeDtypeStruct((BLOCKS, RETURNED * count, LANES), bf)],
         [pltpu.VMEM((BLOCKS, 2 * count, width), bf)] * 2
         + [pltpu.VMEM((BLOCKS, 4 * count, width), bf)] * 2
         + [pltpu.VMEM((BLOCKS, 2 * count, width), f32), pltpu.VMEM((2 * count, width), f32),
            pltpu.VMEM((BLOCKS, 4 * count, width), f32)]
-        + [pltpu.VMEM((2 * count, BLOCKS * LANES), bf)] * 2,
-        name="operator_grads",
-    )(moved, rates.reshape(2 * count, 1), spectra, *placed, *forward, *inverse)
+        + [pltpu.VMEM((2 * count, BLOCKS * LANES), bf)] * 2
+        + [pltpu.VMEM((BLOCKS, width, width), bf)] * 2,
+        (True,) * 6,
+        (True,),
+        "operator_grads",
+        32,
+    )(moved, rates.reshape(2 * count, 1), spectra, angle, zero, terms)[0]
+
+
+def pack_kernel(value, inner, outer, grad, sent, outer_in, grad_in, sems):
+    count = sent.shape[1] // SENT
+    copies = fetched(
+        (outer, grad, value, inner),
+        (outer_in, grad_in, sent.at[:, :count], sent.at[:, count : 2 * count]),
+        sems,
+    )
+    for copy in copies[:2]:
+        copy.wait()
+    for a in range(BLOCKS):
+        both = grad_in[a].astype(jnp.float32) * outer_in[a].astype(jnp.float32)
+        sent[a, 2 * count :] = fourth_power(both, PRODUCT_SCALE)
+    for copy in copies[2:]:
+        copy.wait()
+
+
+def packed(*arrays):
+    channels, lanes = arrays[0].shape
+    count = channels // BLOCKS
+    block = pltpu.VMEM((BLOCKS, count, lanes), jnp.bfloat16)
+    return device_call(
+        pack_kernel,
+        [jax.ShapeDtypeStruct((BLOCKS, SENT * count, lanes), jnp.bfloat16)],
+        [block, block, pltpu.SemaphoreType.DMA((4,))],
+        (False,) * 4,
+        (True,),
+        "packed",
+        LIMIT,
+    )(*(x.reshape(BLOCKS, count, lanes) for x in arrays))[0]
+
+
+def sum_kernel(back, total):
+    first = 3 * (back.shape[1] // RETURNED)
+    part = jnp.zeros(total.shape, jnp.float32)
+    for a in range(BLOCKS):
+        size = jnp.abs(back[a, first:].astype(jnp.float32))
+        part = part + jnp.sum(size.reshape((-1,) + total.shape), 0)
+    total[...] = jnp.broadcast_to(jnp.sum(part, keepdims=True), total.shape)
+
+
+def square_total(back):
+    return device_call(
+        sum_kernel, [jax.ShapeDtypeStruct((8, LANES), jnp.float32)], [], (True,), (True,), "square_total", 16
+    )(back)[0]
+
+
+def unpack_kernel(back, grad, grad_value, grad_inner, grad_outer, grad_in, outer_out, sems):
+    count = back.shape[1] // RETURNED
+    copies = fetched(
+        (grad, back.at[:, :count], back.at[:, count : 2 * count]), (grad_in, grad_value, grad_inner), sems
+    )
+    copies[0].wait()
+    for a in range(BLOCKS):
+        act = fourth_root(back[a, 2 * count : 3 * count], OUTER_SCALE)
+        outer_out[a] = (grad_in[a].astype(jnp.float32) * act).astype(jnp.bfloat16)
+    last = pltpu.make_async_copy(outer_out, grad_outer, sems.at[3])
+    last.start()
+    for copy in (*copies[1:], last):
+        copy.wait()
+
+
+def unpacked(back, grad):
+    channels, lanes = grad.shape
+    count = channels // BLOCKS
+    block = jax.ShapeDtypeStruct((BLOCKS, count, lanes), jnp.bfloat16)
+    held = pltpu.VMEM(block.shape, block.dtype)
+    grads = device_call(
+        unpack_kernel,
+        [block] * 3,
+        [held, held, pltpu.SemaphoreType.DMA((4,))],
+        (True, False),
+        (False,) * 3,
+        "unpacked",
+        16,
+    )(back, grad.reshape(block.shape))
+    return [x.reshape(channels, lanes) for x in grads]
+
+
+def scale_kernel(entries, back, one, two, three, four, out, held, sem):
+    count = back.shape[1] // RETURNED
+    mean = (one[...] + two[...] + three[...] + four[...]) * (1.0 / entries) + 1e-06
+    scale = lax.rsqrt(mean)[:1]
+    features = held.shape[1]
+    for a in range(BLOCKS):
+        for place in range(2):
+            first = 3 * count + place * features
+            coded = back[a, first : first + features].astype(jnp.float32)
+            size = jnp.sqrt(jnp.abs(coded)) * scale
+            held[place, :, a * LANES : (a + 1) * LANES] = jnp.where(coded < 0, -size, size)
+    copy = pltpu.make_async_copy(held, out, sem)
+    copy.start()
+    copy.wait()
+
+
+def scaled(back, sums, entries, features):
+    shape = (2, features, BLOCKS * LANES)
+    return device_call(
+        functools.partial(scale_kernel, entries),
+        [jax.ShapeDtypeStruct(shape, jnp.float32)],
+        [pltpu.VMEM(shape, jnp.float32), pltpu.SemaphoreType.DMA],
+        (True,) * 5,
+        (False,),
+        "scaled",
+        16,
+    )(back, *sums)[0]
 
 
 highest = lax.Precision.HIGHEST
@@ -424,48 +588,33 @@
     return (value_out, inner_out, outer_out, proj_grad * scale)
 
 
-def swapped(x, hop):
-    size = lax.axis_size("seq")
-    return lax.ppermute(x, "seq", [(i, i ^ hop) for i in range(size)])
-
-
-def gathered(x):
-    place = lax.axis_index("seq")
-    hop = BLOCKS // 2
-    held = x[None]
-    while hop:
-        other = swapped(held, hop)
-        mine_first = (place & hop) == 0
-        held = jnp.where(mine_first, jnp.stack([held, other], 1), jnp.stack([other, held], 1))
-        held = held.reshape((-1,) + x.shape)
-        hop //= 2
-    return held
-
-
 def body(value_in, gate_inner, gate_outer, out_grad, filter_proj, decay, frequency):
     seq_pos = lax.axis_index("seq")
     channels, lanes = value_in.shape
     count = channels // BLOCKS
     length = BLOCKS * lanes
-    forward, inverse = ([jnp.asarray(part) for part in split_table(table)] for table in class_tables())
-    proj_rows = lax.dynamic_slice_in_dim(filter_proj, seq_pos * count, count, 1)
-    rates = lax.dynamic_slice_in_dim(decay, seq_pos * count, count, 1)
+    angle, zero = jnp.asarray(angles()), jnp.asarray(class_zero())
+
+    def own_rows(x):
+        rows = lax.dynamic_slice_in_dim(x, seq_pos * count, count, 1)
+        return rows.reshape((2 * count,) + x.shape[2:])
+
+    sent = packed(value_in, gate_inner, gate_outer, out_grad)
+    moved = lax.all_to_all(sent, "seq", split_axis=0, concat_axis=0, tiled=True)
+    rates = own_rows(decay)
     features = jnp.sin(frequency[None, :] * (lax.iota(jnp.float32, length)[:, None] + 1.0))
-    spectra = filter_spectra(proj_rows, rates, features, forward)
-    stacked = jnp.concatenate(
-        [x.reshape(BLOCKS, count, lanes) for x in (value_in, gate_inner, gate_outer, out_grad)], 1
-    )
-    moved = lax.all_to_all(stacked, "seq", split_axis=0, concat_axis=0, tiled=True)
-    grads, own_grad = operator_grads(moved, rates, spectra, features, forward, inverse)
-    back = lax.all_to_all(grads, "seq", split_axis=0, concat_axis=0, tiled=True)
-    outs = [back[:, i * count : (i + 1) * count].reshape(channels, lanes) for i in range(3)]
-    proj_grad = gathered(own_grad)
-    square_sum = jnp.sum(proj_grad * proj_grad)
-    for hop in (1, 2):
-        square_sum = square_sum + lax.ppermute(square_sum, "ch", [(i, i ^ hop) for i in range(4)])
-    scale = lax.rsqrt(square_sum / (proj_grad.size * 4) + 1e-06)
-    both = proj_grad.reshape(channels, 2, -1).transpose(1, 0, 2)
-    return (*outs, both * scale)
+    terms = jnp.concatenate(split_features(features), 1)
+    spectra = filter_spectra(own_rows(filter_proj), rates, terms, angle, zero)
+    results = operator_grads(moved, rates, spectra, angle, zero, terms)
+    back = lax.all_to_all(results, "seq", split_axis=0, concat_axis=0, tiled=True)
+    own_sum = square_total(back)
+    groups = lax.axis_size("ch")
+    sums = [own_sum] + [
+        lax.ppermute(own_sum, "ch", [(i, i ^ hop) for i in range(groups)]) for hop in range(1, groups)
+    ]
+    grads = unpacked(back, out_grad)
+    proj_grad = scaled(back, sums, filter_proj.size * groups, features.shape[1])
+    return (*grads, proj_grad.transpose(0, 2, 1))
 
 
 def solution(mesh):

time: 100 us -> 76.7 us (0.77)
  waiting for transfers between devices: 42.6 us -> 11.4 us
  blocking collectives: 0 us -> 29.4 us
  starting transfers between devices: 18.2 us -> 9.21 us
  other arithmetic: 11.1 us -> 4.01 us
  Pallas kernels: 19.8 us -> 17.4 us
  between operations: 2.7 us -> 0.8 us
  local copies, waits for them, and re-layouts: 5.34 us -> 4.01 us
    ppermute x5 -> x3, waiting for transfers between devices: 31.2 us -> 0.67 us  [body(): lax.ppermute(own_sum, 'ch', [(i, i ^ hop) for i in range(groups)])]
    all_to_all x0 -> x1, blocking collectives: none -> 29.4 us  [body(): lax.all_to_all(results, 'seq', split_axis=0, concat_axis=0, tiled=True)]
    ppermute x5 -> x3, starting transfers between devices: 7.28 us -> 1.92 us  [body(): lax.ppermute(own_sum, 'ch', [(i, i ^ hop) for i in range(groups)])]
    all_to_all x2 -> x1, starting transfers between devices: 10.9 us -> 7.29 us  [body(): moved = lax.all_to_all(sent, 'seq', split_axis=0, concat_axis=0, tiled=True)]
    pallas_call x2 -> x6, Pallas kernels: 19.8 us -> 17.4 us  [the longest x1 9.56 us: operator_grads(): device_call(main_kernel, [jax.ShapeDtypeStruct((BLOCKS, RETURNED * count,...]
    unnamed x6 -> x14, local copies, waits for them, and re-layouts: 0.98 us -> 3.06 us
    concatenate x2, other arithmetic: 3 us -> 0.94 us  [the longest x1 0.85 us: body(): terms = jnp.concatenate(split_features(features), 1)]
    select_n x3 -> x0, other arithmetic: 1.88 us -> none  [gathered(): jnp.where(mine_first, jnp.stack([held, other], 1), jnp.stack([other, held...]
  transfers between devices with their start and end apart: 7 -> 4, of which waited for: 6 -> 2; matrix products, arithmetic and copies ran while one was open for 12% -> 7% of each run, Pallas kernels for 6% -> 6%
where the time goes in v1:
time: 76.7 us; the launch traced here: 76.3 us
  blocking collectives  29.4 us (38%)
  Pallas kernels  17.4 us (23%)
  waiting for transfers between devices  11.4 us (15%)
  starting transfers between devices  9.21 us (12%)
  local copies, waits for them, and re-layouts  4.01 us (5%)
  other arithmetic  4.01 us (5%)
  between operations  0.8 us (1%)
    all_to_all x1, blocking collectives, body(): lax.all_to_all(results, 'seq', split_axis=0, concat_axis=0, tiled=True)  29.4 us
    all_to_all x1, waiting for transfers between devices, body(): moved = lax.all_to_all(sent, 'seq', split_axis=0, concat_axis=0, tiled=True)  10.7 us
    pallas_call x1, Pallas kernels, operator_grads(): device_call(main_kernel, [jax.ShapeDtypeStruct((BLOCKS, RETURNED * count,...  9.56 us
    all_to_all x1, starting transfers between devices, body(): moved = lax.all_to_all(sent, 'seq', split_axis=0, concat_axis=0, tiled=True)  7.29 us
    pallas_call x1, Pallas kernels, filter_spectra(): device_call(filter_kernel, [jax.ShapeDtypeStruct((BLOCKS, rows, width), f...  3.33 us
    unnamed x14, local copies, waits for them, and re-layouts  3.06 us
    convert_element_type x2, other arithmetic, split_features(): return (high.astype(jnp.bfloat16), (features - high).astype(jnp.bfloat16))  3.03 us
    pallas_call x1, Pallas kernels, packed(): device_call(pack_kernel, [jax.ShapeDtypeStruct((BLOCKS, SENT * count, lan...  2.18 us
  transfers between devices with their start and end apart: 4, of which 2 were waited for; matrix products, arithmetic and copies ran while one was open for 7% of the time, Pallas kernels for 6%

profile of v1, /device:TPU:0, one launch (start us, length us, event | category | flops | bytes accessed | tf_op | source)
XLA Modules:
  0.0 76.3 jit_solution(17688467624648078814)
XLA Ops:
  0.7 2.2 %packed.1 = bf16[8,384,128]{2,1,0:T(8,128)(2,1)} custom-call(bf16[8,128,128]{2,1,0:T(8,128)(2,1)} %bitcast.15, bf16[8,128,128]{2,1,0:T(8,128)(2,1)} %bitcast.16, bf16[8,128,128]{2,1,0:T(8,128)(2,1)} %bitcast.17, bf16[8,128,128]{2,1,0:T(8,128)(2,1)} %bitcast.12), custom_call_target="tpu_custom_call" | custom-call | tf_op jit(solution)/shard_map/packed/pallas_call | solution.py:363
  2.9 7.3 %all-to-all-start = ((bf16[8,384,128]{2,1,0:T(8,128)(2,1)}), bf16[8,384,128]{2,1,0:T(8,128)(2,1)S(1)}, u32[]{:S(2)}, u32[]{:S(2)}) async-start(bf16[8,384,128]{2,1,0:T(8,128)(2,1)} %packed.1), calls=%async_computation | async-start | bytes 1572864 | tf_op jit(solution)/shard_map/all_to_all | solution.py:603
  10.2 0.1 copy.17
  10.3 0.7 constant_dynamic-slice_fusion.1
  11.0 0.1 copy.20.rate
  11.2 0.1 pad_maximum_fusion.1.proj
  11.3 1.0 %reduce-precision_convert_fusion.1 = (bf16[8,128,64]{1,2,0:T(8,128)(2,1)S(1)}, bf16[8,128,64]{1,2,0:T(8,128)(2,1)S(1)}) fusion(f32[8,128]{1,0:T(8,128)S(1)} %add_add_fusion, f32[64]{0:T(128)S(1)} %copy-done.6), kind=kLoop, calls=%fused_computation.5 | loop fusion | flops 327680 | bytes 266496 | tf_op jit(solution)/shard_map/convert_element_type | solution.py:103
  12.3 1.0 %copy-done.1 = bf16[4,256,256]{2,1,0:T(8,128)(2,1)S(1)} copy-done((bf16[4,256,256]{2,1,0:T(8,128)(2,1)S(1)}, bf16[4,256,256]{2,1,0:T(8,128)(2,1)}, u32[]{:S(2)}) %copy-start.1) | copy-done | bytes 524312
  13.3 3.3 %filter_spectra.1.filt = f32[8,256,256]{2,1,0:T(8,128)S(1)} custom-call(bf16[256,128]{1,0:T(8,128)(2,1)S(1)} %pad_maximum_fusion.1.proj, f32[256,1]{1,0:T(8,128)S(1)} %copy.20.rate, bf16[8,128,128]{2,1,0:T(8,128)(2,1)S(1)} %maximum_bitcast_fusion.features, f32[4,128,128]{2,1,0:T(8,128)S(1)} %copy-done.4, bf16[4,256,256]{2,1,0:T(8,128)(2,1)S(1)} %copy-done.1), custom_call_target="tpu_custom_call" | custom-call | tf_op jit(solution)/shard_map/filter_spectra/pallas_call | solution.py:310
  16.7 2.1 %reduce-precision_convert_fusion = (bf16[1024,64]{1,0:T(8,128)(2,1)S(1)}, bf16[1024,64]{1,0:T(8,128)(2,1)S(1)}) fusion(f32[64]{0:T(128)S(1)} %copy-done.6, f32[1024]{0:T(1024)S(1)} %iota_add_fusion), kind=kLoop, calls=%fused_computation.1 | loop fusion | flops 327680 | bytes 266496 | tf_op jit(solution)/shard_map/convert_element_type | solution.py:103
  18.7 0.9 %pad_maximum_fusion.features = bf16[1024,128]{1,0:T(8,128)(2,1)} fusion(bf16[1024,64]{1,0:T(8,128)(2,1)S(1)} %get-tuple-element.11, bf16[1024,64]{1,0:T(8,128)(2,1)S(1)} %get-tuple-element.10), kind=kLoop, calls=%fused_computation.8 | loop fusion | flops 524288 | bytes 524288 | tf_op jit(solution)/shard_map/concatenate | solution.py:606
  19.6 10.7 %all-to-all-done.moved = bf16[8,384,128]{2,1,0:T(8,128)(2,1)S(1)} async-done(((bf16[8,384,128]{2,1,0:T(8,128)(2,1)}), bf16[8,384,128]{2,1,0:T(8,128)(2,1)S(1)}, u32[]{:S(2)}, u32[]{:S(2)}) %all-to-all-start) | async-done | bytes 786464 | tf_op jit(solution)/shard_map/all_to_all | solution.py:603
  30.3 1.0 %copy-done.2 = bf16[4,256,256]{2,1,0:T(8,128)(2,1)S(1)} copy-done((bf16[4,256,256]{2,1,0:T(8,128)(2,1)S(1)}, bf16[4,256,256]{2,1,0:T(8,128)(2,1)}, u32[]{:S(2)}) %copy-start.2) | copy-done | bytes 524312
  31.4 0.9 %copy-done.5 = bf16[1024,128]{1,0:T(8,128)(2,1)S(1)} copy-done((bf16[1024,128]{1,0:T(8,128)(2,1)S(1)}, bf16[1024,128]{1,0:T(8,128)(2,1)}, u32[]{:S(2)}) %copy-start.5) | copy-done | bytes 262168
  32.3 9.6 %operator_grads.1 = bf16[8,512,128]{2,1,0:T(8,128)(2,1)S(1)} custom-call(bf16[8,384,128]{2,1,0:T(8,128)(2,1)S(1)} %all-to-all-done.moved, f32[256,1]{1,0:T(8,128)S(1)} %copy.20.rate, f32[8,256,256]{2,1,0:T(8,128)S(1)} %filter_spectra.1.filt, f32[4,128,128]{2,1,0:T(8,128)S(1)} %copy-done.4, bf16[4,256,256]{2,1,0:T(8,128)(2,1)S(1)} %copy-done.2, ...), custom_call_target="tpu_custom_call" | custom-call | tf_op jit(solution)/shard_map/operator_grads/pallas_call | solution.py:327
  41.9 29.4 %all_to_all.10.back = bf16[8,512,128]{2,1,0:T(8,128)(2,1)S(1)} all-to-all(bf16[8,512,128]{2,1,0:T(8,128)(2,1)S(1)} %operator_grads.1), channel_id=1, replica_groups=mesh['seq'=8,'ch'=4] {'seq'}, dimensions={0} | all-to-all | bytes 2097152 | tf_op jit(solution)/shard_map/all_to_all | solution.py:609
  71.3 0.2 square_total.1.one
  71.5 0.1 collective-permute-start.2
  71.6 1.6 %collective-permute-start.1 = (f32[8,128]{1,0:T(8,128)S(1)}, f32[8,128]{1,0:T(8,128)S(1)}, u32[]{:S(2)}, u32[]{:S(2)}) collective-permute-start(f32[8,128]{1,0:T(8,128)S(1)} %square_total.1.one), channel_id=1, source_target_pairs={{0,2},{1,3},{2,0},{3,1},{4,6},{5,7},{6,4},{7,5},{8,10},{9,11},{10,... | collective-permute-start | bytes 12296 | tf_op jit(solution)/shard_map/ppermute | solution.py:613
  73.1 0.3 collective-permute-start
  73.4 1.1 %unpacked.1 = (bf16[8,128,128]{2,1,0:T(8,128)(2,1)}, bf16[8,128,128]{2,1,0:T(8,128)(2,1)}, bf16[8,128,128]{2,1,0:T(8,128)(2,1)}) custom-call(bf16[8,512,128]{2,1,0:T(8,128)(2,1)S(1)} %all_to_all.10.back, bf16[8,128,128]{2,1,0:T(8,128)(2,1)S(1)} %bitcast.13), custom_call_target="tpu_custom_call" | custom-call | tf_op jit(solution)/shard_map/unpacked/pallas_call | solution.py:409
  74.6 0.0 collective-permute-done.2.four
  74.6 0.7 collective-permute-done.1.three
  75.2 1.0 %scaled.1 = f32[2,64,1024]{2,1,0:T(8,128)} custom-call(bf16[8,512,128]{2,1,0:T(8,128)(2,1)S(1)} %all_to_all.10.back, f32[8,128]{1,0:T(8,128)S(1)} %square_total.1.one, f32[8,128]{1,0:T(8,128)S(1)} %collective-permute-done.two, f32[8,128]{1,0:T(8,128)S(1)} %collective-permute-done.1.three, f32[8,128]{1,0:T(8,128)S(1)} %collective-permute-done.2.four), custom_call_target="tpu_custom_call" | custom-call | tf_op jit(solution)/shard_map/scaled/pallas_call | solution.py:439
  (16 shorter events, 0.1 us)
Async XLA Ops:
  0.6 9.5 %copy-start = (bf16[2,1024,64]{1,2,0:T(8,128)(2,1)S(1)}, bf16[2,1024,64]{1,2,0:T(8,128)(2,1)}, u32[]{:S(2)}) copy-start(bf16[2,1024,64]{1,2,0:T(8,128)(2,1)} %param.13) | copy-start | bytes 786436
  0.6 10.6 %copy-start.6 = (f32[64]{0:T(128)S(1)}, f32[64]{0:T(128)}, u32[]{:S(2)}) copy-start(f32[64]{0:T(128)} %param.15) | copy-start | bytes 772
  0.7 11.6 %copy-start.4 = (f32[4,128,128]{2,1,0:T(8,128)S(1)}, f32[4,128,128]{2,1,0:T(8,128)}, u32[]{:S(2)}) copy-start(f32[4,128,128]{2,1,0:T(8,128)} %constant.20.clone.angle) | copy-start | bytes 786436
  2.9 27.5 %all-to-all-start = ((bf16[8,384,128]{2,1,0:T(8,128)(2,1)}), bf16[8,384,128]{2,1,0:T(8,128)(2,1)S(1)}, u32[]{:S(2)}, u32[]{:S(2)}) async-start(bf16[8,384,128]{2,1,0:T(8,128)(2,1)} %packed.1), calls=%async_computation | async-start | bytes 1572864 | tf_op jit(solution)/shard_map/all_to_all | solution.py:603
  12.3 1.0 %copy-start.1 = (bf16[4,256,256]{2,1,0:T(8,128)(2,1)S(1)}, bf16[4,256,256]{2,1,0:T(8,128)(2,1)}, u32[]{:S(2)}) copy-start(bf16[4,256,256]{2,1,0:T(8,128)(2,1)} %constant.21.clone.zero) | copy-start | bytes 1572868
  30.3 1.0 %copy-start.2 = (bf16[4,256,256]{2,1,0:T(8,128)(2,1)S(1)}, bf16[4,256,256]{2,1,0:T(8,128)(2,1)}, u32[]{:S(2)}) copy-start(bf16[4,256,256]{2,1,0:T(8,128)(2,1)} %constant.21.clone.zero) | copy-start | bytes 1572868
  31.4 0.9 %copy-start.5 = (bf16[1024,128]{1,0:T(8,128)(2,1)S(1)}, bf16[1024,128]{1,0:T(8,128)(2,1)}, u32[]{:S(2)}) copy-start(bf16[1024,128]{1,0:T(8,128)(2,1)} %pad_maximum_fusion.features) | copy-start | bytes 786436
  41.9 31.5 %copy-start.3 = (bf16[1024,128]{1,0:T(8,128)(2,1)S(1)}, bf16[1024,128]{1,0:T(8,128)(2,1)}, u32[]{:S(2)}) copy-start(bf16[1024,128]{1,0:T(8,128)(2,1)} %param.12) | copy-start | bytes 786436
  71.5 3.1 %collective-permute-start.2 = (f32[8,128]{1,0:T(8,128)S(1)}, f32[8,128]{1,0:T(8,128)S(1)}, u32[]{:S(2)}, u32[]{:S(2)}) collective-permute-start(f32[8,128]{1,0:T(8,128)S(1)} %square_total.1.one), channel_id=1, source_target_pairs={{0,3},{1,2},{2,1},{3,0},{4,7},{5,6},{6,5},{7,4},{8,11},{9,10},{10,... | collective-permute-start | bytes 12296 | tf_op jit(solution)/shard_map/ppermute | solution.py:613
  71.6 3.7 %collective-permute-start.1 = (f32[8,128]{1,0:T(8,128)S(1)}, f32[8,128]{1,0:T(8,128)S(1)}, u32[]{:S(2)}, u32[]{:S(2)}) collective-permute-start(f32[8,128]{1,0:T(8,128)S(1)} %square_total.1.one), channel_id=1, source_target_pairs={{0,2},{1,3},{2,0},{3,1},{4,6},{5,7},{6,4},{7,5},{8,10},{9,11},{10,... | collective-permute-start | bytes 12296 | tf_op jit(solution)/shard_map/ppermute | solution.py:613
  73.1 2.1 %collective-permute-start = (f32[8,128]{1,0:T(8,128)S(1)}, f32[8,128]{1,0:T(8,128)S(1)}, u32[]{:S(2)}, u32[]{:S(2)}) collective-permute-start(f32[8,128]{1,0:T(8,128)S(1)} %square_total.1.one), channel_id=1, source_target_pairs={{0,1},{1,0},{2,3},{3,2},{4,5},{5,4},{6,7},{7,6},{8,9},{9,8},{10,11... | collective-permute-start | bytes 12296 | tf_op jit(solution)/shard_map/ppermute | solution.py:613

commit v2 on v1

--- a/solution.py
+++ b/solution.py
@@ -13,35 +13,23 @@
 LANES = 128
 COS1, COS2, COS3 = (math.cos(math.pi / 8), math.cos(math.pi / 4), math.cos(3 * math.pi / 8))
 STEP = 16
+SIN_AT, SIGN_AT = 16, 32
+PEERS = (1, 4, 2, 6, 3, 5, 7)
 SENT, RETURNED = 3, 4
-LIMIT = 60
+PACK_LIMIT, MAIN_LIMIT = 60, 32
 PRODUCT_SCALE, OUTER_SCALE = 2.0**24, 2.0**-3
-
-
-def class_zero():
-    points = BLOCKS * LANES * 2
-    lane = np.arange(LANES)
-    half = LANES // 2
-    forward = np.zeros((2 * LANES, 2 * LANES))
-    for offset, first, rows in ((0, 0, slice(0, LANES)), (8, half, slice(LANES, 2 * LANES))):
-        angle = 2 * np.pi * np.outer(lane, 16 * lane[:half] + offset) / points
-        forward[rows, first : first + half] = np.cos(angle)
-        forward[rows, LANES + first : LANES + first + half] = -np.sin(angle)
-    forward[:LANES, LANES] = (-1.0) ** lane
-    inverse = forward.T.copy()
-    inverse[[0, LANES]] *= 0.5
-    parts = []
-    for table in (forward, inverse):
-        high = table.astype(ml_dtypes.bfloat16)
-        parts += [high, (table - high.astype(np.float64)).astype(ml_dtypes.bfloat16)]
-    return np.stack(parts)
 
 
 def angles():
     lane = np.arange(LANES)
     whole = 2 * np.pi * np.outer(lane, lane) / LANES
-    turn = 2 * np.pi * np.outer(lane, lane) / (2 * BLOCKS * LANES)
-    return np.stack([np.cos(whole), np.sin(whole), np.cos(turn), np.sin(turn)]).astype(np.float32)
+    turn = 2 * np.pi * np.outer(lane, np.arange(BLOCKS + 1)) / (2 * BLOCKS * LANES)
+    turn[:, BLOCKS] += np.pi * lane
+    columns = np.zeros((LANES, LANES))
+    columns[:, : BLOCKS + 1] = np.cos(turn)
+    columns[:, SIN_AT : SIN_AT + BLOCKS + 1] = np.sin(turn)
+    columns[:, SIGN_AT] = 1.0 - 2.0 * (lane % 2)
+    return np.stack([np.cos(whole), np.sin(whole), columns]).astype(np.float32)
 
 
 def fold(x):
@@ -117,15 +105,26 @@
 
 
 def make_table(angle, residue, table_hi, table_lo):
-    cos, sin = angle[0], angle[1]
-    turn_cos, turn_sin = angle[2, :, residue : residue + 1], angle[3, :, residue : residue + 1]
-    real = cos * turn_cos - sin * turn_sin
-    imag = -(sin * turn_cos + cos * turn_sin)
-    left, right = slice(0, LANES), slice(LANES, 2 * LANES)
-    for (rows, lanes), x in (((left, left), real), ((left, right), imag), ((right, left), imag), ((right, right), -real)):
-        high, low = halves(x)
-        table_hi[residue, rows, lanes] = high
-        table_lo[residue, rows, lanes] = low
+    def turned(column):
+        cos, sin = angle[0], angle[1]
+        turn_cos, turn_sin = angle[2, :, column : column + 1], angle[2, :, SIN_AT + column : SIN_AT + column + 1]
+        return cos * turn_cos - sin * turn_sin, -(sin * turn_cos + cos * turn_sin)
+
+    real, imag = turned(residue)
+    if residue:
+        blocks = ((real, imag), (imag, -real))
+    else:
+        lane = lax.broadcasted_iota(jnp.int32, real.shape, 1)
+        below = lane < LANES // 2
+        sign = jnp.broadcast_to(angle[2, :, SIGN_AT : SIGN_AT + 1], real.shape)
+        top = jnp.where(below, real, 0.0), jnp.where(lane == 0, sign, jnp.where(below, imag, 0.0))
+        blocks = (top, tuple(jnp.where(below, 0.0, x) for x in turned(BLOCKS)))
+    for i, row in enumerate(blocks):
+        for j, x in enumerate(row):
+            high, low = halves(x)
+            at = residue, slice(i * LANES, (i + 1) * LANES), slice(j * LANES, (j + 1) * LANES)
+            table_hi[at] = high
+            table_lo[at] = low
 
 
 def times_transposed(high, low, table_hi, table_lo):
@@ -150,7 +149,7 @@
         re, im = rr - ii, ri + ir
     if residue == 0:
         shared = lax.broadcasted_iota(jnp.int32, re.shape, 1) == 0
-        re, im = jnp.where(shared, rr, re), jnp.where(shared, ii, im)
+        re, im = jnp.where(shared, 0.5 * rr, re), jnp.where(shared, 0.5 * ii, im)
     return re, im
 
 
@@ -168,10 +167,11 @@
     return copies
 
 
-def filter_kernel(proj, rate, features, angle, zero, spectra, filters, fold_hi, fold_lo, table_hi, table_lo):
+def filter_kernel(proj, rate, features, angle, spectra, filters, fold_hi, fold_lo, table_hi, table_lo):
     rows = proj.shape[0]
     for a in range(BLOCKS):
-        filters[a] = jnp.dot(proj[...], features[a], preferred_element_type=jnp.float32)
+        terms = features[a * LANES : (a + 1) * LANES]
+        filters[a] = lax.dot_general(proj[...], terms, (((1,), (1,)), ((), ())), preferred_element_type=jnp.float32)
 
     @pl.loop(0, rows // STEP)
     def _(step):
@@ -179,29 +179,33 @@
         window = window_blocks(rate[at, :])
         store_folded(fold_hi, fold_lo, at, [filters[a, at, :] * window[a] for a in range(BLOCKS)])
 
-    spectra[0] = times(fold_hi[0], fold_lo[0], zero[0], zero[1])
-    for residue in range(1, BLOCKS):
+    for residue in range(BLOCKS):
         make_table(angle, residue, table_hi, table_lo)
         spectra[residue] = times(fold_hi[residue], fold_lo[residue], table_hi[residue], table_lo[residue])
 
 
-def main_kernel(
-    moved, rate, filt, angle, zero, features,
-    results,
-    one_hi, one_lo, two_hi, two_lo, spec, spec2, back, weighted_hi, weighted_lo, table_hi, table_lo,
-):
+def places():
+    place = lax.axis_index("seq")
+    return [place] + [place ^ peer for peer in PEERS]
+
+
+def main_kernel(*refs):
+    received, (rate, filt, angle, features), sent = refs[:BLOCKS], refs[BLOCKS : BLOCKS + 4], refs[BLOCKS + 4 : 2 * BLOCKS + 4]
+    (
+        moved, results, one_hi, one_lo, two_hi, two_lo, spec, spec2, back, weighted_hi, weighted_lo, table_hi, table_lo,
+    ) = refs[2 * BLOCKS + 4 :]
     count = moved.shape[1] // SENT
     value, inner, product = (moved.at[:, i * count : (i + 1) * count] for i in range(SENT))
     grad_value, grad_inner, outer_coded = (results.at[:, i * count : (i + 1) * count] for i in range(3))
+    for place, block in zip(places(), received):
+        moved[place] = block[...]
+
     def forward(residue):
-        tables = (table_hi[residue], table_lo[residue]) if residue else (zero[0], zero[1])
-        return times(one_hi[residue], one_lo[residue], *tables)
+        return times(one_hi[residue], one_lo[residue], table_hi[residue], table_lo[residue])
 
     def inverse(residue, rows):
-        high, low = two_hi[residue, rows, :], two_lo[residue, rows, :]
-        if residue:
-            return times_transposed(high, low, table_hi[residue], table_lo[residue])
-        return times(high, low, zero[2], zero[3])
+        return times_transposed(
+            two_hi[residue, rows, :], two_lo[residue, rows, :], table_hi[residue], table_lo[residue])
 
     def chunk(step):
         return pl.ds(pl.multiple_of(step * STEP, STEP), STEP), pl.ds(pl.multiple_of(count + step * STEP, STEP), STEP)
@@ -218,8 +222,7 @@
         store_folded(one_hi, one_lo, below, [fourth_root(product[a, at, :], PRODUCT_SCALE) for a in range(BLOCKS)])
 
     for residue in range(BLOCKS):
-        if residue:
-            make_table(angle, residue, table_hi, table_lo)
+        make_table(angle, residue, table_hi, table_lo)
         spec[residue] = forward(residue)
         put(two_hi, two_lo, (residue, upper), multiplied(
             pair(filt, residue, upper), pair(spec, residue, upper), False, residue))
@@ -284,6 +287,8 @@
         coded = (part * jnp.abs(part)).astype(jnp.bfloat16)
         for a in range(BLOCKS):
             results[a, 3 * count + place * half : 3 * count + (place + 1) * half] = coded
+    for place, block in zip(places(), sent):
+        block[...] = results[place]
 
 
 def device_call(kernel, out_shape, scratch, in_vmem, out_vmem, name, limit):
@@ -301,10 +306,9 @@
     )
 
 
-def filter_spectra(proj_rows, rates, terms, angle, zero):
+def filter_spectra(proj_rows, rates, terms, angle):
     rows = proj_rows.shape[0]
     twice = jnp.concatenate([proj_rows, proj_rows], 1)
-    terms = terms.reshape(BLOCKS, LANES, -1).transpose(0, 2, 1)
     bf, f32 = jnp.bfloat16, jnp.float32
     width = 2 * LANES
     return device_call(
@@ -313,95 +317,111 @@
         [pltpu.VMEM((BLOCKS, rows, LANES), f32)]
         + [pltpu.VMEM((BLOCKS, rows, width), bf)] * 2
         + [pltpu.VMEM((BLOCKS, width, width), bf)] * 2,
-        (True,) * 5,
+        (True,) * 4,
         (True,),
         "filter_spectra",
         16,
-    )(twice, rates.reshape(rows, 1), terms, angle, zero)[0]
-
-
-def operator_grads(moved, rates, spectra, angle, zero, terms):
-    count = moved.shape[1] // SENT
+    )(twice, rates.reshape(rows, 1), terms, angle)[0]
+
+
+def operator_grads(received, rates, spectra, angle, terms):
+    count = received[0].shape[0] // SENT
     bf, f32 = jnp.bfloat16, jnp.float32
     width = 2 * LANES
     return device_call(
         main_kernel,
-        [jax.ShapeDtypeStruct((BLOCKS, RETURNED * count, LANES), bf)],
-        [pltpu.VMEM((BLOCKS, 2 * count, width), bf)] * 2
+        [jax.ShapeDtypeStruct((RETURNED * count, LANES), bf)] * BLOCKS,
+        [pltpu.VMEM((BLOCKS, SENT * count, LANES), bf), pltpu.VMEM((BLOCKS, RETURNED * count, LANES), bf)]
+        + [pltpu.VMEM((BLOCKS, 2 * count, width), bf)] * 2
         + [pltpu.VMEM((BLOCKS, 4 * count, width), bf)] * 2
         + [pltpu.VMEM((BLOCKS, 2 * count, width), f32), pltpu.VMEM((2 * count, width), f32),
            pltpu.VMEM((BLOCKS, 4 * count, width), f32)]
         + [pltpu.VMEM((2 * count, BLOCKS * LANES), bf)] * 2
         + [pltpu.VMEM((BLOCKS, width, width), bf)] * 2,
-        (True,) * 6,
-        (True,),
+        (True,) * (BLOCKS + 4),
+        (True,) * BLOCKS,
         "operator_grads",
-        32,
-    )(moved, rates.reshape(2 * count, 1), spectra, angle, zero, terms)[0]
-
-
-def pack_kernel(value, inner, outer, grad, sent, outer_in, grad_in, sems):
-    count = sent.shape[1] // SENT
-    copies = fetched(
-        (outer, grad, value, inner),
-        (outer_in, grad_in, sent.at[:, :count], sent.at[:, count : 2 * count]),
-        sems,
-    )
-    for copy in copies[:2]:
+        MAIN_LIMIT,
+    )(*received, rates.reshape(2 * count, 1), spectra, angle, terms)
+
+
+def pack_kernel(value, inner, outer, grad, *refs):
+    sent, (outer_in, grad_in, sems) = refs[:BLOCKS], refs[BLOCKS:]
+    count = sent[0].shape[0] // SENT
+    first = fetched((outer, grad), (outer_in, grad_in), sems)
+    rest = []
+    for i, (place, block) in enumerate(zip(places(), sent)):
+        for j, source in enumerate((value, inner)):
+            copy = pltpu.make_async_copy(source.at[place], block.at[j * count : (j + 1) * count], sems.at[2 + 2 * i + j])
+            copy.start()
+            rest.append(copy)
+    for copy in first:
         copy.wait()
-    for a in range(BLOCKS):
-        both = grad_in[a].astype(jnp.float32) * outer_in[a].astype(jnp.float32)
-        sent[a, 2 * count :] = fourth_power(both, PRODUCT_SCALE)
-    for copy in copies[2:]:
+    for place, block in zip(places(), sent):
+        both = grad_in[place].astype(jnp.float32) * outer_in[place].astype(jnp.float32)
+        block[2 * count :] = fourth_power(both, PRODUCT_SCALE)
+    for copy in rest:
         copy.wait()
 
 
 def packed(*arrays):
     channels, lanes = arrays[0].shape
     count = channels // BLOCKS
-    block = pltpu.VMEM((BLOCKS, count, lanes), jnp.bfloat16)
+    held = pltpu.VMEM((BLOCKS, count, lanes), jnp.bfloat16)
     return device_call(
         pack_kernel,
-        [jax.ShapeDtypeStruct((BLOCKS, SENT * count, lanes), jnp.bfloat16)],
-        [block, block, pltpu.SemaphoreType.DMA((4,))],
+        [jax.ShapeDtypeStruct((SENT * count, lanes), jnp.bfloat16)] * BLOCKS,
+        [held, held, pltpu.SemaphoreType.DMA((2 + 2 * BLOCKS,))],
         (False,) * 4,
-        (True,),
+        (True,) * BLOCKS,
         "packed",
-        LIMIT,
-    )(*(x.reshape(BLOCKS, count, lanes) for x in arrays))[0]
-
-
-def sum_kernel(back, total):
-    first = 3 * (back.shape[1] // RETURNED)
+        PACK_LIMIT,
+    )(*(x.reshape(BLOCKS, count, lanes) for x in arrays))
+
+
+def exchanged(blocks):
+    swaps = [[(i, i ^ peer) for i in range(BLOCKS)] for peer in PEERS]
+    return [blocks[0]] + [lax.ppermute(block, "seq", swap) for block, swap in zip(blocks[1:], swaps)]
+
+
+def sum_kernel(*refs):
+    received, total = refs[:-1], refs[-1]
+    first = 3 * (received[0].shape[0] // RETURNED)
     part = jnp.zeros(total.shape, jnp.float32)
-    for a in range(BLOCKS):
-        size = jnp.abs(back[a, first:].astype(jnp.float32))
+    for block in received:
+        size = jnp.abs(block[first:].astype(jnp.float32))
         part = part + jnp.sum(size.reshape((-1,) + total.shape), 0)
     total[...] = jnp.broadcast_to(jnp.sum(part, keepdims=True), total.shape)
 
 
-def square_total(back):
+def square_total(received):
     return device_call(
-        sum_kernel, [jax.ShapeDtypeStruct((8, LANES), jnp.float32)], [], (True,), (True,), "square_total", 16
-    )(back)[0]
-
-
-def unpack_kernel(back, grad, grad_value, grad_inner, grad_outer, grad_in, outer_out, sems):
-    count = back.shape[1] // RETURNED
-    copies = fetched(
-        (grad, back.at[:, :count], back.at[:, count : 2 * count]), (grad_in, grad_value, grad_inner), sems
-    )
-    copies[0].wait()
-    for a in range(BLOCKS):
-        act = fourth_root(back[a, 2 * count : 3 * count], OUTER_SCALE)
-        outer_out[a] = (grad_in[a].astype(jnp.float32) * act).astype(jnp.bfloat16)
-    last = pltpu.make_async_copy(outer_out, grad_outer, sems.at[3])
+        sum_kernel, [jax.ShapeDtypeStruct((8, LANES), jnp.float32)], [], (True,) * BLOCKS, (True,), "square_total", 16
+    )(*received)[0]
+
+
+def unpack_kernel(*refs):
+    received, (grad, *outs), (grad_in, outer_out, sems) = refs[:BLOCKS], refs[BLOCKS : BLOCKS + 4], refs[BLOCKS + 4 :]
+    count = received[0].shape[0] // RETURNED
+    fetch = pltpu.make_async_copy(grad, grad_in, sems.at[2 * BLOCKS])
+    fetch.start()
+    copies = []
+    for i, (place, block) in enumerate(zip(places(), received)):
+        for j, out in enumerate(outs[:2]):
+            copy = pltpu.make_async_copy(block.at[j * count : (j + 1) * count], out.at[place], sems.at[2 * i + j])
+            copy.start()
+            copies.append(copy)
+    fetch.wait()
+    for place, block in zip(places(), received):
+        act = fourth_root(block[2 * count : 3 * count], OUTER_SCALE)
+        outer_out[place] = (grad_in[place].astype(jnp.float32) * act).astype(jnp.bfloat16)
+    last = pltpu.make_async_copy(outer_out, outs[2], sems.at[2 * BLOCKS + 1])
     last.start()
-    for copy in (*copies[1:], last):
+    for copy in (*copies, last):
         copy.wait()
 
 
-def unpacked(back, grad):
+def unpacked(received, grad):
     channels, lanes = grad.shape
     count = channels // BLOCKS
     block = jax.ShapeDtypeStruct((BLOCKS, count, lanes), jnp.bfloat16)
@@ -409,42 +429,46 @@
     grads = device_call(
         unpack_kernel,
         [block] * 3,
-        [held, held, pltpu.SemaphoreType.DMA((4,))],
-        (True, False),
+        [held, held, pltpu.SemaphoreType.DMA((2 * BLOCKS + 2,))],
+        (True,) * BLOCKS + (False,),
         (False,) * 3,
         "unpacked",
         16,
-    )(back, grad.reshape(block.shape))
+    )(*received, grad.reshape(block.shape))
     return [x.reshape(channels, lanes) for x in grads]
 
 
-def scale_kernel(entries, back, one, two, three, four, out, held, sem):
-    count = back.shape[1] // RETURNED
-    mean = (one[...] + two[...] + three[...] + four[...]) * (1.0 / entries) + 1e-06
-    scale = lax.rsqrt(mean)[:1]
+def scale_kernel(entries, *refs):
+    received, sums, (out, held, sem) = refs[:BLOCKS], refs[BLOCKS:-3], refs[-3:]
+    count = received[0].shape[0] // RETURNED
+    total = sums[0][...]
+    for part in sums[1:]:
+        total = total + part[...]
+    scale = lax.rsqrt(total * (1.0 / entries) + 1e-06)[:1]
     features = held.shape[1]
-    for a in range(BLOCKS):
-        for place in range(2):
-            first = 3 * count + place * features
-            coded = back[a, first : first + features].astype(jnp.float32)
+    for place, block in zip(places(), received):
+        lanes = pl.ds(pl.multiple_of(place * LANES, LANES), LANES)
+        for i in range(2):
+            first = 3 * count + i * features
+            coded = block[first : first + features].astype(jnp.float32)
             size = jnp.sqrt(jnp.abs(coded)) * scale
-            held[place, :, a * LANES : (a + 1) * LANES] = jnp.where(coded < 0, -size, size)
+            held[i, :, lanes] = jnp.where(coded < 0, -size, size)
     copy = pltpu.make_async_copy(held, out, sem)
     copy.start()
     copy.wait()
 
 
-def scaled(back, sums, entries, features):
+def scaled(received, sums, entries, features):
     shape = (2, features, BLOCKS * LANES)
     return device_call(
         functools.partial(scale_kernel, entries),
         [jax.ShapeDtypeStruct(shape, jnp.float32)],
         [pltpu.VMEM(shape, jnp.float32), pltpu.SemaphoreType.DMA],
-        (True,) * 5,
+        (True,) * (BLOCKS + len(sums)),
         (False,),
         "scaled",
         16,
-    )(back, *sums)[0]
+    )(*received, *sums)[0]
 
 
 highest = lax.Precision.HIGHEST
@@ -593,20 +617,18 @@
     channels, lanes = value_in.shape
     count = channels // BLOCKS
     length = BLOCKS * lanes
-    angle, zero = jnp.asarray(angles()), jnp.asarray(class_zero())
+    angle = jnp.asarray(angles())
 
     def own_rows(x):
         rows = lax.dynamic_slice_in_dim(x, seq_pos * count, count, 1)
         return rows.reshape((2 * count,) + x.shape[2:])
 
-    sent = packed(value_in, gate_inner, gate_outer, out_grad)
-    moved = lax.all_to_all(sent, "seq", split_axis=0, concat_axis=0, tiled=True)
+    received = exchanged(packed(value_in, gate_inner, gate_outer, out_grad))
     rates = own_rows(decay)
     features = jnp.sin(frequency[None, :] * (lax.iota(jnp.float32, length)[:, None] + 1.0))
     terms = jnp.concatenate(split_features(features), 1)
-    spectra = filter_spectra(own_rows(filter_proj), rates, terms, angle, zero)
-    results = operator_grads(moved, rates, spectra, angle, zero, terms)
-    back = lax.all_to_all(results, "seq", split_axis=0, concat_axis=0, tiled=True)
+    spectra = filter_spectra(own_rows(filter_proj), rates, terms, angle)
+    back = exchanged(operator_grads(received, rates, spectra, angle, terms))
     own_sum = square_total(back)
     groups = lax.axis_size("ch")
     sums = [own_sum] + [

time: 76.7 us -> 65.5 us (0.85)
  blocking collectives: 29.4 us -> 0 us
  starting transfers between devices: 9.21 us -> 25.8 us
  waiting for transfers between devices: 11.4 us -> 16.6 us
  local copies, waits for them, and re-layouts: 4.01 us -> 0.97 us
  other arithmetic: 4.01 us -> 3.01 us
    all_to_all x1 -> x0, blocking collectives: 29.4 us -> none  [body(): lax.all_to_all(results, 'seq', split_axis=0, concat_axis=0, tiled=True)]
    ppermute x0 -> x14, starting transfers between devices: none -> 23.9 us  [exchanged(): lax.ppermute(block, 'seq', swap)]
    ppermute x0 -> x14, waiting for transfers between devices: none -> 16.1 us  [exchanged(): lax.ppermute(block, 'seq', swap)]
    all_to_all x1 -> x0, waiting for transfers between devices: 10.7 us -> none  [body(): moved = lax.all_to_all(sent, 'seq', split_axis=0, concat_axis=0, tiled=True)]
    all_to_all x1 -> x0, starting transfers between devices: 7.29 us -> none  [body(): moved = lax.all_to_all(sent, 'seq', split_axis=0, concat_axis=0, tiled=True)]
    unnamed x14 -> x8, local copies, waits for them, and re-layouts: 3.06 us -> 0.03 us
    convert_element_type x2 -> x1, other arithmetic: 3.03 us -> 2.76 us  [split_features(): return (high.astype(jnp.bfloat16), (features - high).astype(jnp.bfloat16))]
  transfers between devices with their start and end apart: 4 -> 17, of which waited for: 2 -> 7; matrix products, arithmetic and copies ran while one was open for 7% -> 6% of each run, Pallas kernels for 6% -> 7%
where the time goes in v2:
time: 65.5 us; the launch traced here: 65.3 us
  starting transfers between devices  25.8 us (39%)
  Pallas kernels  18.1 us (28%)
  waiting for transfers between devices  16.6 us (25%)
  other arithmetic  3.01 us (5%)
  local copies, waits for them, and re-layouts  0.97 us (1%)
  between operations  0.8 us (1%)
    ppermute x14, starting transfers between devices, exchanged(): lax.ppermute(block, 'seq', swap)  23.9 us
    ppermute x14, waiting for transfers between devices, exchanged(): lax.ppermute(block, 'seq', swap)  16.1 us
    pallas_call x1, Pallas kernels, operator_grads(): device_call(main_kernel, [jax.ShapeDtypeStruct((RETURNED * count, LANES),...  9.8 us
    pallas_call x1, Pallas kernels, filter_spectra(): device_call(filter_kernel, [jax.ShapeDtypeStruct((BLOCKS, rows, width), f...  3.48 us
    convert_element_type x1, other arithmetic, split_features(): return (high.astype(jnp.bfloat16), (features - high).astype(jnp.bfloat16))  2.76 us
    pallas_call x1, Pallas kernels, packed(): device_call(pack_kernel, [jax.ShapeDtypeStruct((SENT * count, lanes), jnp...  2.28 us
    ppermute x3, starting transfers between devices, body(): lax.ppermute(own_sum, 'ch', [(i, i ^ hop) for i in range(groups)])  1.92 us
  transfers between devices with their start and end apart: 17, of which 7 were waited for; matrix products, arithmetic and copies ran while one was open for 6% of the time, Pallas kernels for 7%

profile of v2, /device:TPU:0, one launch (start us, length us, event | category | flops | bytes accessed | tf_op | source)
XLA Modules:
  0.0 65.3 jit_solution(8591054787453845878)
XLA Ops:
  0.7 2.3 %packed.1 = (bf16[384,128]{1,0:T(8,128)(2,1)}, bf16[384,128]{1,0:T(8,128)(2,1)}, bf16[384,128]{1,0:T(8,128)(2,1)}, bf16[384,128]{1,0:T(8,128)(2,1)}, bf16[384,12...) custom-call(bf16[8,128,128]{2,1,0:T(8,128)(2,1)} %bitcast.14, ...), custom_call_target="tpu_custom_call" | custom-call | tf_op jit(solution)/shard_map/packed/pallas_call | solution.py:371
  3.0 3.0 %collective-permute-start = (bf16[384,128]{1,0:T(8,128)(2,1)}, bf16[384,128]{1,0:T(8,128)(2,1)S(1)}, u32[]{:S(2)}, u32[]{:S(2)}) collective-permute-start(bf16[384,128]{1,0:T(8,128)(2,1)} %get-tuple-element.24), channel_id=1, source_target_pairs={{0,4},{4,0},{8,12},{12,8},{16,20},{20,16},{24,28},{28,24},{1,5},{5... | collective-permute-start | bytes 294920 | tf_op jit(solution)/shard_map/ppermute | solution.py:384
  6.0 2.6 %collective-permute-start.1 = (bf16[384,128]{1,0:T(8,128)(2,1)}, bf16[384,128]{1,0:T(8,128)(2,1)S(1)}, u32[]{:S(2)}, u32[]{:S(2)}) collective-permute-start(bf16[384,128]{1,0:T(8,128)(2,1)} %get-tuple-element.25), channel_id=1, source_target_pairs={{0,16},{4,20},{8,24},{12,28},{16,0},{20,4},{24,8},{28,12},{1,17},{... | collective-permute-start | bytes 294920 | tf_op jit(solution)/shard_map/ppermute | solution.py:384
  8.6 1.6 %collective-permute-start.2 = (bf16[384,128]{1,0:T(8,128)(2,1)}, bf16[384,128]{1,0:T(8,128)(2,1)S(1)}, u32[]{:S(2)}, u32[]{:S(2)}) collective-permute-start(bf16[384,128]{1,0:T(8,128)(2,1)} %get-tuple-element.26), channel_id=1, source_target_pairs={{0,8},{4,12},{8,0},{12,4},{16,24},{20,28},{24,16},{28,20},{1,9},{5... | collective-permute-start | bytes 294920 | tf_op jit(solution)/shard_map/ppermute | solution.py:384
  10.4 0.6 collective-permute-start.4
  11.0 0.7 %constant_dynamic-slice_fusion.1 = f32[2,128]{1,0:T(2,128)S(1)} fusion(f32[2,1024]{1,0:T(2,128)} %param.13, s32[]{:T(128)S(6)} %select_n.4), kind=kLoop, calls=%fused_computation.8 | loop fusion | bytes 2052 | tf_op jit(solution)/shard_map/dynamic_slice | solution.py:623
  12.0 2.8 %reduce-precision_convert_fusion = (bf16[1024,64]{1,0:T(8,128)(2,1)S(1)}, bf16[1024,64]{1,0:T(8,128)(2,1)S(1)}) fusion(f32[64]{0:T(128)} %param.14, f32[1024]{0:T(1024)S(1)} %iota_add_fusion), kind=kLoop, calls=%fused_computation.1 | loop fusion | flops 327680 | bytes 266496 | tf_op jit(solution)/shard_map/convert_element_type | solution.py:91
  14.9 4.5 %collective-permute-start.5 = (bf16[384,128]{1,0:T(8,128)(2,1)}, bf16[384,128]{1,0:T(8,128)(2,1)S(1)}, u32[]{:S(2)}, u32[]{:S(2)}) collective-permute-start(bf16[384,128]{1,0:T(8,128)(2,1)} %get-tuple-element.29), channel_id=1, source_target_pairs={{0,20},{4,16},{8,28},{12,24},{16,4},{20,0},{24,12},{28,8},{1,21},{... | collective-permute-start | bytes 294920 | tf_op jit(solution)/shard_map/ppermute | solution.py:384
  19.5 3.5 %filter_spectra.1.refs_9_ = f32[8,256,256]{2,1,0:T(8,128)S(1)} custom-call(bf16[256,128]{1,0:T(8,128)(2,1)S(1)} %pad_maximum_fusion.1.proj, f32[256,1]{1,0:T(8,128)S(1)} %copy.19.rate.refs_8_, bf16[1024,128]{1,0:T(8,128)(2,1)S(1)} %pad_maximum_fusion.features.refs_11_, f32[3,128,128]{2,1,0:T(8,128)S(1)} %copy-done.2), custom_call_target="tpu_custom_call" | custom-call | tf_op jit(solution)/shard_map/filter_spectra/pallas_call | solution.py:314
  23.1 2.1 %collective-permute-done.5.refs_6_ = bf16[384,128]{1,0:T(8,128)(2,1)S(1)} collective-permute-done((bf16[384,128]{1,0:T(8,128)(2,1)}, bf16[384,128]{1,0:T(8,128)(2,1)S(1)}, u32[]{:S(2)}, u32[]{:S(2)}) %collective-permute-start.5) | collective-permute-done | bytes 98336 | tf_op jit(solution)/shard_map/ppermute | solution.py:384
  25.2 1.9 %collective-permute-done.6.refs_7_ = bf16[384,128]{1,0:T(8,128)(2,1)S(1)} collective-permute-done((bf16[384,128]{1,0:T(8,128)(2,1)}, bf16[384,128]{1,0:T(8,128)(2,1)S(1)}, u32[]{:S(2)}, u32[]{:S(2)}) %collective-permute-start.6) | collective-permute-done | bytes 98336 | tf_op jit(solution)/shard_map/ppermute | solution.py:384
  27.1 9.8 %operator_grads.1 = (bf16[512,128]{1,0:T(8,128)(2,1)S(1)}, bf16[512,128]{1,0:T(8,128)(2,1)S(1)}, bf16[512,128]{1,0:T(8,128)(2,1)S(1)}, bf16[512,128]{1,0:T(8,128...) custom-call(bf16[384,128]{1,0:T(8,128)(2,1)S(1)} %copy-done.3, ...), custom_call_target="tpu_custom_call" | custom-call | tf_op jit(solution)/shard_map/operator_grads/pallas_call | solution.py:331
  37.4 2.6 %collective-permute-start.8 = (bf16[512,128]{1,0:T(8,128)(2,1)S(1)}, bf16[512,128]{1,0:T(8,128)(2,1)S(1)}, u32[]{:S(2)}, u32[]{:S(2)}) collective-permute-start(bf16[512,128]{1,0:T(8,128)(2,1)S(1)} %get-tuple-element.33), channel_id=1, source_target_pairs={{0,16},{4,20},{8,24},{12,28},{16,0},{20,4},{24,8},{28,12},{1,17},{... | collective-permute-start | bytes 393224 | tf_op jit(solution)/shard_map/ppermute | solution.py:384
  40.5 1.4 %collective-permute-start.10 = (bf16[512,128]{1,0:T(8,128)(2,1)S(1)}, bf16[512,128]{1,0:T(8,128)(2,1)S(1)}, u32[]{:S(2)}, u32[]{:S(2)}) collective-permute-start(bf16[512,128]{1,0:T(8,128)(2,1)S(1)} %get-tuple-element.35), channel_id=1, source_target_pairs={{0,24},{4,28},{8,16},{12,20},{16,8},{20,12},{24,0},{28,4},{1,25},{... | collective-permute-start | bytes 393224 | tf_op jit(solution)/shard_map/ppermute | solution.py:384
  41.8 0.9 %collective-permute-start.11 = (bf16[512,128]{1,0:T(8,128)(2,1)S(1)}, bf16[512,128]{1,0:T(8,128)(2,1)S(1)}, u32[]{:S(2)}, u32[]{:S(2)}) collective-permute-start(bf16[512,128]{1,0:T(8,128)(2,1)S(1)} %get-tuple-element.36), channel_id=1, source_target_pairs={{0,12},{4,8},{8,4},{12,0},{16,28},{20,24},{24,20},{28,16},{1,13},{... | collective-permute-start | bytes 393224 | tf_op jit(solution)/shard_map/ppermute | solution.py:384
  42.7 3.1 %collective-permute-start.12 = (bf16[512,128]{1,0:T(8,128)(2,1)S(1)}, bf16[512,128]{1,0:T(8,128)(2,1)S(1)}, u32[]{:S(2)}, u32[]{:S(2)}) collective-permute-start(bf16[512,128]{1,0:T(8,128)(2,1)S(1)} %get-tuple-element.37), channel_id=1, source_target_pairs={{0,20},{4,16},{8,28},{12,24},{16,4},{20,0},{24,12},{28,8},{1,21},{... | collective-permute-start | bytes 393224 | tf_op jit(solution)/shard_map/ppermute | solution.py:384
  45.7 1.8 %collective-permute-done.8.refs_2_ = bf16[512,128]{1,0:T(8,128)(2,1)S(1)} collective-permute-done((bf16[512,128]{1,0:T(8,128)(2,1)S(1)}, bf16[512,128]{1,0:T(8,128)(2,1)S(1)}, u32[]{:S(2)}, u32[]{:S(2)}) %collective-permute-start.8) | collective-permute-done | bytes 131104 | tf_op jit(solution)/shard_map/ppermute | solution.py:384
  47.6 2.5 %collective-permute-start.13 = (bf16[512,128]{1,0:T(8,128)(2,1)S(1)}, bf16[512,128]{1,0:T(8,128)(2,1)S(1)}, u32[]{:S(2)}, u32[]{:S(2)}) collective-permute-start(bf16[512,128]{1,0:T(8,128)(2,1)S(1)} %get-tuple-element.38), channel_id=1, source_target_pairs={{0,28},{4,24},{8,20},{12,16},{16,12},{20,8},{24,4},{28,0},{1,29},{... | collective-permute-start | bytes 393224 | tf_op jit(solution)/shard_map/ppermute | solution.py:384
  50.1 0.8 %collective-permute-done.10.refs_4_ = bf16[512,128]{1,0:T(8,128)(2,1)S(1)} collective-permute-done((bf16[512,128]{1,0:T(8,128)(2,1)S(1)}, bf16[512,128]{1,0:T(8,128)(2,1)S(1)}, u32[]{:S(2)}, u32[]{:S(2)}) %collective-permute-start.10) | collective-permute-done | bytes 131104 | tf_op jit(solution)/shard_map/ppermute | solution.py:384
  50.9 3.4 %collective-permute-done.11.refs_5_ = bf16[512,128]{1,0:T(8,128)(2,1)S(1)} collective-permute-done((bf16[512,128]{1,0:T(8,128)(2,1)S(1)}, bf16[512,128]{1,0:T(8,128)(2,1)S(1)}, u32[]{:S(2)}, u32[]{:S(2)}) %collective-permute-start.11) | collective-permute-done | bytes 131104 | tf_op jit(solution)/shard_map/ppermute | solution.py:384
  54.3 6.1 %collective-permute-done.12.refs_6_ = bf16[512,128]{1,0:T(8,128)(2,1)S(1)} collective-permute-done((bf16[512,128]{1,0:T(8,128)(2,1)S(1)}, bf16[512,128]{1,0:T(8,128)(2,1)S(1)}, u32[]{:S(2)}, u32[]{:S(2)}) %collective-permute-start.12) | collective-permute-done | bytes 131104 | tf_op jit(solution)/shard_map/ppermute | solution.py:384
  60.6 1.6 %collective-permute-start.15 = (f32[8,128]{1,0:T(8,128)S(1)}, f32[8,128]{1,0:T(8,128)S(1)}, u32[]{:S(2)}, u32[]{:S(2)}) collective-permute-start(f32[8,128]{1,0:T(8,128)S(1)} %square_total.1.refs_8_), channel_id=1, source_target_pairs={{0,2},{1,3},{2,0},{3,1},{4,6},{5,7},{6,4},{7,5},{8,10},{9,11},{10,... | collective-permute-start | bytes 12296 | tf_op jit(solution)/shard_map/ppermute | solution.py:635
  62.5 1.3 %unpacked.1 = (bf16[8,128,128]{2,1,0:T(8,128)(2,1)}, bf16[8,128,128]{2,1,0:T(8,128)(2,1)}, bf16[8,128,128]{2,1,0:T(8,128)(2,1)}) custom-call(bf16[512,128]{1,0:T(8,128)(2,1)S(1)} %get-tuple-element.31.refs_0_, bf16[512,128]{1,0:T(8,128)(2,1)S(1)} %collective-permute-done.7.refs_1_, bf16[512,128]{1,0:T(8,128)(2,1)S(1)} %collective-permute-done.8.refs_2_, ...), custom_call_target="tpu_custom_call" | custom-call | tf_op jit(solution)/shard_map/unpacked/pallas_call | solution.py:429
  64.3 1.0 %scaled.1 = f32[2,64,1024]{2,1,0:T(8,128)} custom-call(bf16[512,128]{1,0:T(8,128)(2,1)S(1)} %get-tuple-element.31.refs_0_, bf16[512,128]{1,0:T(8,128)(2,1)S(1)} %collective-permute-done.7.refs_1_, bf16[512,128]{1,0:T(8,128)(2,1)S(1)} %collective-permute-done.8.refs_2_, bf16[512,128]{1,0:T(8,128)(2,1)S(1)} %collective-permute-done.9.refs_3_, ...), custom_call_target="tpu_custom_call" | custom-call | tf_op jit(solution)/shard_map/scaled/pallas_call | solution.py:463
  (32 shorter events, 2.8 us)
Async XLA Ops:
  0.6 11.1 %copy-start = (bf16[2,1024,64]{1,2,0:T(8,128)(2,1)S(1)}, bf16[2,1024,64]{1,2,0:T(8,128)(2,1)}, u32[]{:S(2)}) copy-start(bf16[2,1024,64]{1,2,0:T(8,128)(2,1)} %param.12) | copy-start | bytes 786436
  0.6 18.9 %copy-start.2 = (f32[3,128,128]{2,1,0:T(8,128)S(1)}, f32[3,128,128]{2,1,0:T(8,128)}, u32[]{:S(2)}) copy-start(f32[3,128,128]{2,1,0:T(8,128)} %constant.16.clone.angle.refs_10_) | copy-start | bytes 589828
  3.0 12.0 %collective-permute-start = (bf16[384,128]{1,0:T(8,128)(2,1)}, bf16[384,128]{1,0:T(8,128)(2,1)S(1)}, u32[]{:S(2)}, u32[]{:S(2)}) collective-permute-start(bf16[384,128]{1,0:T(8,128)(2,1)} %get-tuple-element.24), channel_id=1, source_target_pairs={{0,4},{4,0},{8,12},{12,8},{16,20},{20,16},{24,28},{28,24},{1,5},{5... | collective-permute-start | bytes 294920 | tf_op jit(solution)/shard_map/ppermute | solution.py:384
  6.0 13.4 %collective-permute-start.1 = (bf16[384,128]{1,0:T(8,128)(2,1)}, bf16[384,128]{1,0:T(8,128)(2,1)S(1)}, u32[]{:S(2)}, u32[]{:S(2)}) collective-permute-start(bf16[384,128]{1,0:T(8,128)(2,1)} %get-tuple-element.25), channel_id=1, source_target_pairs={{0,16},{4,20},{8,24},{12,28},{16,0},{20,4},{24,8},{28,12},{1,17},{... | collective-permute-start | bytes 294920 | tf_op jit(solution)/shard_map/ppermute | solution.py:384
  8.6 14.5 %collective-permute-start.2 = (bf16[384,128]{1,0:T(8,128)(2,1)}, bf16[384,128]{1,0:T(8,128)(2,1)S(1)}, u32[]{:S(2)}, u32[]{:S(2)}) collective-permute-start(bf16[384,128]{1,0:T(8,128)(2,1)} %get-tuple-element.26), channel_id=1, source_target_pairs={{0,8},{4,12},{8,0},{12,4},{16,24},{20,28},{24,16},{28,20},{1,9},{5... | collective-permute-start | bytes 294920 | tf_op jit(solution)/shard_map/ppermute | solution.py:384
  10.2 12.9 %collective-permute-start.3 = (bf16[384,128]{1,0:T(8,128)(2,1)}, bf16[384,128]{1,0:T(8,128)(2,1)S(1)}, u32[]{:S(2)}, u32[]{:S(2)}) collective-permute-start(bf16[384,128]{1,0:T(8,128)(2,1)} %get-tuple-element.27), channel_id=1, source_target_pairs={{0,24},{4,28},{8,16},{12,20},{16,8},{20,12},{24,0},{28,4},{1,25},{... | collective-permute-start | bytes 294920 | tf_op jit(solution)/shard_map/ppermute | solution.py:384
  10.4 12.7 %collective-permute-start.4 = (bf16[384,128]{1,0:T(8,128)(2,1)}, bf16[384,128]{1,0:T(8,128)(2,1)S(1)}, u32[]{:S(2)}, u32[]{:S(2)}) collective-permute-start(bf16[384,128]{1,0:T(8,128)(2,1)} %get-tuple-element.28), channel_id=1, source_target_pairs={{0,12},{4,8},{8,4},{12,0},{16,28},{20,24},{24,20},{28,16},{1,13},{... | collective-permute-start | bytes 294920 | tf_op jit(solution)/shard_map/ppermute | solution.py:384
  12.0 15.1 %copy-start.3 = (bf16[384,128]{1,0:T(8,128)(2,1)S(1)}, bf16[384,128]{1,0:T(8,128)(2,1)}, u32[]{:S(2)}) copy-start(bf16[384,128]{1,0:T(8,128)(2,1)} %get-tuple-element.23.refs_0_) | copy-start | bytes 294916
  14.9 10.3 %collective-permute-start.5 = (bf16[384,128]{1,0:T(8,128)(2,1)}, bf16[384,128]{1,0:T(8,128)(2,1)S(1)}, u32[]{:S(2)}, u32[]{:S(2)}) collective-permute-start(bf16[384,128]{1,0:T(8,128)(2,1)} %get-tuple-element.29), channel_id=1, source_target_pairs={{0,20},{4,16},{8,28},{12,24},{16,4},{20,0},{24,12},{28,8},{1,21},{... | collective-permute-start | bytes 294920 | tf_op jit(solution)/shard_map/ppermute | solution.py:384
  19.4 7.6 %collective-permute-start.6 = (bf16[384,128]{1,0:T(8,128)(2,1)}, bf16[384,128]{1,0:T(8,128)(2,1)S(1)}, u32[]{:S(2)}, u32[]{:S(2)}) collective-permute-start(bf16[384,128]{1,0:T(8,128)(2,1)} %get-tuple-element.30), channel_id=1, source_target_pairs={{0,28},{4,24},{8,20},{12,16},{16,12},{20,8},{24,4},{28,0},{1,29},{... | collective-permute-start | bytes 294920 | tf_op jit(solution)/shard_map/ppermute | solution.py:384
  27.1 35.4 %copy-start.1 = (bf16[1024,128]{1,0:T(8,128)(2,1)S(1)}, bf16[1024,128]{1,0:T(8,128)(2,1)}, u32[]{:S(2)}) copy-start(bf16[1024,128]{1,0:T(8,128)(2,1)} %param.11) | copy-start | bytes 786436
  36.9 5.8 %collective-permute-start.7 = (bf16[512,128]{1,0:T(8,128)(2,1)S(1)}, bf16[512,128]{1,0:T(8,128)(2,1)S(1)}, u32[]{:S(2)}, u32[]{:S(2)}) collective-permute-start(bf16[512,128]{1,0:T(8,128)(2,1)S(1)} %get-tuple-element.32), channel_id=1, source_target_pairs={{0,4},{4,0},{8,12},{12,8},{16,20},{20,16},{24,28},{28,24},{1,5},{5... | collective-permute-start | bytes 393224 | tf_op jit(solution)/shard_map/ppermute | solution.py:384
  37.4 10.1 %collective-permute-start.8 = (bf16[512,128]{1,0:T(8,128)(2,1)S(1)}, bf16[512,128]{1,0:T(8,128)(2,1)S(1)}, u32[]{:S(2)}, u32[]{:S(2)}) collective-permute-start(bf16[512,128]{1,0:T(8,128)(2,1)S(1)} %get-tuple-element.33), channel_id=1, source_target_pairs={{0,16},{4,20},{8,24},{12,28},{16,0},{20,4},{24,8},{28,12},{1,17},{... | collective-permute-start | bytes 393224 | tf_op jit(solution)/shard_map/ppermute | solution.py:384
  40.0 10.1 %collective-permute-start.9 = (bf16[512,128]{1,0:T(8,128)(2,1)S(1)}, bf16[512,128]{1,0:T(8,128)(2,1)S(1)}, u32[]{:S(2)}, u32[]{:S(2)}) collective-permute-start(bf16[512,128]{1,0:T(8,128)(2,1)S(1)} %get-tuple-element.34), channel_id=1, source_target_pairs={{0,8},{4,12},{8,0},{12,4},{16,24},{20,28},{24,16},{28,20},{1,9},{5... | collective-permute-start | bytes 393224 | tf_op jit(solution)/shard_map/ppermute | solution.py:384
  40.5 10.4 %collective-permute-start.10 = (bf16[512,128]{1,0:T(8,128)(2,1)S(1)}, bf16[512,128]{1,0:T(8,128)(2,1)S(1)}, u32[]{:S(2)}, u32[]{:S(2)}) collective-permute-start(bf16[512,128]{1,0:T(8,128)(2,1)S(1)} %get-tuple-element.35), channel_id=1, source_target_pairs={{0,24},{4,28},{8,16},{12,20},{16,8},{20,12},{24,0},{28,4},{1,25},{... | collective-permute-start | bytes 393224 | tf_op jit(solution)/shard_map/ppermute | solution.py:384
  41.8 12.5 %collective-permute-start.11 = (bf16[512,128]{1,0:T(8,128)(2,1)S(1)}, bf16[512,128]{1,0:T(8,128)(2,1)S(1)}, u32[]{:S(2)}, u32[]{:S(2)}) collective-permute-start(bf16[512,128]{1,0:T(8,128)(2,1)S(1)} %get-tuple-element.36), channel_id=1, source_target_pairs={{0,12},{4,8},{8,4},{12,0},{16,28},{20,24},{24,20},{28,16},{1,13},{... | collective-permute-start | bytes 393224 | tf_op jit(solution)/shard_map/ppermute | solution.py:384
  42.7 17.7 %collective-permute-start.12 = (bf16[512,128]{1,0:T(8,128)(2,1)S(1)}, bf16[512,128]{1,0:T(8,128)(2,1)S(1)}, u32[]{:S(2)}, u32[]{:S(2)}) collective-permute-start(bf16[512,128]{1,0:T(8,128)(2,1)S(1)} %get-tuple-element.37), channel_id=1, source_target_pairs={{0,20},{4,16},{8,28},{12,24},{16,4},{20,0},{24,12},{28,8},{1,21},{... | collective-permute-start | bytes 393224 | tf_op jit(solution)/shard_map/ppermute | solution.py:384
  47.6 12.8 %collective-permute-start.13 = (bf16[512,128]{1,0:T(8,128)(2,1)S(1)}, bf16[512,128]{1,0:T(8,128)(2,1)S(1)}, u32[]{:S(2)}, u32[]{:S(2)}) collective-permute-start(bf16[512,128]{1,0:T(8,128)(2,1)S(1)} %get-tuple-element.38), channel_id=1, source_target_pairs={{0,28},{4,24},{8,20},{12,16},{16,12},{20,8},{24,4},{28,0},{1,29},{... | collective-permute-start | bytes 393224 | tf_op jit(solution)/shard_map/ppermute | solution.py:384
  60.6 3.2 %collective-permute-start.16 = (f32[8,128]{1,0:T(8,128)S(1)}, f32[8,128]{1,0:T(8,128)S(1)}, u32[]{:S(2)}, u32[]{:S(2)}) collective-permute-start(f32[8,128]{1,0:T(8,128)S(1)} %square_total.1.refs_8_), channel_id=1, source_target_pairs={{0,3},{1,2},{2,1},{3,0},{4,7},{5,6},{6,5},{7,4},{8,11},{9,10},{10,... | collective-permute-start | bytes 12296 | tf_op jit(solution)/shard_map/ppermute | solution.py:635
  60.6 3.7 %collective-permute-start.15 = (f32[8,128]{1,0:T(8,128)S(1)}, f32[8,128]{1,0:T(8,128)S(1)}, u32[]{:S(2)}, u32[]{:S(2)}) collective-permute-start(f32[8,128]{1,0:T(8,128)S(1)} %square_total.1.refs_8_), channel_id=1, source_target_pairs={{0,2},{1,3},{2,0},{3,1},{4,6},{5,7},{6,4},{7,5},{8,10},{9,11},{10,... | collective-permute-start | bytes 12296 | tf_op jit(solution)/shard_map/ppermute | solution.py:635
  62.2 2.1 %collective-permute-start.14 = (f32[8,128]{1,0:T(8,128)S(1)}, f32[8,128]{1,0:T(8,128)S(1)}, u32[]{:S(2)}, u32[]{:S(2)}) collective-permute-start(f32[8,128]{1,0:T(8,128)S(1)} %square_total.1.refs_8_), channel_id=1, source_target_pairs={{0,1},{1,0},{2,3},{3,2},{4,5},{5,4},{6,7},{7,6},{8,9},{9,8},{10,11... | collective-permute-start | bytes 12296 | tf_op jit(solution)/shard_map/ppermute | solution.py:635

commit v3 on v2

--- a/solution.py
+++ b/solution.py
@@ -14,7 +14,10 @@
 COS1, COS2, COS3 = (math.cos(math.pi / 8), math.cos(math.pi / 4), math.cos(3 * math.pi / 8))
 STEP = 16
 SIN_AT, SIGN_AT = 16, 32
-PEERS = (1, 4, 2, 6, 3, 5, 7)
+FIRST_PEERS = (1, 4, 2, 6, 3, 5, 7)
+LAST_PEERS = (1, 4, 6, 2, 5, 7, 3)
+HELD_FOR = (1,)
+NEAR = 1
 SENT, RETURNED = 3, 4
 PACK_LIMIT, MAIN_LIMIT = 60, 32
 PRODUCT_SCALE, OUTER_SCALE = 2.0**24, 2.0**-3
@@ -184,9 +187,13 @@
         spectra[residue] = times(fold_hi[residue], fold_lo[residue], table_hi[residue], table_lo[residue])
 
 
-def places():
+def direct(peer):
+    return not peer & NEAR
+
+
+def places(peers):
     place = lax.axis_index("seq")
-    return [place] + [place ^ peer for peer in PEERS]
+    return [place] + [place ^ peer for peer in peers]
 
 
 def main_kernel(*refs):
@@ -197,7 +204,7 @@
     count = moved.shape[1] // SENT
     value, inner, product = (moved.at[:, i * count : (i + 1) * count] for i in range(SENT))
     grad_value, grad_inner, outer_coded = (results.at[:, i * count : (i + 1) * count] for i in range(3))
-    for place, block in zip(places(), received):
+    for place, block in zip(places(FIRST_PEERS), received):
         moved[place] = block[...]
 
     def forward(residue):
@@ -215,7 +222,7 @@
 
     upper, lower = slice(0, count), slice(count, 2 * count)
 
-    @pl.loop(0, count // STEP)
+    @pl.loop(0, count // STEP, unroll=count // STEP)
     def _(step):
         at, below = chunk(step)
         store_folded(one_hi, one_lo, at, [value[a, at, :].astype(jnp.float32) for a in range(BLOCKS)])
@@ -231,7 +238,7 @@
         rows = slice(0, 2 * count)
         back[residue, rows, :] = inverse(residue, rows)
 
-    @pl.loop(0, count // STEP)
+    @pl.loop(0, count // STEP, unroll=count // STEP)
     def _(step):
         at, below = chunk(step)
         gate = [inner[a, at, :].astype(jnp.float32) for a in range(BLOCKS)]
@@ -256,7 +263,7 @@
             put(two_hi, two_lo, (residue, slice(place * count, (place + 1) * count)), product)
         back[residue] = inverse(residue, slice(0, 4 * count))
 
-    @pl.loop(0, count // STEP)
+    @pl.loop(0, count // STEP, unroll=count // STEP)
     def _(step):
         def signal(place):
             at = pl.ds(pl.multiple_of(place * count + step * STEP, STEP), STEP)
@@ -287,8 +294,8 @@
         coded = (part * jnp.abs(part)).astype(jnp.bfloat16)
         for a in range(BLOCKS):
             results[a, 3 * count + place * half : 3 * count + (place + 1) * half] = coded
-    for place, block in zip(places(), sent):
-        block[...] = results[place]
+    for place, block in zip(places(LAST_PEERS), sent):
+        block[...] = results[place, : block.shape[0]]
 
 
 def device_call(kernel, out_shape, scratch, in_vmem, out_vmem, name, limit):
@@ -330,7 +337,7 @@
     width = 2 * LANES
     return device_call(
         main_kernel,
-        [jax.ShapeDtypeStruct((RETURNED * count, LANES), bf)] * BLOCKS,
+        [jax.ShapeDtypeStruct(((3 + direct(peer)) * count, LANES), bf) for peer in (0,) + LAST_PEERS],
         [pltpu.VMEM((BLOCKS, SENT * count, LANES), bf), pltpu.VMEM((BLOCKS, RETURNED * count, LANES), bf)]
         + [pltpu.VMEM((BLOCKS, 2 * count, width), bf)] * 2
         + [pltpu.VMEM((BLOCKS, 4 * count, width), bf)] * 2
@@ -350,14 +357,14 @@
     count = sent[0].shape[0] // SENT
     first = fetched((outer, grad), (outer_in, grad_in), sems)
     rest = []
-    for i, (place, block) in enumerate(zip(places(), sent)):
+    for i, (place, block) in enumerate(zip(places(FIRST_PEERS), sent)):
         for j, source in enumerate((value, inner)):
             copy = pltpu.make_async_copy(source.at[place], block.at[j * count : (j + 1) * count], sems.at[2 + 2 * i + j])
             copy.start()
             rest.append(copy)
     for copy in first:
         copy.wait()
-    for place, block in zip(places(), sent):
+    for place, block in zip(places(FIRST_PEERS), sent):
         both = grad_in[place].astype(jnp.float32) * outer_in[place].astype(jnp.float32)
         block[2 * count :] = fourth_power(both, PRODUCT_SCALE)
     for copy in rest:
@@ -379,40 +386,74 @@
     )(*(x.reshape(BLOCKS, count, lanes) for x in arrays))
 
 
-def exchanged(blocks):
-    swaps = [[(i, i ^ peer) for i in range(BLOCKS)] for peer in PEERS]
+def exchanged(blocks, peers):
+    swaps = [[(i, i ^ peer) for i in range(BLOCKS)] for peer in peers]
     return [blocks[0]] + [lax.ppermute(block, "seq", swap) for block, swap in zip(blocks[1:], swaps)]
 
 
+def gather_kernel(*refs):
+    received, out = refs[:-1], refs[-1]
+    count = out.shape[0] // len(received)
+    for i, block in enumerate(received):
+        out[i * count : (i + 1) * count] = block[3 * count :]
+
+
+def second_hop(blocks):
+    count = blocks[0].shape[0] // RETURNED
+    gathered = device_call(
+        gather_kernel,
+        [jax.ShapeDtypeStruct((len(blocks) * count, LANES), jnp.bfloat16)],
+        [],
+        (True,) * len(blocks),
+        (True,),
+        "gather_proj",
+        16,
+    )(*blocks)[0]
+    return lax.ppermute(gathered, "seq", [(i, i ^ NEAR) for i in range(BLOCKS)])
+
+
+def proj_parts(direct_blocks, relayed):
+    peers = [0] + [peer for peer in LAST_PEERS if direct(peer)]
+    count = relayed.shape[0] // len(peers)
+    for peer, block in zip(peers, direct_blocks):
+        yield peer, block[3 * count :].astype(jnp.float32)
+    for i, peer in enumerate(peers):
+        yield peer ^ NEAR, relayed[i * count : (i + 1) * count].astype(jnp.float32)
+
+
 def sum_kernel(*refs):
-    received, total = refs[:-1], refs[-1]
-    first = 3 * (received[0].shape[0] // RETURNED)
+    *blocks, relayed, total = refs
     part = jnp.zeros(total.shape, jnp.float32)
-    for block in received:
-        size = jnp.abs(block[first:].astype(jnp.float32))
-        part = part + jnp.sum(size.reshape((-1,) + total.shape), 0)
+    for _, coded in proj_parts(blocks, relayed):
+        part = part + jnp.sum(jnp.abs(coded).reshape((-1,) + total.shape), 0)
     total[...] = jnp.broadcast_to(jnp.sum(part, keepdims=True), total.shape)
 
 
-def square_total(received):
+def square_total(blocks, relayed):
     return device_call(
-        sum_kernel, [jax.ShapeDtypeStruct((8, LANES), jnp.float32)], [], (True,) * BLOCKS, (True,), "square_total", 16
-    )(*received)[0]
+        sum_kernel,
+        [jax.ShapeDtypeStruct((8, LANES), jnp.float32)],
+        [],
+        (True,) * (len(blocks) + 1),
+        (True,),
+        "square_total",
+        16,
+    )(*blocks, relayed)[0]
 
 
 def unpack_kernel(*refs):
     received, (grad, *outs), (grad_in, outer_out, sems) = refs[:BLOCKS], refs[BLOCKS : BLOCKS + 4], refs[BLOCKS + 4 :]
-    count = received[0].shape[0] // RETURNED
+    count = grad.shape[1]
     fetch = pltpu.make_async_copy(grad, grad_in, sems.at[2 * BLOCKS])
     fetch.start()
     copies = []
-    for i, (place, block) in enumerate(zip(places(), received)):
+    for i, (place, block) in enumerate(zip(places(LAST_PEERS), received)):
         for j, out in enumerate(outs[:2]):
             copy = pltpu.make_async_copy(block.at[j * count : (j + 1) * count], out.at[place], sems.at[2 * i + j])
             copy.start()
             copies.append(copy)
     fetch.wait()
-    for place, block in zip(places(), received):
+    for place, block in zip(places(LAST_PEERS), received):
         act = fourth_root(block[2 * count : 3 * count], OUTER_SCALE)
         outer_out[place] = (grad_in[place].astype(jnp.float32) * act).astype(jnp.bfloat16)
     last = pltpu.make_async_copy(outer_out, outs[2], sems.at[2 * BLOCKS + 1])
@@ -438,37 +479,36 @@
     return [x.reshape(channels, lanes) for x in grads]
 
 
-def scale_kernel(entries, *refs):
-    received, sums, (out, held, sem) = refs[:BLOCKS], refs[BLOCKS:-3], refs[-3:]
-    count = received[0].shape[0] // RETURNED
+def scale_kernel(entries, blocks, *refs):
+    received, relayed, sums, (out, held, sem) = refs[:blocks], refs[blocks], refs[blocks + 1 : -3], refs[-3:]
     total = sums[0][...]
     for part in sums[1:]:
         total = total + part[...]
     scale = lax.rsqrt(total * (1.0 / entries) + 1e-06)[:1]
     features = held.shape[1]
-    for place, block in zip(places(), received):
-        lanes = pl.ds(pl.multiple_of(place * LANES, LANES), LANES)
+    own = lax.axis_index("seq")
+    for peer, coded in proj_parts(received, relayed):
+        lanes = pl.ds(pl.multiple_of((own ^ peer) * LANES, LANES), LANES)
+        size = jnp.sqrt(jnp.abs(coded)) * scale
+        both = jnp.where(coded < 0, -size, size)
         for i in range(2):
-            first = 3 * count + i * features
-            coded = block[first : first + features].astype(jnp.float32)
-            size = jnp.sqrt(jnp.abs(coded)) * scale
-            held[i, :, lanes] = jnp.where(coded < 0, -size, size)
+            held[i, :, lanes] = both[i * features : (i + 1) * features]
     copy = pltpu.make_async_copy(held, out, sem)
     copy.start()
     copy.wait()
 
 
-def scaled(received, sums, entries, features):
+def scaled(blocks, relayed, sums, entries, features):
     shape = (2, features, BLOCKS * LANES)
     return device_call(
-        functools.partial(scale_kernel, entries),
+        functools.partial(scale_kernel, entries, len(blocks)),
         [jax.ShapeDtypeStruct(shape, jnp.float32)],
         [pltpu.VMEM(shape, jnp.float32), pltpu.SemaphoreType.DMA],
-        (True,) * (BLOCKS + len(sums)),
+        (True,) * (len(blocks) + 1 + len(sums)),
         (False,),
         "scaled",
         16,
-    )(*received, *sums)[0]
+    )(*blocks, relayed, *sums)[0]
 
 
 highest = lax.Precision.HIGHEST
@@ -623,19 +663,26 @@
         rows = lax.dynamic_slice_in_dim(x, seq_pos * count, count, 1)
         return rows.reshape((2 * count,) + x.shape[2:])
 
-    received = exchanged(packed(value_in, gate_inner, gate_outer, out_grad))
+    received = exchanged(packed(value_in, gate_inner, gate_outer, out_grad), FIRST_PEERS)
     rates = own_rows(decay)
     features = jnp.sin(frequency[None, :] * (lax.iota(jnp.float32, length)[:, None] + 1.0))
     terms = jnp.concatenate(split_features(features), 1)
     spectra = filter_spectra(own_rows(filter_proj), rates, terms, angle)
-    back = exchanged(operator_grads(received, rates, spectra, angle, terms))
-    own_sum = square_total(back)
+    back = exchanged(operator_grads(received, rates, spectra, angle, terms), LAST_PEERS)
+    at = {peer: i + 1 for i, peer in enumerate(LAST_PEERS)}
+    near = [0] + [at[peer] for peer in LAST_PEERS if direct(peer)]
+    held = near + [at[peer] for peer in HELD_FOR]
+    for i, block in zip(held, lax.optimization_barrier([back[i] for i in held])):
+        back[i] = block
+    blocks = [back[i] for i in near]
+    relayed = second_hop(blocks)
+    own_sum = square_total(blocks, relayed)
     groups = lax.axis_size("ch")
     sums = [own_sum] + [
         lax.ppermute(own_sum, "ch", [(i, i ^ hop) for i in range(groups)]) for hop in range(1, groups)
     ]
     grads = unpacked(back, out_grad)
-    proj_grad = scaled(back, sums, filter_proj.size * groups, features.shape[1])
+    proj_grad = scaled(blocks, relayed, sums, filter_proj.size * groups, features.shape[1])
     return (*grads, proj_grad.transpose(0, 2, 1))
 
 

time: 65.5 us -> 62 us (0.947)
  waiting for transfers between devices: 16.6 us -> 14.8 us
  Pallas kernels: 18.1 us -> 17.3 us
  starting transfers between devices: 25.8 us -> 25 us
    ppermute x14, starting transfers between devices: 23.9 us -> 22.3 us  [exchanged(): lax.ppermute(block, 'seq', swap)]
    ppermute x14, waiting for transfers between devices: 16.1 us -> 14.8 us  [exchanged(): lax.ppermute(block, 'seq', swap)]
    ppermute x0 -> x1, starting transfers between devices: none -> 1.06 us  [second_hop(): return lax.ppermute(gathered, 'seq', [(i, i ^ NEAR) for i in range(BLOCKS)])]
    pallas_call x2 -> x3, Pallas kernels: 10.8 us -> 10 us  [the longest x1 9 us: operator_grads(): device_call(main_kernel, [jax.ShapeDtypeStruct(((3 + direct(peer)) * coun...]
  transfers between devices with their start and end apart: 17 -> 18, of which waited for: 7 -> 6; matrix products, arithmetic and copies ran while one was open for 6% -> 6% of each run, Pallas kernels for 7% -> 8%
where the time goes in v3:
time: 62 us; the launch traced here: 61.8 us
  starting transfers between devices  25 us (40%)
  Pallas kernels  17.3 us (28%)
  waiting for transfers between devices  14.8 us (24%)
  other arithmetic  3.01 us (5%)
  local copies, waits for them, and re-layouts  0.97 us (2%)
  between operations  0.82 us (1%)
    ppermute x14, starting transfers between devices, exchanged(): lax.ppermute(block, 'seq', swap)  22.3 us
    ppermute x14, waiting for transfers between devices, exchanged(): lax.ppermute(block, 'seq', swap)  14.8 us
    pallas_call x1, Pallas kernels, operator_grads(): device_call(main_kernel, [jax.ShapeDtypeStruct(((3 + direct(peer)) * coun...  9 us
    pallas_call x1, Pallas kernels, filter_spectra(): device_call(filter_kernel, [jax.ShapeDtypeStruct((BLOCKS, rows, width), f...  3.48 us
    convert_element_type x1, other arithmetic, split_features(): return (high.astype(jnp.bfloat16), (features - high).astype(jnp.bfloat16))  2.76 us
    pallas_call x1, Pallas kernels, packed(): device_call(pack_kernel, [jax.ShapeDtypeStruct((SENT * count, lanes), jnp...  2.27 us
    ppermute x3, starting transfers between devices, body(): lax.ppermute(own_sum, 'ch', [(i, i ^ hop) for i in range(groups)])  1.63 us
    pallas_call x1, Pallas kernels, unpacked(): device_call(unpack_kernel, [block] * 3, [held, held, pltpu.SemaphoreType....  1.3 us
  transfers between devices with their start and end apart: 18, of which 6 were waited for; matrix products, arithmetic and copies ran while one was open for 6% of the time, Pallas kernels for 8%

profile of v3, /device:TPU:0, one launch (start us, length us, event | category | flops | bytes accessed | tf_op | source)
XLA Modules:
  0.0 61.8 jit_solution(5006606686307721191)
XLA Ops:
  0.7 2.3 %packed.1 = (bf16[384,128]{1,0:T(8,128)(2,1)}, bf16[384,128]{1,0:T(8,128)(2,1)}, bf16[384,128]{1,0:T(8,128)(2,1)}, bf16[384,128]{1,0:T(8,128)(2,1)}, bf16[384,12...) custom-call(bf16[8,128,128]{2,1,0:T(8,128)(2,1)} %bitcast.14, ...), custom_call_target="tpu_custom_call" | custom-call | tf_op jit(solution)/shard_map/packed/pallas_call | solution.py:378
  2.9 3.0 %collective-permute-start = (bf16[384,128]{1,0:T(8,128)(2,1)}, bf16[384,128]{1,0:T(8,128)(2,1)S(1)}, u32[]{:S(2)}, u32[]{:S(2)}) collective-permute-start(bf16[384,128]{1,0:T(8,128)(2,1)} %get-tuple-element.29), channel_id=1, source_target_pairs={{0,4},{4,0},{8,12},{12,8},{16,20},{20,16},{24,28},{28,24},{1,5},{5... | collective-permute-start | bytes 294920 | tf_op jit(solution)/shard_map/ppermute | solution.py:391
  6.0 2.6 %collective-permute-start.1 = (bf16[384,128]{1,0:T(8,128)(2,1)}, bf16[384,128]{1,0:T(8,128)(2,1)S(1)}, u32[]{:S(2)}, u32[]{:S(2)}) collective-permute-start(bf16[384,128]{1,0:T(8,128)(2,1)} %get-tuple-element.30), channel_id=1, source_target_pairs={{0,16},{4,20},{8,24},{12,28},{16,0},{20,4},{24,8},{28,12},{1,17},{... | collective-permute-start | bytes 294920 | tf_op jit(solution)/shard_map/ppermute | solution.py:391
  8.6 1.6 %collective-permute-start.2 = (bf16[384,128]{1,0:T(8,128)(2,1)}, bf16[384,128]{1,0:T(8,128)(2,1)S(1)}, u32[]{:S(2)}, u32[]{:S(2)}) collective-permute-start(bf16[384,128]{1,0:T(8,128)(2,1)} %get-tuple-element.31), channel_id=1, source_target_pairs={{0,8},{4,12},{8,0},{12,4},{16,24},{20,28},{24,16},{28,20},{1,9},{5... | collective-permute-start | bytes 294920 | tf_op jit(solution)/shard_map/ppermute | solution.py:391
  10.4 0.6 %collective-permute-start.4 = (bf16[384,128]{1,0:T(8,128)(2,1)}, bf16[384,128]{1,0:T(8,128)(2,1)S(1)}, u32[]{:S(2)}, u32[]{:S(2)}) collective-permute-start(bf16[384,128]{1,0:T(8,128)(2,1)} %get-tuple-element.33), channel_id=1, source_target_pairs={{0,12},{4,8},{8,4},{12,0},{16,28},{20,24},{24,20},{28,16},{1,13},{... | collective-permute-start | bytes 294920 | tf_op jit(solution)/shard_map/ppermute | solution.py:391
  11.0 0.7 %constant_dynamic-slice_fusion.1 = f32[2,128]{1,0:T(2,128)S(1)} fusion(f32[2,1024]{1,0:T(2,128)} %param.13, s32[]{:T(128)S(6)} %select_n.4), kind=kLoop, calls=%fused_computation.8 | loop fusion | bytes 2052 | tf_op jit(solution)/shard_map/dynamic_slice | solution.py:663
  12.0 2.8 %reduce-precision_convert_fusion = (bf16[1024,64]{1,0:T(8,128)(2,1)S(1)}, bf16[1024,64]{1,0:T(8,128)(2,1)S(1)}) fusion(f32[64]{0:T(128)} %param.14, f32[1024]{0:T(1024)S(1)} %iota_add_fusion), kind=kLoop, calls=%fused_computation.1 | loop fusion | flops 327680 | bytes 266496 | tf_op jit(solution)/shard_map/convert_element_type | solution.py:94
  14.9 4.5 %collective-permute-start.5 = (bf16[384,128]{1,0:T(8,128)(2,1)}, bf16[384,128]{1,0:T(8,128)(2,1)S(1)}, u32[]{:S(2)}, u32[]{:S(2)}) collective-permute-start(bf16[384,128]{1,0:T(8,128)(2,1)} %get-tuple-element.34), channel_id=1, source_target_pairs={{0,20},{4,16},{8,28},{12,24},{16,4},{20,0},{24,12},{28,8},{1,21},{... | collective-permute-start | bytes 294920 | tf_op jit(solution)/shard_map/ppermute | solution.py:391
  19.5 3.5 %filter_spectra.1.refs_9_ = f32[8,256,256]{2,1,0:T(8,128)S(1)} custom-call(bf16[256,128]{1,0:T(8,128)(2,1)S(1)} %pad_maximum_fusion.1.proj, f32[256,1]{1,0:T(8,128)S(1)} %copy.19.rate.refs_8_, bf16[1024,128]{1,0:T(8,128)(2,1)S(1)} %pad_maximum_fusion.features.refs_11_, f32[3,128,128]{2,1,0:T(8,128)S(1)} %copy-done.2), custom_call_target="tpu_custom_call" | custom-call | tf_op jit(solution)/shard_map/filter_spectra/pallas_call | solution.py:321
  23.0 2.1 %collective-permute-done.5.refs_6_ = bf16[384,128]{1,0:T(8,128)(2,1)S(1)} collective-permute-done((bf16[384,128]{1,0:T(8,128)(2,1)}, bf16[384,128]{1,0:T(8,128)(2,1)S(1)}, u32[]{:S(2)}, u32[]{:S(2)}) %collective-permute-start.5) | collective-permute-done | bytes 98336 | tf_op jit(solution)/shard_map/ppermute | solution.py:391
  25.2 1.9 %collective-permute-done.6.refs_7_ = bf16[384,128]{1,0:T(8,128)(2,1)S(1)} collective-permute-done((bf16[384,128]{1,0:T(8,128)(2,1)}, bf16[384,128]{1,0:T(8,128)(2,1)S(1)}, u32[]{:S(2)}, u32[]{:S(2)}) %collective-permute-start.6) | collective-permute-done | bytes 98336 | tf_op jit(solution)/shard_map/ppermute | solution.py:391
  27.0 9.0 %operator_grads.1 = (bf16[512,128]{1,0:T(8,128)(2,1)S(1)}, bf16[384,128]{1,0:T(8,128)(2,1)S(1)}, bf16[512,128]{1,0:T(8,128)(2,1)S(1)}, bf16[512,128]{1,0:T(8,128...) custom-call(bf16[384,128]{1,0:T(8,128)(2,1)S(1)} %copy-done.3, ...), custom_call_target="tpu_custom_call" | custom-call | tf_op jit(solution)/shard_map/operator_grads/pallas_call | solution.py:338
  36.1 1.8 %collective-permute-start.7 = (bf16[512,128]{1,0:T(8,128)(2,1)S(1)}, bf16[512,128]{1,0:T(8,128)(2,1)S(1)}, u32[]{:S(2)}, u32[]{:S(2)}) collective-permute-start(bf16[512,128]{1,0:T(8,128)(2,1)S(1)} %get-tuple-element.37), channel_id=1, source_target_pairs={{0,16},{4,20},{8,24},{12,28},{16,0},{20,4},{24,8},{28,12},{1,17},{... | collective-permute-start | bytes 393224 | tf_op jit(solution)/shard_map/ppermute | solution.py:391
  37.9 1.4 %collective-permute-start.8 = (bf16[512,128]{1,0:T(8,128)(2,1)S(1)}, bf16[512,128]{1,0:T(8,128)(2,1)S(1)}, u32[]{:S(2)}, u32[]{:S(2)}) collective-permute-start(bf16[512,128]{1,0:T(8,128)(2,1)S(1)} %get-tuple-element.38), channel_id=1, source_target_pairs={{0,24},{4,28},{8,16},{12,20},{16,8},{20,12},{24,0},{28,4},{1,25},{... | collective-permute-start | bytes 393224 | tf_op jit(solution)/shard_map/ppermute | solution.py:391
  40.1 4.1 %collective-permute-done.10.refs_1_ = bf16[384,128]{1,0:T(8,128)(2,1)S(1)} collective-permute-done((bf16[384,128]{1,0:T(8,128)(2,1)S(1)}, bf16[384,128]{1,0:T(8,128)(2,1)S(1)}, u32[]{:S(2)}, u32[]{:S(2)}) %collective-permute-start.10) | collective-permute-done | bytes 98336 | tf_op jit(solution)/shard_map/ppermute | solution.py:391
  44.2 3.0 %collective-permute-done.7.refs_2_.refs_1_ = bf16[512,128]{1,0:T(8,128)(2,1)S(1)} collective-permute-done((bf16[512,128]{1,0:T(8,128)(2,1)S(1)}, bf16[512,128]{1,0:T(8,128)(2,1)S(1)}, u32[]{:S(2)}, u32[]{:S(2)}) %collective-permute-start.7) | collective-permute-done | bytes 131104 | tf_op jit(solution)/shard_map/ppermute | solution.py:391
  47.2 1.1 %collective-permute-start.14 = (bf16[512,128]{1,0:T(8,128)(2,1)S(1)}, bf16[512,128]{1,0:T(8,128)(2,1)S(1)}, u32[]{:S(2)}, u32[]{:S(2)}) collective-permute-start(bf16[512,128]{1,0:T(8,128)(2,1)S(1)} %gather_proj.1), channel_id=1, source_target_pairs={{0,4},{4,0},{8,12},{12,8},{16,20},{20,16},{24,28},{28,24},{1,5},{5... | collective-permute-start | bytes 393224 | tf_op jit(solution)/shard_map/ppermute | solution.py:412
  48.3 2.2 %collective-permute-start.11 = (bf16[384,128]{1,0:T(8,128)(2,1)S(1)}, bf16[384,128]{1,0:T(8,128)(2,1)S(1)}, u32[]{:S(2)}, u32[]{:S(2)}) collective-permute-start(bf16[384,128]{1,0:T(8,128)(2,1)S(1)} %get-tuple-element.46), channel_id=1, source_target_pairs={{0,20},{4,16},{8,28},{12,24},{16,4},{20,0},{24,12},{28,8},{1,21},{... | collective-permute-start | bytes 294920 | tf_op jit(solution)/shard_map/ppermute | solution.py:391
  50.5 3.5 %collective-permute-start.12 = (bf16[384,128]{1,0:T(8,128)(2,1)S(1)}, bf16[384,128]{1,0:T(8,128)(2,1)S(1)}, u32[]{:S(2)}, u32[]{:S(2)}) collective-permute-start(bf16[384,128]{1,0:T(8,128)(2,1)S(1)} %get-tuple-element.47), channel_id=1, source_target_pairs={{0,28},{4,24},{8,20},{12,16},{16,12},{20,8},{24,4},{28,0},{1,29},{... | collective-permute-start | bytes 294920 | tf_op jit(solution)/shard_map/ppermute | solution.py:391
  54.2 1.6 %collective-permute-start.16 = (f32[8,128]{1,0:T(8,128)S(1)}, f32[8,128]{1,0:T(8,128)S(1)}, u32[]{:S(2)}, u32[]{:S(2)}) collective-permute-start(f32[8,128]{1,0:T(8,128)S(1)} %square_total.1.refs_5_), channel_id=1, source_target_pairs={{0,2},{1,3},{2,0},{3,1},{4,6},{5,7},{6,4},{7,5},{8,10},{9,11},{10,... | collective-permute-start | bytes 12296 | tf_op jit(solution)/shard_map/ppermute | solution.py:682
  55.7 2.3 %collective-permute-done.11.refs_5_ = bf16[384,128]{1,0:T(8,128)(2,1)S(1)} collective-permute-done((bf16[384,128]{1,0:T(8,128)(2,1)S(1)}, bf16[384,128]{1,0:T(8,128)(2,1)S(1)}, u32[]{:S(2)}, u32[]{:S(2)}) %collective-permute-start.11) | collective-permute-done | bytes 98336 | tf_op jit(solution)/shard_map/ppermute | solution.py:391
  58.1 1.4 %collective-permute-done.13.refs_7_ = bf16[384,128]{1,0:T(8,128)(2,1)S(1)} collective-permute-done((bf16[384,128]{1,0:T(8,128)(2,1)S(1)}, bf16[384,128]{1,0:T(8,128)(2,1)S(1)}, u32[]{:S(2)}, u32[]{:S(2)}) %collective-permute-start.13) | collective-permute-done | bytes 98336 | tf_op jit(solution)/shard_map/ppermute | solution.py:391
  59.4 1.3 %unpacked.1 = (bf16[8,128,128]{2,1,0:T(8,128)(2,1)}, bf16[8,128,128]{2,1,0:T(8,128)(2,1)}, bf16[8,128,128]{2,1,0:T(8,128)(2,1)}) custom-call(bf16[512,128]{1,0:T(8,128)(2,1)S(1)} %get-tuple-element.41.refs_0_, bf16[384,128]{1,0:T(8,128)(2,1)S(1)} %collective-permute-done.10.refs_1_, bf16[512,128]{1,0:T(8,128)(2,1)S(1)} %collective-permute-done.7.refs_2_.refs_1_, ...), custom_call_target="tpu_custom_call" | custom-call | tf_op jit(solution)/shard_map/unpacked/pallas_call | solution.py:470
  60.8 1.0 %scaled.1 = f32[2,64,1024]{2,1,0:T(8,128)} custom-call(bf16[512,128]{1,0:T(8,128)(2,1)S(1)} %get-tuple-element.41.refs_0_, bf16[512,128]{1,0:T(8,128)(2,1)S(1)} %collective-permute-done.7.refs_2_.refs_1_, bf16[512,128]{1,0:T(8,128)(2,1)S(1)} %collective-permute-done.8.refs_3_.refs_2_, bf16[512,128]{1,0:T(8,128)(2,1)S(1)} %collective-permute-done.9.refs_4_.refs_3_, ...), custom_call_target="tpu_custom_call" | custom-call | tf_op jit(solution)/shard_map/scaled/pallas_call | solution.py:503
  (35 shorter events, 1.9 us)
Async XLA Ops:
  0.6 11.0 %copy-start = (bf16[2,1024,64]{1,2,0:T(8,128)(2,1)S(1)}, bf16[2,1024,64]{1,2,0:T(8,128)(2,1)}, u32[]{:S(2)}) copy-start(bf16[2,1024,64]{1,2,0:T(8,128)(2,1)} %param.12) | copy-start | bytes 786436
  0.6 18.9 %copy-start.2 = (f32[3,128,128]{2,1,0:T(8,128)S(1)}, f32[3,128,128]{2,1,0:T(8,128)}, u32[]{:S(2)}) copy-start(f32[3,128,128]{2,1,0:T(8,128)} %constant.16.clone.angle.refs_10_) | copy-start | bytes 589828
  2.9 12.0 %collective-permute-start = (bf16[384,128]{1,0:T(8,128)(2,1)}, bf16[384,128]{1,0:T(8,128)(2,1)S(1)}, u32[]{:S(2)}, u32[]{:S(2)}) collective-permute-start(bf16[384,128]{1,0:T(8,128)(2,1)} %get-tuple-element.29), channel_id=1, source_target_pairs={{0,4},{4,0},{8,12},{12,8},{16,20},{20,16},{24,28},{28,24},{1,5},{5... | collective-permute-start | bytes 294920 | tf_op jit(solution)/shard_map/ppermute | solution.py:391
  6.0 13.4 %collective-permute-start.1 = (bf16[384,128]{1,0:T(8,128)(2,1)}, bf16[384,128]{1,0:T(8,128)(2,1)S(1)}, u32[]{:S(2)}, u32[]{:S(2)}) collective-permute-start(bf16[384,128]{1,0:T(8,128)(2,1)} %get-tuple-element.30), channel_id=1, source_target_pairs={{0,16},{4,20},{8,24},{12,28},{16,0},{20,4},{24,8},{28,12},{1,17},{... | collective-permute-start | bytes 294920 | tf_op jit(solution)/shard_map/ppermute | solution.py:391
  8.6 14.5 %collective-permute-start.2 = (bf16[384,128]{1,0:T(8,128)(2,1)}, bf16[384,128]{1,0:T(8,128)(2,1)S(1)}, u32[]{:S(2)}, u32[]{:S(2)}) collective-permute-start(bf16[384,128]{1,0:T(8,128)(2,1)} %get-tuple-element.31), channel_id=1, source_target_pairs={{0,8},{4,12},{8,0},{12,4},{16,24},{20,28},{24,16},{28,20},{1,9},{5... | collective-permute-start | bytes 294920 | tf_op jit(solution)/shard_map/ppermute | solution.py:391
  10.1 12.9 %collective-permute-start.3 = (bf16[384,128]{1,0:T(8,128)(2,1)}, bf16[384,128]{1,0:T(8,128)(2,1)S(1)}, u32[]{:S(2)}, u32[]{:S(2)}) collective-permute-start(bf16[384,128]{1,0:T(8,128)(2,1)} %get-tuple-element.32), channel_id=1, source_target_pairs={{0,24},{4,28},{8,16},{12,20},{16,8},{20,12},{24,0},{28,4},{1,25},{... | collective-permute-start | bytes 294920 | tf_op jit(solution)/shard_map/ppermute | solution.py:391
  10.4 12.7 %collective-permute-start.4 = (bf16[384,128]{1,0:T(8,128)(2,1)}, bf16[384,128]{1,0:T(8,128)(2,1)S(1)}, u32[]{:S(2)}, u32[]{:S(2)}) collective-permute-start(bf16[384,128]{1,0:T(8,128)(2,1)} %get-tuple-element.33), channel_id=1, source_target_pairs={{0,12},{4,8},{8,4},{12,0},{16,28},{20,24},{24,20},{28,16},{1,13},{... | collective-permute-start | bytes 294920 | tf_op jit(solution)/shard_map/ppermute | solution.py:391
  12.0 15.1 %copy-start.3 = (bf16[384,128]{1,0:T(8,128)(2,1)S(1)}, bf16[384,128]{1,0:T(8,128)(2,1)}, u32[]{:S(2)}) copy-start(bf16[384,128]{1,0:T(8,128)(2,1)} %get-tuple-element.28.refs_0_) | copy-start | bytes 294916
  14.9 10.3 %collective-permute-start.5 = (bf16[384,128]{1,0:T(8,128)(2,1)}, bf16[384,128]{1,0:T(8,128)(2,1)S(1)}, u32[]{:S(2)}, u32[]{:S(2)}) collective-permute-start(bf16[384,128]{1,0:T(8,128)(2,1)} %get-tuple-element.34), channel_id=1, source_target_pairs={{0,20},{4,16},{8,28},{12,24},{16,4},{20,0},{24,12},{28,8},{1,21},{... | collective-permute-start | bytes 294920 | tf_op jit(solution)/shard_map/ppermute | solution.py:391
  19.4 7.6 %collective-permute-start.6 = (bf16[384,128]{1,0:T(8,128)(2,1)}, bf16[384,128]{1,0:T(8,128)(2,1)S(1)}, u32[]{:S(2)}, u32[]{:S(2)}) collective-permute-start(bf16[384,128]{1,0:T(8,128)(2,1)} %get-tuple-element.35), channel_id=1, source_target_pairs={{0,28},{4,24},{8,20},{12,16},{16,12},{20,8},{24,4},{28,0},{1,29},{... | collective-permute-start | bytes 294920 | tf_op jit(solution)/shard_map/ppermute | solution.py:391
  27.0 32.4 %copy-start.1 = (bf16[1024,128]{1,0:T(8,128)(2,1)S(1)}, bf16[1024,128]{1,0:T(8,128)(2,1)}, u32[]{:S(2)}) copy-start(bf16[1024,128]{1,0:T(8,128)(2,1)} %param.11) | copy-start | bytes 786436
  36.1 11.1 %collective-permute-start.7 = (bf16[512,128]{1,0:T(8,128)(2,1)S(1)}, bf16[512,128]{1,0:T(8,128)(2,1)S(1)}, u32[]{:S(2)}, u32[]{:S(2)}) collective-permute-start(bf16[512,128]{1,0:T(8,128)(2,1)S(1)} %get-tuple-element.37), channel_id=1, source_target_pairs={{0,16},{4,20},{8,24},{12,28},{16,0},{20,4},{24,8},{28,12},{1,17},{... | collective-permute-start | bytes 393224 | tf_op jit(solution)/shard_map/ppermute | solution.py:391
  37.9 9.3 %collective-permute-start.8 = (bf16[512,128]{1,0:T(8,128)(2,1)S(1)}, bf16[512,128]{1,0:T(8,128)(2,1)S(1)}, u32[]{:S(2)}, u32[]{:S(2)}) collective-permute-start(bf16[512,128]{1,0:T(8,128)(2,1)S(1)} %get-tuple-element.38), channel_id=1, source_target_pairs={{0,24},{4,28},{8,16},{12,20},{16,8},{20,12},{24,0},{28,4},{1,25},{... | collective-permute-start | bytes 393224 | tf_op jit(solution)/shard_map/ppermute | solution.py:391
  39.3 7.9 %collective-permute-start.9 = (bf16[512,128]{1,0:T(8,128)(2,1)S(1)}, bf16[512,128]{1,0:T(8,128)(2,1)S(1)}, u32[]{:S(2)}, u32[]{:S(2)}) collective-permute-start(bf16[512,128]{1,0:T(8,128)(2,1)S(1)} %get-tuple-element.39), channel_id=1, source_target_pairs={{0,8},{4,12},{8,0},{12,4},{16,24},{20,28},{24,16},{28,20},{1,9},{5... | collective-permute-start | bytes 393224 | tf_op jit(solution)/shard_map/ppermute | solution.py:391
  39.6 4.6 %collective-permute-start.10 = (bf16[384,128]{1,0:T(8,128)(2,1)S(1)}, bf16[384,128]{1,0:T(8,128)(2,1)S(1)}, u32[]{:S(2)}, u32[]{:S(2)}) collective-permute-start(bf16[384,128]{1,0:T(8,128)(2,1)S(1)} %get-tuple-element.40), channel_id=1, source_target_pairs={{0,4},{4,0},{8,12},{12,8},{16,20},{20,16},{24,28},{28,24},{1,5},{5... | collective-permute-start | bytes 294920 | tf_op jit(solution)/shard_map/ppermute | solution.py:391
  47.2 6.7 %collective-permute-start.14 = (bf16[512,128]{1,0:T(8,128)(2,1)S(1)}, bf16[512,128]{1,0:T(8,128)(2,1)S(1)}, u32[]{:S(2)}, u32[]{:S(2)}) collective-permute-start(bf16[512,128]{1,0:T(8,128)(2,1)S(1)} %gather_proj.1), channel_id=1, source_target_pairs={{0,4},{4,0},{8,12},{12,8},{16,20},{20,16},{24,28},{28,24},{1,5},{5... | collective-permute-start | bytes 393224 | tf_op jit(solution)/shard_map/ppermute | solution.py:412
  48.3 9.8 %collective-permute-start.11 = (bf16[384,128]{1,0:T(8,128)(2,1)S(1)}, bf16[384,128]{1,0:T(8,128)(2,1)S(1)}, u32[]{:S(2)}, u32[]{:S(2)}) collective-permute-start(bf16[384,128]{1,0:T(8,128)(2,1)S(1)} %get-tuple-element.46), channel_id=1, source_target_pairs={{0,20},{4,16},{8,28},{12,24},{16,4},{20,0},{24,12},{28,8},{1,21},{... | collective-permute-start | bytes 294920 | tf_op jit(solution)/shard_map/ppermute | solution.py:391
  50.5 7.6 %collective-permute-start.12 = (bf16[384,128]{1,0:T(8,128)(2,1)S(1)}, bf16[384,128]{1,0:T(8,128)(2,1)S(1)}, u32[]{:S(2)}, u32[]{:S(2)}) collective-permute-start(bf16[384,128]{1,0:T(8,128)(2,1)S(1)} %get-tuple-element.47), channel_id=1, source_target_pairs={{0,28},{4,24},{8,20},{12,16},{16,12},{20,8},{24,4},{28,0},{1,29},{... | collective-permute-start | bytes 294920 | tf_op jit(solution)/shard_map/ppermute | solution.py:391
  53.9 5.5 %collective-permute-start.13 = (bf16[384,128]{1,0:T(8,128)(2,1)S(1)}, bf16[384,128]{1,0:T(8,128)(2,1)S(1)}, u32[]{:S(2)}, u32[]{:S(2)}) collective-permute-start(bf16[384,128]{1,0:T(8,128)(2,1)S(1)} %get-tuple-element.48), channel_id=1, source_target_pairs={{0,12},{4,8},{8,4},{12,0},{16,28},{20,24},{24,20},{28,16},{1,13},{... | collective-permute-start | bytes 294920 | tf_op jit(solution)/shard_map/ppermute | solution.py:391
  54.1 6.6 %collective-permute-start.17 = (f32[8,128]{1,0:T(8,128)S(1)}, f32[8,128]{1,0:T(8,128)S(1)}, u32[]{:S(2)}, u32[]{:S(2)}) collective-permute-start(f32[8,128]{1,0:T(8,128)S(1)} %square_total.1.refs_5_), channel_id=1, source_target_pairs={{0,3},{1,2},{2,1},{3,0},{4,7},{5,6},{6,5},{7,4},{8,11},{9,10},{10,... | collective-permute-start | bytes 12296 | tf_op jit(solution)/shard_map/ppermute | solution.py:682
  54.2 6.6 %collective-permute-start.16 = (f32[8,128]{1,0:T(8,128)S(1)}, f32[8,128]{1,0:T(8,128)S(1)}, u32[]{:S(2)}, u32[]{:S(2)}) collective-permute-start(f32[8,128]{1,0:T(8,128)S(1)} %square_total.1.refs_5_), channel_id=1, source_target_pairs={{0,2},{1,3},{2,0},{3,1},{4,6},{5,7},{6,4},{7,5},{8,10},{9,11},{10,... | collective-permute-start | bytes 12296 | tf_op jit(solution)/shard_map/ppermute | solution.py:682
  58.1 2.7 %collective-permute-start.15 = (f32[8,128]{1,0:T(8,128)S(1)}, f32[8,128]{1,0:T(8,128)S(1)}, u32[]{:S(2)}, u32[]{:S(2)}) collective-permute-start(f32[8,128]{1,0:T(8,128)S(1)} %square_total.1.refs_5_), channel_id=1, source_target_pairs={{0,1},{1,0},{2,3},{3,2},{4,5},{5,4},{6,7},{7,6},{8,9},{9,8},{10,11... | collective-permute-start | bytes 12296 | tf_op jit(solution)/shard_map/ppermute | solution.py:682

commit v4 on v3

--- a/solution.py
+++ b/solution.py
@@ -13,6 +13,7 @@
 LANES = 128
 COS1, COS2, COS3 = (math.cos(math.pi / 8), math.cos(math.pi / 4), math.cos(3 * math.pi / 8))
 STEP = 16
+HALVES = 1
 SIN_AT, SIGN_AT = 16, 32
 FIRST_PEERS = (1, 4, 2, 6, 3, 5, 7)
 LAST_PEERS = (1, 4, 6, 2, 5, 7, 3)
@@ -196,104 +197,142 @@
     return [place] + [place ^ peer for peer in peers]
 
 
+def interleaved(*lists):
+    steps = [((i + 0.5) / len(steps), n, step) for n, steps in enumerate(lists) for i, step in enumerate(steps)]
+    for _, _, step in sorted(steps, key=lambda entry: entry[:2]):
+        step()
+
+
 def main_kernel(*refs):
     received, (rate, filt, angle, features), sent = refs[:BLOCKS], refs[BLOCKS : BLOCKS + 4], refs[BLOCKS + 4 : 2 * BLOCKS + 4]
     (
-        moved, results, one_hi, one_lo, two_hi, two_lo, spec, spec2, back, weighted_hi, weighted_lo, table_hi, table_lo,
+        moved, results, one_hi, one_lo, two_hi, two_lo, spec, back, weighted_hi, weighted_lo, total, table_hi, table_lo,
     ) = refs[2 * BLOCKS + 4 :]
     count = moved.shape[1] // SENT
+    part = count // HALVES
     value, inner, product = (moved.at[:, i * count : (i + 1) * count] for i in range(SENT))
     grad_value, grad_inner, outer_coded = (results.at[:, i * count : (i + 1) * count] for i in range(3))
     for place, block in zip(places(FIRST_PEERS), received):
         moved[place] = block[...]
-
-    def forward(residue):
-        return times(one_hi[residue], one_lo[residue], table_hi[residue], table_lo[residue])
-
-    def inverse(residue, rows):
-        return times_transposed(
-            two_hi[residue, rows, :], two_lo[residue, rows, :], table_hi[residue], table_lo[residue])
-
-    def chunk(step):
-        return pl.ds(pl.multiple_of(step * STEP, STEP), STEP), pl.ds(pl.multiple_of(count + step * STEP, STEP), STEP)
-
-    def pair(ref, residue, rows):
-        return ref[residue, rows, :LANES], ref[residue, rows, LANES:]
-
-    upper, lower = slice(0, count), slice(count, 2 * count)
-
-    @pl.loop(0, count // STEP, unroll=count // STEP)
-    def _(step):
-        at, below = chunk(step)
-        store_folded(one_hi, one_lo, at, [value[a, at, :].astype(jnp.float32) for a in range(BLOCKS)])
-        store_folded(one_hi, one_lo, below, [fourth_root(product[a, at, :], PRODUCT_SCALE) for a in range(BLOCKS)])
-
-    for residue in range(BLOCKS):
-        make_table(angle, residue, table_hi, table_lo)
-        spec[residue] = forward(residue)
-        put(two_hi, two_lo, (residue, upper), multiplied(
-            pair(filt, residue, upper), pair(spec, residue, upper), False, residue))
-        put(two_hi, two_lo, (residue, lower), multiplied(
-            pair(filt, residue, lower), pair(spec, residue, lower), True, residue))
-        rows = slice(0, 2 * count)
-        back[residue, rows, :] = inverse(residue, rows)
-
-    @pl.loop(0, count // STEP, unroll=count // STEP)
-    def _(step):
-        at, below = chunk(step)
+    dot = functools.partial(jnp.dot, preferred_element_type=jnp.float32)
+    upper, lower = slice(0, part), slice(part, 2 * part)
+
+    def forward(half, residue):
+        return times(one_hi[residue, half], one_lo[residue, half], table_hi[residue], table_lo[residue])
+
+    def inverse(half, residue, rows):
+        back[residue, half, rows] = times_transposed(
+            two_hi[residue, half, rows], two_lo[residue, half, rows], table_hi[residue], table_lo[residue])
+
+    def pair(ref, residue, half, rows):
+        return ref[residue, half, rows, :LANES], ref[residue, half, rows, LANES:]
+
+    def filter_pair(residue, half, place):
+        rows = slice(place * count + half * part, place * count + (half + 1) * part)
+        return filt[residue, rows, :LANES], filt[residue, rows, LANES:]
+
+    def rows_of(half, step):
+        first = half * part + step * STEP
+        return slice(first, first + STEP), slice(step * STEP, (step + 1) * STEP)
+
+    def signal(half, place, step):
+        first = place * part + step * STEP
+        return unfold([pair(back, residue, half, slice(first, first + STEP)) for residue in range(BLOCKS)])
+
+    def fold_inputs(half, step, place):
+        at, _ = rows_of(half, step)
+        first = place * part + step * STEP
+        if place == 0:
+            blocks = [value[a, at, :].astype(jnp.float32) for a in range(BLOCKS)]
+        else:
+            blocks = [fourth_root(product[a, at, :], PRODUCT_SCALE) for a in range(BLOCKS)]
+        store_folded(one_hi.at[:, half], one_lo.at[:, half], slice(first, first + STEP), blocks)
+
+    def first_class(half, residue):
+        if half == 0:
+            make_table(angle, residue, table_hi, table_lo)
+        spec[residue, half] = forward(half, residue)
+        for place, rows in ((0, upper), (1, lower)):
+            put(two_hi, two_lo, (residue, half, rows), multiplied(
+                filter_pair(residue, half, place), pair(spec, residue, half, rows), place == 1, residue))
+        inverse(half, residue, slice(0, 2 * part))
+
+    def between(half, step):
+        at, first = rows_of(half, step)
+        second = slice(part + first.start, part + first.stop)
         gate = [inner[a, at, :].astype(jnp.float32) for a in range(BLOCKS)]
-        inner_act = unfold([pair(back, residue, at) for residue in range(BLOCKS)])
-        store_folded(one_hi, one_lo, at, [gate[a] * inner_act[a] for a in range(BLOCKS)])
-        grad_mixed = unfold([pair(back, residue, below) for residue in range(BLOCKS)])
+        inner_act = signal(half, 0, step)
+        store_folded(one_hi.at[:, half], one_lo.at[:, half], first, [gate[a] * inner_act[a] for a in range(BLOCKS)])
+        grad_mixed = signal(half, 1, step)
         for a in range(BLOCKS):
             grad_inner[a, at, :] = (grad_mixed[a] * inner_act[a]).astype(jnp.bfloat16)
-        store_folded(one_hi, one_lo, below, [gate[a] * grad_mixed[a] for a in range(BLOCKS)])
-
-    for residue in range(BLOCKS):
-        spec2[...] = forward(residue)
-        mixed = spec2[upper, :LANES], spec2[upper, LANES:]
-        inner_grad = spec2[lower, :LANES], spec2[lower, LANES:]
+        store_folded(one_hi.at[:, half], one_lo.at[:, half], second, [gate[a] * grad_mixed[a] for a in range(BLOCKS)])
+
+    def second_class(half, residue):
+        both = forward(half, residue)
+        mixed = both[upper, :LANES], both[upper, LANES:]
+        inner_grad = both[lower, :LANES], both[lower, LANES:]
         products = (
-            multiplied(pair(filt, residue, lower), mixed, False, residue),
-            multiplied(pair(filt, residue, upper), inner_grad, True, residue),
-            multiplied(pair(spec, residue, upper), inner_grad, True, residue),
-            multiplied(mixed, pair(spec, residue, lower), True, residue),
+            multiplied(filter_pair(residue, half, 1), mixed, False, residue),
+            multiplied(filter_pair(residue, half, 0), inner_grad, True, residue),
+            multiplied(pair(spec, residue, half, upper), inner_grad, True, residue),
+            multiplied(mixed, pair(spec, residue, half, lower), True, residue),
         )
         for place, product in enumerate(products):
-            put(two_hi, two_lo, (residue, slice(place * count, (place + 1) * count)), product)
-        back[residue] = inverse(residue, slice(0, 4 * count))
-
-    @pl.loop(0, count // STEP, unroll=count // STEP)
-    def _(step):
-        def signal(place):
-            at = pl.ds(pl.multiple_of(place * count + step * STEP, STEP), STEP)
-            return unfold([pair(back, residue, at) for residue in range(BLOCKS)])
-
-        at, below = chunk(step)
-        outer_act = signal(0)
+            put(two_hi, two_lo, (residue, half, slice(place * part, (place + 1) * part)), product)
+        inverse(half, residue, slice(2 * part, 4 * part))
+
+    def third_class(half, residue):
+        inverse(half, residue, slice(0, 2 * part))
+
+    def outputs(half, step, place):
+        at, rows = rows_of(half, step)
+        blocks = signal(half, place, step)
+        if place == 0:
+            for a in range(BLOCKS):
+                outer_coded[a, at, :] = fourth_power(blocks[a], OUTER_SCALE)
+        elif place == 1:
+            for a in range(BLOCKS):
+                grad_value[a, at, :] = blocks[a].astype(jnp.bfloat16)
+        else:
+            which = place - 2
+            window = window_blocks(rate[which * count + at.start : which * count + at.stop, :])
+            rows = slice(which * part + rows.start, which * part + rows.stop)
+            for a in range(BLOCKS):
+                high, low = halves(blocks[a] * window[a])
+                lanes = slice(a * LANES, (a + 1) * LANES)
+                weighted_hi[half, rows, lanes] = high
+                weighted_lo[half, rows, lanes] = low
+
+    def project(half):
+        both = dot(weighted_hi[half], features[...]) + dot(weighted_lo[half], features[...])
+        for which in range(2):
+            first = which * count + half * part
+            total[first : first + part] = both[which * part : (which + 1) * part]
+
+    def steps(function, half, *others):
+        calls = BLOCKS if function in (first_class, second_class, third_class) else part // STEP
+        return [
+            functools.partial(function, half, i, *other) for i in range(calls) for other in (others or ((),))
+        ]
+
+    for half in range(HALVES):
+        interleaved(steps(fold_inputs, half, (0,), (1,)))
+        interleaved(steps(first_class, half))
+        interleaved(steps(between, half))
+        interleaved(steps(second_class, half))
+        interleaved(steps(third_class, half), steps(outputs, half, (2,), (3,)))
+        project(half)
+        interleaved(steps(outputs, half, (0,), (1,)))
+
+    whole = total[...].T
+    width = whole.shape[0] // 2
+    whole = whole[:width] + whole[width:]
+    for place in range(2):
+        piece = whole[:, place * count : (place + 1) * count]
+        coded = (piece * jnp.abs(piece)).astype(jnp.bfloat16)
         for a in range(BLOCKS):
-            outer_coded[a, at, :] = fourth_power(outer_act[a], OUTER_SCALE)
-        value_grad = signal(1)
-        for a in range(BLOCKS):
-            grad_value[a, at, :] = value_grad[a].astype(jnp.bfloat16)
-        for place, rows in ((2, at), (3, below)):
-            filter_grad = signal(place)
-            window = window_blocks(rate[rows, :])
-            for a in range(BLOCKS):
-                high, low = halves(filter_grad[a] * window[a])
-                lanes = slice(a * LANES, (a + 1) * LANES)
-                weighted_hi[rows, lanes] = high
-                weighted_lo[rows, lanes] = low
-
-    dot = functools.partial(jnp.dot, preferred_element_type=jnp.float32)
-    total = (dot(weighted_hi[...], features[...]) + dot(weighted_lo[...], features[...])).T
-    half = total.shape[0] // 2
-    total = total[:half] + total[half:]
-    for place in range(2):
-        part = total[:, place * count : (place + 1) * count]
-        coded = (part * jnp.abs(part)).astype(jnp.bfloat16)
-        for a in range(BLOCKS):
-            results[a, 3 * count + place * half : 3 * count + (place + 1) * half] = coded
+            results[a, 3 * count + place * width : 3 * count + (place + 1) * width] = coded
     for place, block in zip(places(LAST_PEERS), sent):
         block[...] = results[place, : block.shape[0]]
 
@@ -333,17 +372,18 @@
 
 def operator_grads(received, rates, spectra, angle, terms):
     count = received[0].shape[0] // SENT
+    part = count // HALVES
     bf, f32 = jnp.bfloat16, jnp.float32
     width = 2 * LANES
     return device_call(
         main_kernel,
         [jax.ShapeDtypeStruct(((3 + direct(peer)) * count, LANES), bf) for peer in (0,) + LAST_PEERS],
         [pltpu.VMEM((BLOCKS, SENT * count, LANES), bf), pltpu.VMEM((BLOCKS, RETURNED * count, LANES), bf)]
-        + [pltpu.VMEM((BLOCKS, 2 * count, width), bf)] * 2
-        + [pltpu.VMEM((BLOCKS, 4 * count, width), bf)] * 2
-        + [pltpu.VMEM((BLOCKS, 2 * count, width), f32), pltpu.VMEM((2 * count, width), f32),
-           pltpu.VMEM((BLOCKS, 4 * count, width), f32)]
-        + [pltpu.VMEM((2 * count, BLOCKS * LANES), bf)] * 2
+        + [pltpu.VMEM((BLOCKS, HALVES, 2 * part, width), bf)] * 2
+        + [pltpu.VMEM((BLOCKS, HALVES, 4 * part, width), bf)] * 2
+        + [pltpu.VMEM((BLOCKS, HALVES, 2 * part, width), f32), pltpu.VMEM((BLOCKS, HALVES, 4 * part, width), f32)]
+        + [pltpu.VMEM((HALVES, 2 * part, BLOCKS * LANES), bf)] * 2
+        + [pltpu.VMEM((2 * count, LANES), f32)]
         + [pltpu.VMEM((BLOCKS, width, width), bf)] * 2,
         (True,) * (BLOCKS + 4),
         (True,) * BLOCKS,

time: 62 us -> 60.8 us (0.981)
  Pallas kernels: 17.3 us -> 16.1 us
    pallas_call x1, Pallas kernels: 9 us -> 7.79 us  [operator_grads(): device_call(main_kernel, [jax.ShapeDtypeStruct(((3 + direct(peer)) * coun...]
  transfers between devices with their start and end apart: 18 -> 18, of which waited for: 6 -> 6; matrix products, arithmetic and copies ran while one was open for 6% -> 7% of each run, Pallas kernels for 8% -> 8%
where the time goes in v4:
time: 60.8 us; the launch traced here: 60.6 us
  starting transfers between devices  25 us (41%)
  Pallas kernels  16.1 us (26%)
  waiting for transfers between devices  14.8 us (24%)
  other arithmetic  3.01 us (5%)
  local copies, waits for them, and re-layouts  0.97 us (2%)
  between operations  0.82 us (1%)
    ppermute x14, starting transfers between devices, exchanged(): lax.ppermute(block, 'seq', swap)  22.3 us
    ppermute x14, waiting for transfers between devices, exchanged(): lax.ppermute(block, 'seq', swap)  14.8 us
    pallas_call x1, Pallas kernels, operator_grads(): device_call(main_kernel, [jax.ShapeDtypeStruct(((3 + direct(peer)) * coun...  7.79 us
    pallas_call x1, Pallas kernels, filter_spectra(): device_call(filter_kernel, [jax.ShapeDtypeStruct((BLOCKS, rows, width), f...  3.48 us
    convert_element_type x1, other arithmetic, split_features(): return (high.astype(jnp.bfloat16), (features - high).astype(jnp.bfloat16))  2.76 us
    pallas_call x1, Pallas kernels, packed(): device_call(pack_kernel, [jax.ShapeDtypeStruct((SENT * count, lanes), jnp...  2.27 us
    ppermute x3, starting transfers between devices, body(): lax.ppermute(own_sum, 'ch', [(i, i ^ hop) for i in range(groups)])  1.63 us
    pallas_call x1, Pallas kernels, unpacked(): device_call(unpack_kernel, [block] * 3, [held, held, pltpu.SemaphoreType....  1.3 us
  transfers between devices with their start and end apart: 18, of which 6 were waited for; matrix products, arithmetic and copies ran while one was open for 7% of the time, Pallas kernels for 8%

profile of v4, /device:TPU:0, one launch (start us, length us, event | category | flops | bytes accessed | tf_op | source)
XLA Modules:
  0.0 60.6 jit_solution(7094128443891176002)
XLA Ops:
  0.7 2.3 %packed.1 = (bf16[384,128]{1,0:T(8,128)(2,1)}, bf16[384,128]{1,0:T(8,128)(2,1)}, bf16[384,128]{1,0:T(8,128)(2,1)}, bf16[384,128]{1,0:T(8,128)(2,1)}, bf16[384,12...) custom-call(bf16[8,128,128]{2,1,0:T(8,128)(2,1)} %bitcast.14, ...), custom_call_target="tpu_custom_call" | custom-call | tf_op jit(solution)/shard_map/packed/pallas_call | solution.py:418
  2.9 3.0 %collective-permute-start = (bf16[384,128]{1,0:T(8,128)(2,1)}, bf16[384,128]{1,0:T(8,128)(2,1)S(1)}, u32[]{:S(2)}, u32[]{:S(2)}) collective-permute-start(bf16[384,128]{1,0:T(8,128)(2,1)} %get-tuple-element.29), channel_id=1, source_target_pairs={{0,4},{4,0},{8,12},{12,8},{16,20},{20,16},{24,28},{28,24},{1,5},{5... | collective-permute-start | bytes 294920 | tf_op jit(solution)/shard_map/ppermute | solution.py:431
  6.0 2.6 %collective-permute-start.1 = (bf16[384,128]{1,0:T(8,128)(2,1)}, bf16[384,128]{1,0:T(8,128)(2,1)S(1)}, u32[]{:S(2)}, u32[]{:S(2)}) collective-permute-start(bf16[384,128]{1,0:T(8,128)(2,1)} %get-tuple-element.30), channel_id=1, source_target_pairs={{0,16},{4,20},{8,24},{12,28},{16,0},{20,4},{24,8},{28,12},{1,17},{... | collective-permute-start | bytes 294920 | tf_op jit(solution)/shard_map/ppermute | solution.py:431
  8.6 1.6 %collective-permute-start.2 = (bf16[384,128]{1,0:T(8,128)(2,1)}, bf16[384,128]{1,0:T(8,128)(2,1)S(1)}, u32[]{:S(2)}, u32[]{:S(2)}) collective-permute-start(bf16[384,128]{1,0:T(8,128)(2,1)} %get-tuple-element.31), channel_id=1, source_target_pairs={{0,8},{4,12},{8,0},{12,4},{16,24},{20,28},{24,16},{28,20},{1,9},{5... | collective-permute-start | bytes 294920 | tf_op jit(solution)/shard_map/ppermute | solution.py:431
  10.4 0.6 %collective-permute-start.4 = (bf16[384,128]{1,0:T(8,128)(2,1)}, bf16[384,128]{1,0:T(8,128)(2,1)S(1)}, u32[]{:S(2)}, u32[]{:S(2)}) collective-permute-start(bf16[384,128]{1,0:T(8,128)(2,1)} %get-tuple-element.33), channel_id=1, source_target_pairs={{0,12},{4,8},{8,4},{12,0},{16,28},{20,24},{24,20},{28,16},{1,13},{... | collective-permute-start | bytes 294920 | tf_op jit(solution)/shard_map/ppermute | solution.py:431
  11.0 0.7 %constant_dynamic-slice_fusion.1 = f32[2,128]{1,0:T(2,128)S(1)} fusion(f32[2,1024]{1,0:T(2,128)} %param.13, s32[]{:T(128)S(6)} %select_n.4), kind=kLoop, calls=%fused_computation.8 | loop fusion | bytes 2052 | tf_op jit(solution)/shard_map/dynamic_slice | solution.py:703
  12.0 2.8 %reduce-precision_convert_fusion = (bf16[1024,64]{1,0:T(8,128)(2,1)S(1)}, bf16[1024,64]{1,0:T(8,128)(2,1)S(1)}) fusion(f32[64]{0:T(128)} %param.14, f32[1024]{0:T(1024)S(1)} %iota_add_fusion), kind=kLoop, calls=%fused_computation.1 | loop fusion | flops 327680 | bytes 266496 | tf_op jit(solution)/shard_map/convert_element_type | solution.py:95
  14.9 4.5 %collective-permute-start.5 = (bf16[384,128]{1,0:T(8,128)(2,1)}, bf16[384,128]{1,0:T(8,128)(2,1)S(1)}, u32[]{:S(2)}, u32[]{:S(2)}) collective-permute-start(bf16[384,128]{1,0:T(8,128)(2,1)} %get-tuple-element.34), channel_id=1, source_target_pairs={{0,20},{4,16},{8,28},{12,24},{16,4},{20,0},{24,12},{28,8},{1,21},{... | collective-permute-start | bytes 294920 | tf_op jit(solution)/shard_map/ppermute | solution.py:431
  19.5 3.5 %filter_spectra.1.refs_9_ = f32[8,256,256]{2,1,0:T(8,128)S(1)} custom-call(bf16[256,128]{1,0:T(8,128)(2,1)S(1)} %pad_maximum_fusion.1.proj, f32[256,1]{1,0:T(8,128)S(1)} %copy.19.rate.refs_8_, bf16[1024,128]{1,0:T(8,128)(2,1)S(1)} %pad_maximum_fusion.features.refs_11_, f32[3,128,128]{2,1,0:T(8,128)S(1)} %copy-done.2), custom_call_target="tpu_custom_call" | custom-call | tf_op jit(solution)/shard_map/filter_spectra/pallas_call | solution.py:360
  23.0 2.1 %collective-permute-done.5.refs_6_ = bf16[384,128]{1,0:T(8,128)(2,1)S(1)} collective-permute-done((bf16[384,128]{1,0:T(8,128)(2,1)}, bf16[384,128]{1,0:T(8,128)(2,1)S(1)}, u32[]{:S(2)}, u32[]{:S(2)}) %collective-permute-start.5) | collective-permute-done | bytes 98336 | tf_op jit(solution)/shard_map/ppermute | solution.py:431
  25.2 1.9 %collective-permute-done.6.refs_7_ = bf16[384,128]{1,0:T(8,128)(2,1)S(1)} collective-permute-done((bf16[384,128]{1,0:T(8,128)(2,1)}, bf16[384,128]{1,0:T(8,128)(2,1)S(1)}, u32[]{:S(2)}, u32[]{:S(2)}) %collective-permute-start.6) | collective-permute-done | bytes 98336 | tf_op jit(solution)/shard_map/ppermute | solution.py:431
  27.0 7.8 %operator_grads.1 = (bf16[512,128]{1,0:T(8,128)(2,1)S(1)}, bf16[384,128]{1,0:T(8,128)(2,1)S(1)}, bf16[512,128]{1,0:T(8,128)(2,1)S(1)}, bf16[512,128]{1,0:T(8,128...) custom-call(bf16[384,128]{1,0:T(8,128)(2,1)S(1)} %copy-done.3, ...), custom_call_target="tpu_custom_call" | custom-call | tf_op jit(solution)/shard_map/operator_grads/pallas_call | solution.py:378
  34.8 1.8 %collective-permute-start.7 = (bf16[512,128]{1,0:T(8,128)(2,1)S(1)}, bf16[512,128]{1,0:T(8,128)(2,1)S(1)}, u32[]{:S(2)}, u32[]{:S(2)}) collective-permute-start(bf16[512,128]{1,0:T(8,128)(2,1)S(1)} %get-tuple-element.37), channel_id=1, source_target_pairs={{0,16},{4,20},{8,24},{12,28},{16,0},{20,4},{24,8},{28,12},{1,17},{... | collective-permute-start | bytes 393224 | tf_op jit(solution)/shard_map/ppermute | solution.py:431
  36.7 1.4 %collective-permute-start.8 = (bf16[512,128]{1,0:T(8,128)(2,1)S(1)}, bf16[512,128]{1,0:T(8,128)(2,1)S(1)}, u32[]{:S(2)}, u32[]{:S(2)}) collective-permute-start(bf16[512,128]{1,0:T(8,128)(2,1)S(1)} %get-tuple-element.38), channel_id=1, source_target_pairs={{0,24},{4,28},{8,16},{12,20},{16,8},{20,12},{24,0},{28,4},{1,25},{... | collective-permute-start | bytes 393224 | tf_op jit(solution)/shard_map/ppermute | solution.py:431
  38.9 4.1 %collective-permute-done.10.refs_1_ = bf16[384,128]{1,0:T(8,128)(2,1)S(1)} collective-permute-done((bf16[384,128]{1,0:T(8,128)(2,1)S(1)}, bf16[384,128]{1,0:T(8,128)(2,1)S(1)}, u32[]{:S(2)}, u32[]{:S(2)}) %collective-permute-start.10) | collective-permute-done | bytes 98336 | tf_op jit(solution)/shard_map/ppermute | solution.py:431
  43.0 3.0 %collective-permute-done.7.refs_2_.refs_1_ = bf16[512,128]{1,0:T(8,128)(2,1)S(1)} collective-permute-done((bf16[512,128]{1,0:T(8,128)(2,1)S(1)}, bf16[512,128]{1,0:T(8,128)(2,1)S(1)}, u32[]{:S(2)}, u32[]{:S(2)}) %collective-permute-start.7) | collective-permute-done | bytes 131104 | tf_op jit(solution)/shard_map/ppermute | solution.py:431
  46.0 1.1 %collective-permute-start.14 = (bf16[512,128]{1,0:T(8,128)(2,1)S(1)}, bf16[512,128]{1,0:T(8,128)(2,1)S(1)}, u32[]{:S(2)}, u32[]{:S(2)}) collective-permute-start(bf16[512,128]{1,0:T(8,128)(2,1)S(1)} %gather_proj.1), channel_id=1, source_target_pairs={{0,4},{4,0},{8,12},{12,8},{16,20},{20,16},{24,28},{28,24},{1,5},{5... | collective-permute-start | bytes 393224 | tf_op jit(solution)/shard_map/ppermute | solution.py:452
  47.1 2.2 %collective-permute-start.11 = (bf16[384,128]{1,0:T(8,128)(2,1)S(1)}, bf16[384,128]{1,0:T(8,128)(2,1)S(1)}, u32[]{:S(2)}, u32[]{:S(2)}) collective-permute-start(bf16[384,128]{1,0:T(8,128)(2,1)S(1)} %get-tuple-element.46), channel_id=1, source_target_pairs={{0,20},{4,16},{8,28},{12,24},{16,4},{20,0},{24,12},{28,8},{1,21},{... | collective-permute-start | bytes 294920 | tf_op jit(solution)/shard_map/ppermute | solution.py:431
  49.2 3.5 %collective-permute-start.12 = (bf16[384,128]{1,0:T(8,128)(2,1)S(1)}, bf16[384,128]{1,0:T(8,128)(2,1)S(1)}, u32[]{:S(2)}, u32[]{:S(2)}) collective-permute-start(bf16[384,128]{1,0:T(8,128)(2,1)S(1)} %get-tuple-element.47), channel_id=1, source_target_pairs={{0,28},{4,24},{8,20},{12,16},{16,12},{20,8},{24,4},{28,0},{1,29},{... | collective-permute-start | bytes 294920 | tf_op jit(solution)/shard_map/ppermute | solution.py:431
  53.0 1.6 %collective-permute-start.16 = (f32[8,128]{1,0:T(8,128)S(1)}, f32[8,128]{1,0:T(8,128)S(1)}, u32[]{:S(2)}, u32[]{:S(2)}) collective-permute-start(f32[8,128]{1,0:T(8,128)S(1)} %square_total.1.refs_5_), channel_id=1, source_target_pairs={{0,2},{1,3},{2,0},{3,1},{4,6},{5,7},{6,4},{7,5},{8,10},{9,11},{10,... | collective-permute-start | bytes 12296 | tf_op jit(solution)/shard_map/ppermute | solution.py:722
  54.5 2.3 %collective-permute-done.11.refs_5_ = bf16[384,128]{1,0:T(8,128)(2,1)S(1)} collective-permute-done((bf16[384,128]{1,0:T(8,128)(2,1)S(1)}, bf16[384,128]{1,0:T(8,128)(2,1)S(1)}, u32[]{:S(2)}, u32[]{:S(2)}) %collective-permute-start.11) | collective-permute-done | bytes 98336 | tf_op jit(solution)/shard_map/ppermute | solution.py:431
  56.9 1.4 %collective-permute-done.13.refs_7_ = bf16[384,128]{1,0:T(8,128)(2,1)S(1)} collective-permute-done((bf16[384,128]{1,0:T(8,128)(2,1)S(1)}, bf16[384,128]{1,0:T(8,128)(2,1)S(1)}, u32[]{:S(2)}, u32[]{:S(2)}) %collective-permute-start.13) | collective-permute-done | bytes 98336 | tf_op jit(solution)/shard_map/ppermute | solution.py:431
  58.2 1.3 %unpacked.1 = (bf16[8,128,128]{2,1,0:T(8,128)(2,1)}, bf16[8,128,128]{2,1,0:T(8,128)(2,1)}, bf16[8,128,128]{2,1,0:T(8,128)(2,1)}) custom-call(bf16[512,128]{1,0:T(8,128)(2,1)S(1)} %get-tuple-element.41.refs_0_, bf16[384,128]{1,0:T(8,128)(2,1)S(1)} %collective-permute-done.10.refs_1_, bf16[512,128]{1,0:T(8,128)(2,1)S(1)} %collective-permute-done.7.refs_2_.refs_1_, ...), custom_call_target="tpu_custom_call" | custom-call | tf_op jit(solution)/shard_map/unpacked/pallas_call | solution.py:510
  59.6 1.0 %scaled.1 = f32[2,64,1024]{2,1,0:T(8,128)} custom-call(bf16[512,128]{1,0:T(8,128)(2,1)S(1)} %get-tuple-element.41.refs_0_, bf16[512,128]{1,0:T(8,128)(2,1)S(1)} %collective-permute-done.7.refs_2_.refs_1_, bf16[512,128]{1,0:T(8,128)(2,1)S(1)} %collective-permute-done.8.refs_3_.refs_2_, bf16[512,128]{1,0:T(8,128)(2,1)S(1)} %collective-permute-done.9.refs_4_.refs_3_, ...), custom_call_target="tpu_custom_call" | custom-call | tf_op jit(solution)/shard_map/scaled/pallas_call | solution.py:543
  (35 shorter events, 1.9 us)
Async XLA Ops:
  0.6 11.0 %copy-start = (bf16[2,1024,64]{1,2,0:T(8,128)(2,1)S(1)}, bf16[2,1024,64]{1,2,0:T(8,128)(2,1)}, u32[]{:S(2)}) copy-start(bf16[2,1024,64]{1,2,0:T(8,128)(2,1)} %param.12) | copy-start | bytes 786436
  0.6 18.9 %copy-start.2 = (f32[3,128,128]{2,1,0:T(8,128)S(1)}, f32[3,128,128]{2,1,0:T(8,128)}, u32[]{:S(2)}) copy-start(f32[3,128,128]{2,1,0:T(8,128)} %constant.16.clone.angle.refs_10_) | copy-start | bytes 589828
  2.9 12.0 %collective-permute-start = (bf16[384,128]{1,0:T(8,128)(2,1)}, bf16[384,128]{1,0:T(8,128)(2,1)S(1)}, u32[]{:S(2)}, u32[]{:S(2)}) collective-permute-start(bf16[384,128]{1,0:T(8,128)(2,1)} %get-tuple-element.29), channel_id=1, source_target_pairs={{0,4},{4,0},{8,12},{12,8},{16,20},{20,16},{24,28},{28,24},{1,5},{5... | collective-permute-start | bytes 294920 | tf_op jit(solution)/shard_map/ppermute | solution.py:431
  6.0 13.4 %collective-permute-start.1 = (bf16[384,128]{1,0:T(8,128)(2,1)}, bf16[384,128]{1,0:T(8,128)(2,1)S(1)}, u32[]{:S(2)}, u32[]{:S(2)}) collective-permute-start(bf16[384,128]{1,0:T(8,128)(2,1)} %get-tuple-element.30), channel_id=1, source_target_pairs={{0,16},{4,20},{8,24},{12,28},{16,0},{20,4},{24,8},{28,12},{1,17},{... | collective-permute-start | bytes 294920 | tf_op jit(solution)/shard_map/ppermute | solution.py:431
  8.6 14.5 %collective-permute-start.2 = (bf16[384,128]{1,0:T(8,128)(2,1)}, bf16[384,128]{1,0:T(8,128)(2,1)S(1)}, u32[]{:S(2)}, u32[]{:S(2)}) collective-permute-start(bf16[384,128]{1,0:T(8,128)(2,1)} %get-tuple-element.31), channel_id=1, source_target_pairs={{0,8},{4,12},{8,0},{12,4},{16,24},{20,28},{24,16},{28,20},{1,9},{5... | collective-permute-start | bytes 294920 | tf_op jit(solution)/shard_map/ppermute | solution.py:431
  10.1 12.9 %collective-permute-start.3 = (bf16[384,128]{1,0:T(8,128)(2,1)}, bf16[384,128]{1,0:T(8,128)(2,1)S(1)}, u32[]{:S(2)}, u32[]{:S(2)}) collective-permute-start(bf16[384,128]{1,0:T(8,128)(2,1)} %get-tuple-element.32), channel_id=1, source_target_pairs={{0,24},{4,28},{8,16},{12,20},{16,8},{20,12},{24,0},{28,4},{1,25},{... | collective-permute-start | bytes 294920 | tf_op jit(solution)/shard_map/ppermute | solution.py:431
  10.4 12.7 %collective-permute-start.4 = (bf16[384,128]{1,0:T(8,128)(2,1)}, bf16[384,128]{1,0:T(8,128)(2,1)S(1)}, u32[]{:S(2)}, u32[]{:S(2)}) collective-permute-start(bf16[384,128]{1,0:T(8,128)(2,1)} %get-tuple-element.33), channel_id=1, source_target_pairs={{0,12},{4,8},{8,4},{12,0},{16,28},{20,24},{24,20},{28,16},{1,13},{... | collective-permute-start | bytes 294920 | tf_op jit(solution)/shard_map/ppermute | solution.py:431
  12.0 15.1 %copy-start.3 = (bf16[384,128]{1,0:T(8,128)(2,1)S(1)}, bf16[384,128]{1,0:T(8,128)(2,1)}, u32[]{:S(2)}) copy-start(bf16[384,128]{1,0:T(8,128)(2,1)} %get-tuple-element.28.refs_0_) | copy-start | bytes 294916
  14.9 10.3 %collective-permute-start.5 = (bf16[384,128]{1,0:T(8,128)(2,1)}, bf16[384,128]{1,0:T(8,128)(2,1)S(1)}, u32[]{:S(2)}, u32[]{:S(2)}) collective-permute-start(bf16[384,128]{1,0:T(8,128)(2,1)} %get-tuple-element.34), channel_id=1, source_target_pairs={{0,20},{4,16},{8,28},{12,24},{16,4},{20,0},{24,12},{28,8},{1,21},{... | collective-permute-start | bytes 294920 | tf_op jit(solution)/shard_map/ppermute | solution.py:431
  19.4 7.6 %collective-permute-start.6 = (bf16[384,128]{1,0:T(8,128)(2,1)}, bf16[384,128]{1,0:T(8,128)(2,1)S(1)}, u32[]{:S(2)}, u32[]{:S(2)}) collective-permute-start(bf16[384,128]{1,0:T(8,128)(2,1)} %get-tuple-element.35), channel_id=1, source_target_pairs={{0,28},{4,24},{8,20},{12,16},{16,12},{20,8},{24,4},{28,0},{1,29},{... | collective-permute-start | bytes 294920 | tf_op jit(solution)/shard_map/ppermute | solution.py:431
  27.0 31.2 %copy-start.1 = (bf16[1024,128]{1,0:T(8,128)(2,1)S(1)}, bf16[1024,128]{1,0:T(8,128)(2,1)}, u32[]{:S(2)}) copy-start(bf16[1024,128]{1,0:T(8,128)(2,1)} %param.11) | copy-start | bytes 786436
  34.8 11.1 %collective-permute-start.7 = (bf16[512,128]{1,0:T(8,128)(2,1)S(1)}, bf16[512,128]{1,0:T(8,128)(2,1)S(1)}, u32[]{:S(2)}, u32[]{:S(2)}) collective-permute-start(bf16[512,128]{1,0:T(8,128)(2,1)S(1)} %get-tuple-element.37), channel_id=1, source_target_pairs={{0,16},{4,20},{8,24},{12,28},{16,0},{20,4},{24,8},{28,12},{1,17},{... | collective-permute-start | bytes 393224 | tf_op jit(solution)/shard_map/ppermute | solution.py:431
  36.7 9.3 %collective-permute-start.8 = (bf16[512,128]{1,0:T(8,128)(2,1)S(1)}, bf16[512,128]{1,0:T(8,128)(2,1)S(1)}, u32[]{:S(2)}, u32[]{:S(2)}) collective-permute-start(bf16[512,128]{1,0:T(8,128)(2,1)S(1)} %get-tuple-element.38), channel_id=1, source_target_pairs={{0,24},{4,28},{8,16},{12,20},{16,8},{20,12},{24,0},{28,4},{1,25},{... | collective-permute-start | bytes 393224 | tf_op jit(solution)/shard_map/ppermute | solution.py:431
  38.1 7.9 %collective-permute-start.9 = (bf16[512,128]{1,0:T(8,128)(2,1)S(1)}, bf16[512,128]{1,0:T(8,128)(2,1)S(1)}, u32[]{:S(2)}, u32[]{:S(2)}) collective-permute-start(bf16[512,128]{1,0:T(8,128)(2,1)S(1)} %get-tuple-element.39), channel_id=1, source_target_pairs={{0,8},{4,12},{8,0},{12,4},{16,24},{20,28},{24,16},{28,20},{1,9},{5... | collective-permute-start | bytes 393224 | tf_op jit(solution)/shard_map/ppermute | solution.py:431
  38.4 4.6 %collective-permute-start.10 = (bf16[384,128]{1,0:T(8,128)(2,1)S(1)}, bf16[384,128]{1,0:T(8,128)(2,1)S(1)}, u32[]{:S(2)}, u32[]{:S(2)}) collective-permute-start(bf16[384,128]{1,0:T(8,128)(2,1)S(1)} %get-tuple-element.40), channel_id=1, source_target_pairs={{0,4},{4,0},{8,12},{12,8},{16,20},{20,16},{24,28},{28,24},{1,5},{5... | collective-permute-start | bytes 294920 | tf_op jit(solution)/shard_map/ppermute | solution.py:431
  46.0 6.7 %collective-permute-start.14 = (bf16[512,128]{1,0:T(8,128)(2,1)S(1)}, bf16[512,128]{1,0:T(8,128)(2,1)S(1)}, u32[]{:S(2)}, u32[]{:S(2)}) collective-permute-start(bf16[512,128]{1,0:T(8,128)(2,1)S(1)} %gather_proj.1), channel_id=1, source_target_pairs={{0,4},{4,0},{8,12},{12,8},{16,20},{20,16},{24,28},{28,24},{1,5},{5... | collective-permute-start | bytes 393224 | tf_op jit(solution)/shard_map/ppermute | solution.py:452
  47.1 9.8 %collective-permute-start.11 = (bf16[384,128]{1,0:T(8,128)(2,1)S(1)}, bf16[384,128]{1,0:T(8,128)(2,1)S(1)}, u32[]{:S(2)}, u32[]{:S(2)}) collective-permute-start(bf16[384,128]{1,0:T(8,128)(2,1)S(1)} %get-tuple-element.46), channel_id=1, source_target_pairs={{0,20},{4,16},{8,28},{12,24},{16,4},{20,0},{24,12},{28,8},{1,21},{... | collective-permute-start | bytes 294920 | tf_op jit(solution)/shard_map/ppermute | solution.py:431
  49.2 7.6 %collective-permute-start.12 = (bf16[384,128]{1,0:T(8,128)(2,1)S(1)}, bf16[384,128]{1,0:T(8,128)(2,1)S(1)}, u32[]{:S(2)}, u32[]{:S(2)}) collective-permute-start(bf16[384,128]{1,0:T(8,128)(2,1)S(1)} %get-tuple-element.47), channel_id=1, source_target_pairs={{0,28},{4,24},{8,20},{12,16},{16,12},{20,8},{24,4},{28,0},{1,29},{... | collective-permute-start | bytes 294920 | tf_op jit(solution)/shard_map/ppermute | solution.py:431
  52.7 5.5 %collective-permute-start.13 = (bf16[384,128]{1,0:T(8,128)(2,1)S(1)}, bf16[384,128]{1,0:T(8,128)(2,1)S(1)}, u32[]{:S(2)}, u32[]{:S(2)}) collective-permute-start(bf16[384,128]{1,0:T(8,128)(2,1)S(1)} %get-tuple-element.48), channel_id=1, source_target_pairs={{0,12},{4,8},{8,4},{12,0},{16,28},{20,24},{24,20},{28,16},{1,13},{... | collective-permute-start | bytes 294920 | tf_op jit(solution)/shard_map/ppermute | solution.py:431
  52.9 6.6 %collective-permute-start.17 = (f32[8,128]{1,0:T(8,128)S(1)}, f32[8,128]{1,0:T(8,128)S(1)}, u32[]{:S(2)}, u32[]{:S(2)}) collective-permute-start(f32[8,128]{1,0:T(8,128)S(1)} %square_total.1.refs_5_), channel_id=1, source_target_pairs={{0,3},{1,2},{2,1},{3,0},{4,7},{5,6},{6,5},{7,4},{8,11},{9,10},{10,... | collective-permute-start | bytes 12296 | tf_op jit(solution)/shard_map/ppermute | solution.py:722
  53.0 6.6 %collective-permute-start.16 = (f32[8,128]{1,0:T(8,128)S(1)}, f32[8,128]{1,0:T(8,128)S(1)}, u32[]{:S(2)}, u32[]{:S(2)}) collective-permute-start(f32[8,128]{1,0:T(8,128)S(1)} %square_total.1.refs_5_), channel_id=1, source_target_pairs={{0,2},{1,3},{2,0},{3,1},{4,6},{5,7},{6,4},{7,5},{8,10},{9,11},{10,... | collective-permute-start | bytes 12296 | tf_op jit(solution)/shard_map/ppermute | solution.py:722
  56.9 2.7 %collective-permute-start.15 = (f32[8,128]{1,0:T(8,128)S(1)}, f32[8,128]{1,0:T(8,128)S(1)}, u32[]{:S(2)}, u32[]{:S(2)}) collective-permute-start(f32[8,128]{1,0:T(8,128)S(1)} %square_total.1.refs_5_), channel_id=1, source_target_pairs={{0,1},{1,0},{2,3},{3,2},{4,5},{5,4},{6,7},{7,6},{8,9},{9,8},{10,11... | collective-permute-start | bytes 12296 | tf_op jit(solution)/shard_map/ppermute | solution.py:722
